TPU v7x, 32 devices: a whole 2x2x4 slice. The times are simulated.
32 devices in a mesh: term: 8 (over z, core), row: 4 (over y, x).
Axes of the slice: x: 2, y: 2, z: 4, core: 2. Of those that a mesh axis runs over, the one named last changes fastest.
Arguments:
- psi: bfloat16 [2048, 2048], P('row'), may hold values from -6 to 6
- left_ops: bfloat16 [8, 2048, 2048], P('term', 'row'), may hold values from -0.046875 to 0.046875
- right_ops: bfloat16 [8, 2048, 2048], P('term', 'row'), may hold values from -0.1875 to 0.1875
- block_mask: int32 [8, 16, 16], P('term', 'row'), may hold values from 0 to 1, as said below
Outputs:
- sigma: bfloat16 [2048, 2048], P('row', 'term')
Inputs may be any that keep to these rules, and one draw needn't show every extreme that they name: Entries are 0 or 1; block_mask[t, i, i] = 1 for every term and block.
All inputs are finite; a program needn't handle non-finite values.
Results may differ from a plain program's by a relative error of at most 0.0049.
Values may be sent and summed in bfloat16 or wider, within the bound.
No kernel may reach another device: no remote copies, remote signals or barrier semaphores. Data moves between devices by JAX's collectives and lax.ppermute only.
A program may use at most 64 MiB of HBM per device.

v0:
```python
import jax
import jax.numpy as jnp
from jax import lax
from jax.sharding import PartitionSpec as P


def swapped(value, axis, bit):
    mask = 2**bit
    pairs = [(source, source ^ mask) for source in range(lax.axis_size(axis))]
    return lax.ppermute(value, axis, pairs)


def make_fold(operands, piece):
    outputs = []
    for member in range(operands.shape[0]):
        columns = operands[member]
        outputs.append(jnp.dot(columns, piece, preferred_element_type=jnp.float32))
    return jnp.stack(outputs)


def shards(psi, left_ops, right_ops, block_mask):
    rows = psi.shape[0]
    width = psi.shape[1]
    local_terms = left_ops.shape[0]
    row_blocks = block_mask.shape[1]
    col_blocks = block_mask.shape[2]
    blk = width // col_blocks
    grid = jnp.broadcast_to(
        block_mask[:, :, None, :, None], (local_terms, row_blocks, blk, col_blocks, blk)
    )
    masked = left_ops * grid.reshape(local_terms, rows, width).astype(jnp.bfloat16)
    half = width // 2
    side = lax.axis_index("term") % 2
    own_cols = lax.dynamic_slice_in_dim(psi, side * half, half, 1)
    keep_right = lax.dynamic_slice_in_dim(right_ops, side * half, half, 2)
    give_right = lax.dynamic_slice_in_dim(right_ops, (1 - side) * half, half, 2)
    partner_masked, partner_right, partner_mask = swapped(
        (masked, give_right, block_mask.astype(jnp.bfloat16)), "term", 0
    )
    operands = jnp.concatenate([masked, partner_masked], 0)
    inner = make_fold(operands, lax.all_gather(own_cols, "row", axis=0, tiled=True))
    inner = inner.astype(jnp.bfloat16)
    both_right = jnp.concatenate([keep_right, partner_right], 0)
    partial_value = jnp.einsum(
        "kih,kah->ia",
        inner,
        lax.all_gather(both_right, "row", axis=1, tiled=True),
        preferred_element_type=jnp.float32,
    )
    return lax.psum_scatter(partial_value, "term", scatter_dimension=1, tiled=True).astype(
        jnp.bfloat16
    )


def solution(mesh):
    in_specs = (
        P("row", None),
        P("term", "row", None),
        P("term", "row", None),
        P("term", "row", None),
    )
    out_specs = P("row", "term")
    return jax.shard_map(shards, mesh=mesh, in_specs=in_specs, out_specs=out_specs, check_vma=False)
```

profile of v0, /device:TPU:2, one launch (start us, length us, event | category | flops | bytes accessed | tf_op | source)
XLA Modules:
  0.0 221.5 jit_solution(1439953561811724758)
XLA Ops:
  6.5 0.0 copy-start
  6.5 0.0 all-gather.3.cloned.1.call-start
  6.5 1.6 copy-done
  8.1 1.1 constant_dynamic-slice_fusion.2
  9.2 0.0 all-gather.3.cloned.1.call-update
  9.2 0.0 all-gather.5.cloned.1.call-start
  9.3 1.7 constant_dynamic-slice_fusion.1
  11.0 0.1 collective-permute-start.1
  11.1 2.6 %collective-permute-done.1 = bf16[1,512,1024]{2,1,0:T(8,128)(2,1)S(1)} collective-permute-done((bf16[1,512,1024]{2,1,0:T(8,128)(2,1)S(1)}, bf16[1,512,1024]{2,1,0:T(8,128)(2,1)S(1)}, u32[]{:S(2)}, u32[]{:S(2)}) %collective-permute-start.1) | collective-permute-done | bytes 1048608 | tf_op jit(solution)/shard_map/ppermute | solution.py:10
  13.7 1.5 pad_maximum_fusion
  15.2 0.0 copy-start.1
  15.2 0.0 all-gather.5.cloned.1.call-update
  15.3 0.0 reduce-scatter.2.cloned.1.call-start
  15.3 0.6 copy-done.1
  15.9 1.6 broadcast_in_dim.2
  17.6 4.4 %convert_element_type.24 = bf16[1,512,2048]{2,1,0:T(8,128)(2,1)} reshape(bf16[4,128,16,128]{3,2,1,0:T(8,128)(2,1)} %broadcast_in_dim.2) | data formatting | bytes 4194304 | tf_op jit(solution)/shard_map/convert_element_type | solution.py:31
  21.9 4.5 %mul.10 = bf16[1,512,2048]{2,1,0:T(8,128)(2,1)} multiply(bf16[1,512,2048]{2,1,0:T(8,128)(2,1)} %param.5, bf16[1,512,2048]{2,1,0:T(8,128)(2,1)} %convert_element_type.24) | non-fusion elementwise | flops 1048576 | bytes 6291456 | tf_op jit(solution)/shard_map/mul | solution.py:31
  26.4 0.1 collective-permute-start
  26.5 36.8 %all-gather.3.cloned.1.call-done = bf16[2048,1024]{1,0:T(8,128)(2,1)} async-done(((bf16[512,1024]{1,0:T(8,128)(2,1)}), bf16[2048,1024]{1,0:T(8,128)(2,1)}) %all-gather.3.cloned.1.call-update) | async-done | bytes 4194320 | tf_op jit(solution)/shard_map/all_gather | solution.py:41
  63.3 0.0 copy-start.2
  63.3 5.3 %fusion.16 = bf16[1,512,1024]{2,1,0:T(8,128)(2,1)S(1)} fusion(bf16[2048,1024]{1,0:T(8,128)(2,1)} %all-gather.3.cloned.1.call-done, bf16[1,512,2048]{2,1,0:T(8,128)(2,1)} %mul.10), kind=kOutput, calls=%fused_computation.12 | convolution fusion | flops 2148007936 | bytes 7340032 | tf_op jit(solution)/shard_map/dot_general | solution.py:17
  68.6 0.0 collective-permute-done
  68.6 0.0 copy-done.2
  68.6 4.9 %fusion.13 = bf16[1,512,1024]{2,1,0:T(8,128)(2,1)} fusion(bf16[2048,1024]{1,0:T(8,128)(2,1)S(1)} %copy-done.2, bf16[1,512,2048]{2,1,0:T(8,128)(2,1)} %collective-permute-done), kind=kOutput, calls=%fused_computation.11 | convolution fusion | flops 2148007936 | bytes 7340032 | tf_op jit(solution)/shard_map/dot_general | solution.py:17
  73.6 79.2 %all-gather.5.cloned.1.call-done = bf16[2,2048,1024]{2,1,0:T(8,128)(2,1)} async-done(((bf16[2,512,1024]{2,1,0:T(8,128)(2,1)}), bf16[2,2048,1024]{2,1,0:T(8,128)(2,1)}) %all-gather.5.cloned.1.call-update) | async-done | bytes 8388624 | tf_op jit(solution)/shard_map/all_gather | solution.py:47
  152.8 10.2 %convolution_bitcast_fusion = f32[512,2048]{1,0:T(8,128)} fusion(bf16[2,2048,1024]{2,1,0:T(8,128)(2,1)} %all-gather.5.cloned.1.call-done, bf16[1,512,1024]{2,1,0:T(8,128)(2,1)} %fusion.13, bf16[1,512,1024]{2,1,0:T(8,128)(2,1)S(1)} %fusion.16), kind=kOutput, calls=%fused_computation | convolution fusion | flops 4296015872 | bytes 14680064 | tf_op jit(solution)/shard_map/kih,kah->ia/dot_general | solution.py:44
  163.0 0.0 reduce-scatter.2.cloned.1.call-update
  163.0 50.2 %reduce-scatter.2.cloned.1.call-done = f32[512,256]{1,0:T(8,128)} async-done(((f32[512,2048]{1,0:T(8,128)}), f32[512,256]{1,0:T(8,128)}) %reduce-scatter.2.cloned.1.call-update) | async-done | bytes 524304 | tf_op jit(solution)/shard_map/reduce_scatter | solution.py:50
  213.2 1.8 convert_element_type.25
  (1 shorter events, 0.0 us)
Async XLA Ops:
  6.5 1.6 copy-start
  6.5 56.8 %all-gather.3.cloned.1.call-start = ((), (), s32[]{:S(2)}) async-start(), calls=%async_computation.1 | async-start | bytes 5242880 | tf_op jit(solution)/shard_map/all_gather | solution.py:41
  9.2 143.6 %all-gather.5.cloned.1.call-start = ((), (), s32[]{:S(2)}) async-start(), calls=%async_computation.2 | async-start | bytes 10485760 | tf_op jit(solution)/shard_map/all_gather | solution.py:47
  11.0 2.7 %collective-permute-start.1 = (bf16[1,512,1024]{2,1,0:T(8,128)(2,1)S(1)}, bf16[1,512,1024]{2,1,0:T(8,128)(2,1)S(1)}, u32[]{:S(2)}, u32[]{:S(2)}) collective-permute-start(bf16[1,512,1024]{2,1,0:T(8,128)(2,1)S(1)} %get-tuple-element.6), channel_id=1, source_target_pairs={{0,4},{4,0},{8,12},{12,8},{16,20},{20,16},{24,28},{28,24},{1,5},{5... | collective-permute-start | bytes 3145736 | tf_op jit(solution)/shard_map/ppermute | solution.py:10
  15.2 0.7 copy-start.1
  15.3 197.9 %reduce-scatter.2.cloned.1.call-start = ((), (), s32[]{:S(2)}) async-start(), calls=%async_computation.3 | async-start | bytes 4718592 | tf_op jit(solution)/shard_map/reduce_scatter | solution.py:50
  26.4 42.3 %collective-permute-start = (bf16[1,512,2048]{2,1,0:T(8,128)(2,1)}, bf16[1,512,2048]{2,1,0:T(8,128)(2,1)}, u32[]{:S(2)}, u32[]{:S(2)}) collective-permute-start(bf16[1,512,2048]{2,1,0:T(8,128)(2,1)} %mul.10), channel_id=1, source_target_pairs={{0,4},{4,0},{8,12},{12,8},{16,20},{20,16},{24,28},{28,24},{1,5},{5... | collective-permute-start | bytes 6291464 | tf_op jit(solution)/shard_map/ppermute | solution.py:10
  63.3 5.3 %copy-start.2 = (bf16[2048,1024]{1,0:T(8,128)(2,1)S(1)}, bf16[2048,1024]{1,0:T(8,128)(2,1)}, u32[]{:S(2)}) copy-start(bf16[2048,1024]{1,0:T(8,128)(2,1)} %all-gather.3.cloned.1.call-done) | copy-start | bytes 12582916
Sparse Core Ops, SparseCore 0:
  9.3 53.9 all-gather.2
  65.2 87.5 all-gather.4
  163.2 50.0 reduce-scatter.1
where the time goes:
time: 223 us; the launch traced here: 222 us
  waiting for transfers between devices  169 us (76%)
  matrix products  20.4 us (9%)
  between operations  13.2 us (6%)
  local copies, waits for them, and re-layouts  11 us (5%)
  other arithmetic  7.72 us (3%)
    all_gather x1, waiting for transfers between devices, shards(): lax.all_gather(both_right, 'row', axis=1, tiled=True)  79.2 us
    reduce_scatter x1, waiting for transfers between devices, shards(): lax.psum_scatter(partial_value, 'term', scatter_dimension=1, tiled=True)  50.2 us
    all_gather x1, waiting for transfers between devices, shards(): lax.all_gather(own_cols, 'row', axis=0, tiled=True)  36.8 us
    dot_general x2, matrix products, make_fold(): outputs.append(jnp.dot(columns, piece, preferred_element_type=jnp.float32))  10.2 us
    dot_general x1, matrix products, shards(): jnp.einsum('kih,kah->ia', inner, lax.all_gather(both_right, 'row', axis=1...  10.2 us
  transfers between devices with their start and end apart: 5, of which 4 were waited for; matrix products, arithmetic and copies ran while one was open for 11% of the time, Pallas kernels for 0%

commit v1 on v0

v1 whole, which is shorter than its diff:
```python
import functools
import math

import jax
import jax.numpy as jnp
from jax import lax
from jax.experimental import pallas as pl
from jax.experimental.pallas import tpu as pltpu
from jax.sharding import PartitionSpec as P

SHARE = 4
PIECES = 2
VMEM_BYTES = 48 * 1024 * 1024
WHOLE = pl.BlockSpec(memory_space=pltpu.VMEM)
ANYWHERE = pl.BlockSpec(memory_space=pl.ANY)


def params():
    return pltpu.CompilerParams(vmem_limit_bytes=VMEM_BYTES)


def mask_kernel(start, blk, mask_ref, left_ref, out_ref):
    block = (start + pl.program_id(0) * left_ref.shape[0]) // blk
    for j in range(left_ref.shape[1] // blk):
        keep = mask_ref[block, j] != 0
        cols = pl.ds(j * blk, blk)
        tile = left_ref[:, cols]
        out_ref[:, cols] = jnp.where(keep, tile, jnp.zeros_like(tile))


def masked_rows(left, mask, start, rows):
    width = left.shape[1]
    blk = width // mask.shape[1]
    unit = math.gcd(rows, blk)
    return pl.pallas_call(
        functools.partial(mask_kernel, start, blk),
        grid=(rows // unit,),
        in_specs=[
            pl.BlockSpec(memory_space=pltpu.SMEM),
            pl.BlockSpec((unit, width), lambda i: (start // unit + i, 0)),
        ],
        out_specs=pl.BlockSpec((unit, width), lambda i: (i, 0)),
        out_shape=jax.ShapeDtypeStruct((rows, width), left.dtype),
        compiler_params=params(),
        cost_estimate=pl.CostEstimate(
            flops=rows * width, bytes_accessed=4 * rows * width, transcendentals=0
        ),
    )(mask, left)


def inner_kernel(n_rows, n_parts, place_ref, *refs):
    row_refs = refs[:n_rows]
    part_refs = refs[n_rows : n_rows + n_parts]
    out_ref, psi, sems = refs[n_rows + n_parts :]
    copies = []
    for p, part in enumerate(part_refs):
        size = part.shape[0]
        where = pl.ds(pl.multiple_of(place_ref[p], size), size)
        copies.append(pltpu.make_async_copy(part, psi.at[where], sems.at[p]))
    for copy in copies:
        copy.start()
    for copy in copies:
        copy.wait()
    width = psi.shape[1]
    step = math.gcd(width, 512)

    def column(j, carry):
        cols = pl.ds(pl.multiple_of(j * step, step), step)
        at = 0
        for ref in row_refs:
            unit = math.gcd(ref.shape[0], 256)
            for i in range(ref.shape[0] // unit):
                value = jnp.dot(
                    ref[i * unit : (i + 1) * unit, :],
                    psi[:, cols],
                    preferred_element_type=jnp.float32,
                )
                out_ref[at : at + unit, cols] = value.astype(out_ref.dtype)
                at += unit
        return carry

    lax.fori_loop(0, width // step, column, 0)


def inner_of(rows, parts, places):
    height = sum(a.shape[0] for a in rows)
    width = parts[0].shape[1]
    depth = sum(a.shape[0] for a in parts)
    return pl.pallas_call(
        functools.partial(inner_kernel, len(rows), len(parts)),
        in_specs=[pl.BlockSpec(memory_space=pltpu.SMEM)]
        + [WHOLE] * len(rows)
        + [ANYWHERE] * len(parts),
        out_specs=WHOLE,
        out_shape=jax.ShapeDtypeStruct((height, width), parts[0].dtype),
        scratch_shapes=[
            pltpu.VMEM((depth, width), parts[0].dtype),
            pltpu.SemaphoreType.DMA((len(parts),)),
        ],
        compiler_params=params(),
        cost_estimate=pl.CostEstimate(
            flops=2 * height * width * depth,
            bytes_accessed=2 * (height * depth + height * width + width * depth),
            transcendentals=0,
        ),
    )(places, *rows, *parts)


def outer_kernel(n_inner, n_right, side_ref, *refs):
    inner_refs = refs[:n_inner]
    right_refs = refs[n_inner : n_inner + n_right]
    keep_ref, give_ref = refs[n_inner + n_right :]
    side = side_ref[0]
    for half, out_ref in ((side, keep_ref), (1 - side, give_ref)):
        right = jnp.concatenate([ref[half] for ref in right_refs], 0)
        at = 0
        for ref in inner_refs:
            unit = math.gcd(ref.shape[0], 256)
            for i in range(ref.shape[0] // unit):
                out_ref[at : at + unit, :] = lax.dot_general(
                    ref[i * unit : (i + 1) * unit, :],
                    right,
                    (((1,), (1,)), ((), ())),
                    preferred_element_type=jnp.float32,
                )
                at += unit


def outer_of(inners, own_right, piece, rights, side):
    height = sum(a.shape[0] for a in inners)
    halves, pieces, wide, depth = own_right.shape
    width = wide * (1 + len(rights))
    shape = jax.ShapeDtypeStruct((height, width), jnp.float32)
    own_spec = pl.BlockSpec((halves, None, wide, depth), lambda i: (0, piece, 0, 0))
    return pl.pallas_call(
        functools.partial(outer_kernel, len(inners), 1 + len(rights)),
        grid=(1,),
        in_specs=[pl.BlockSpec(memory_space=pltpu.SMEM)]
        + [WHOLE] * len(inners)
        + [own_spec]
        + [WHOLE] * len(rights),
        out_specs=[WHOLE, WHOLE],
        out_shape=[shape, shape],
        compiler_params=params(),
        cost_estimate=pl.CostEstimate(
            flops=4 * height * width * depth,
            bytes_accessed=2 * depth * (height + 2 * width) + 8 * height * width,
            transcendentals=0,
        ),
    )(side, *inners, own_right, *rights)


def after(value, *earlier):
    return lax.optimization_barrier((value, *earlier))[0]


def pick(value, index, axis):
    return lax.dynamic_index_in_dim(value, index, axis, keepdims=False)


def shards(psi, left_ops, right_ops, block_mask):
    terms, n = lax.axis_size("term"), lax.axis_size("row")
    s = math.isqrt(n)
    assert s * s == n and terms == 2 * n and left_ops.shape[0] == 1
    height, width = psi.shape
    term, row = lax.axis_index("term"), lax.axis_index("row")
    core, z = term % 2, term // 2
    zh, zl = z // s, z % s
    hi, lo = row // s, row % s

    def from_lo(value, j):
        pairs = [(a * s + (b + j) % s, a * s + b) for a in range(s) for b in range(s)]
        return lax.ppermute(value, "row", pairs)

    def from_hi(value, j):
        pairs = [(((a + j) % s) * s + b, a * s + b) for a in range(s) for b in range(s)]
        return lax.ppermute(value, "row", pairs)

    def from_term(value, bit):
        return lax.ppermute(value, "term", [(a ^ bit, a) for a in range(terms)])

    def to_zl(value, j):
        pairs = [
            ((a * s + b) * 2 + c, (a * s + (b + j) % s) * 2 + c)
            for a in range(s) for b in range(s) for c in range(2)
        ]
        return lax.ppermute(value, "term", pairs)

    def to_zh(value, j):
        pairs = [
            ((a * s + b) * 2 + c, (((a + j) % s) * s + b) * 2 + c)
            for a in range(s) for b in range(s) for c in range(2)
        ]
        return lax.ppermute(value, "term", pairs)

    def crossed(value):
        pairs = [
            (((a * s + b) * 2 + c) * n + y * s + x, ((a * s + x) * 2 + c) * n + y * s + b)
            for a in range(s) for b in range(s) for c in range(2) for y in range(s) for x in range(s)
        ]
        return lax.ppermute(value, ("term", "row"), pairs)

    share = height // SHARE
    mine = term % SHARE
    own_share = lax.dynamic_slice_in_dim(psi, mine * share, share, 0)
    fetched = {(0, 0): own_share}
    for jx in range(1, s):
        fetched[0, jx] = from_lo(own_share, jx)
    for jx in range(s):
        for jy in range(1, s):
            fetched[jy, jx] = from_hi(fetched[0, jx], jy)
    parts, places = [psi], [row * height]
    for (jy, jx), value in fetched.items():
        if (jy, jx) == (0, 0):
            continue
        block = (hi + jy) % s * s + (lo + jx) % s
        along = from_term(value, 2)
        for bits, part in ((0, value), (1, from_term(value, 1)), (2, along), (3, from_term(along, 1))):
            parts.append(part)
            places.append(block * height + (mine ^ bits) * share)
    places = jnp.stack(places).astype(jnp.int32)

    left, mask = left_ops[0], block_mask[0]
    size = height // PIECES
    own_left = [masked_rows(left, mask, p * size, size) for p in range(PIECES)]
    earlier = [fetched[0, jx] for jx in range(1, s)]
    near_left = []
    for p in range(PIECES):
        got = [from_lo(after(own_left[p], *earlier), j) for j in range(1, s)]
        near_left.append(got)
        earlier = got

    wide = height // (2 * PIECES)
    own_right = right_ops[0].reshape(2, PIECES, wide, width)
    earlier = [fetched[jy, jx] for jy in range(1, s) for jx in range(s)]
    near_right = []
    for p in range(PIECES):
        got = [from_hi(after(own_right[:, p], *earlier), j) for j in range(1, s)]
        near_right.append(got)
        earlier = got

    inners = [inner_of(own_left, parts, places)]
    for j in range(s - 1):
        for p in range(PIECES):
            inners.append(inner_of([near_left[p][j]], parts, places))

    side = core.astype(jnp.int32).reshape(1)
    outs = []
    for p in range(PIECES):
        keep, give = outer_of(inners, own_right, p, near_right[p], side)
        total = (keep + from_term(give, 1)).reshape(s, height, s, wide)
        kept = pick(total, (zl - lo) % s, 0)
        for j in range(1, s):
            sent = pick(total, (zl + j - lo) % s, 0).astype(jnp.bfloat16)
            kept = kept + to_zl(sent, j).astype(jnp.float32)
        final = pick(kept, (zh - hi) % s, 1)
        for j in range(1, s):
            sent = pick(kept, (zh + j - hi) % s, 1).astype(jnp.bfloat16)
            final = final + to_zh(sent, j).astype(jnp.float32)
        outs.append(crossed(final.astype(jnp.bfloat16)))
    return jnp.concatenate(outs, 1)


def solution(mesh):
    in_specs = (
        P("row", None),
        P("term", "row", None),
        P("term", "row", None),
        P("term", "row", None),
    )
    out_specs = P("row", "term")
    return jax.shard_map(shards, mesh=mesh, in_specs=in_specs, out_specs=out_specs, check_vma=False)
```

time: 223 us -> 145 us (0.65)
  waiting for transfers between devices: 169 us -> 65.4 us
  Pallas kernels: 0 us -> 38.2 us
  starting transfers between devices: 0.3 us -> 24.8 us
  matrix products: 20.4 us -> 0 us
  between operations: 13.2 us -> 0.25 us
  other arithmetic: 7.72 us -> 4.55 us
    all_gather x2 -> x0, waiting for transfers between devices: 116 us -> none  [the longest x1 79.2 us: shards(): lax.all_gather(both_right, 'row', axis=1, tiled=True)]
    ppermute x2 -> x24, waiting for transfers between devices: 2.65 us -> 65.4 us  [the longest x11 23.7 us: from_term(): return lax.ppermute(value, 'term', [(a ^ bit, a) for a in range(terms)])]
    reduce_scatter x1 -> x0, waiting for transfers between devices: 50.2 us -> none  [shards(): lax.psum_scatter(partial_value, 'term', scatter_dimension=1, tiled=True)]
    pallas_call x0 -> x7, Pallas kernels: none -> 38.2 us  [the longest x3 26.1 us: inner_of(): pl.pallas_call(functools.partial(inner_kernel, len(rows), len(parts)), in...]
    ppermute x2 -> x24, starting transfers between devices: 0.21 us -> 24.8 us  [the longest x2 6.85 us: crossed(): return lax.ppermute(value, ('term', 'row'), pairs)]
    dot_general x3 -> x0, matrix products: 20.4 us -> none  [the longest x2 10.2 us: make_fold(): outputs.append(jnp.dot(columns, piece, preferred_element_type=jnp.float32))]
    mul x1 -> x0, other arithmetic: 4.45 us -> none  [shards(): left_ops * grid.reshape(local_terms, rows, width).astype(jnp.bfloat16)]
    convert_element_type x1 -> x2, local copies, waits for them, and re-layouts: 4.35 us -> 0.05 us  [shards(): sent = pick(kept, (zh + j - hi) % s, 1).astype(jnp.bfloat16)]
  transfers between devices with their start and end apart: 5 -> 24, of which waited for: 4 -> 10; matrix products, arithmetic and copies ran while one was open for 11% -> 7% of each run, Pallas kernels for 0% -> 26%
where the time goes in v1:
time: 145 us; the launch traced here: 144 us
  waiting for transfers between devices  65.4 us (45%)
  Pallas kernels  38.2 us (26%)
  starting transfers between devices  24.8 us (17%)
  local copies, waits for them, and re-layouts  11.2 us (8%)
  other arithmetic  4.55 us (3%)
    pallas_call x3, Pallas kernels, inner_of(): pl.pallas_call(functools.partial(inner_kernel, len(rows), len(parts)), in...  26.1 us
    ppermute x11, waiting for transfers between devices, from_term(): return lax.ppermute(value, 'term', [(a ^ bit, a) for a in range(terms)])  23.7 us
    ppermute x3, waiting for transfers between devices, from_lo(): return lax.ppermute(value, 'row', pairs)  13.3 us
    ppermute x4, waiting for transfers between devices, from_hi(): return lax.ppermute(value, 'row', pairs)  11.3 us
    pallas_call x2, Pallas kernels, outer_of(): pl.pallas_call(functools.partial(outer_kernel, len(inners), 1 + len(right...  9.45 us
    ppermute x2, waiting for transfers between devices, to_zl(): return lax.ppermute(value, 'term', pairs)  9.08 us
    ppermute x2, starting transfers between devices, crossed(): return lax.ppermute(value, ('term', 'row'), pairs)  6.85 us
    ppermute x2, waiting for transfers between devices, crossed(): return lax.ppermute(value, ('term', 'row'), pairs)  6.06 us
  transfers between devices with their start and end apart: 24, of which 10 were waited for; matrix products, arithmetic and copies ran while one was open for 7% of the time, Pallas kernels for 26%

profile of v1, /device:TPU:2, one launch (start us, length us, event | category | flops | bytes accessed | tf_op | source)
XLA Modules:
  0.0 144.3 jit_solution(5054114433717959807)
XLA Ops:
  0.0 1.1 constant_dynamic-slice_fusion.4
  1.1 0.1 collective-permute-start
  1.2 2.0 %collective-permute-start.4 = (bf16[128,2048]{1,0:T(8,128)(2,1)S(1)}, bf16[128,2048]{1,0:T(8,128)(2,1)S(1)}, u32[]{:S(2)}, u32[]{:S(2)}) collective-permute-start(bf16[128,2048]{1,0:T(8,128)(2,1)S(1)} %constant_dynamic-slice_fusion.4), channel_id=1, source_target_pairs={{2,0},{3,1},{0,2},{1,3},{6,4},{7,5},{4,6},{5,7},{10,8},{11,9},{8,1... | collective-permute-start | bytes 1572872 | tf_op jit(solution)/shard_map/ppermute | solution.py:177
  3.2 1.6 %copy-done = bf16[1,512,2048]{2,1,0:T(8,128)(2,1)S(1)} copy-done((bf16[1,512,2048]{2,1,0:T(8,128)(2,1)S(1)}, bf16[1,512,2048]{2,1,0:T(8,128)(2,1)}, u32[]{:S(2)}) %copy-start) | copy-done | bytes 2097176
  4.8 0.7 copy-done.4
  5.5 0.9 shard_map.46.refs_0_
  6.4 8.4 %collective-permute-done.refs_3_.refs_2_ = bf16[128,2048]{1,0:T(8,128)(2,1)S(1)} collective-permute-done((bf16[128,2048]{1,0:T(8,128)(2,1)S(1)}, bf16[128,2048]{1,0:T(8,128)(2,1)S(1)}, u32[]{:S(2)}, u32[]{:S(2)}) %collective-permute-start) | collective-permute-done | bytes 524320 | tf_op jit(solution)/shard_map/ppermute | solution.py:173
  14.8 0.3 collective-permute-start.12
  15.1 0.0 collective-permute-start.1
  15.1 1.8 %collective-permute-start.2 = (bf16[128,2048]{1,0:T(8,128)(2,1)S(1)}, bf16[128,2048]{1,0:T(8,128)(2,1)S(1)}, u32[]{:S(2)}, u32[]{:S(2)}) collective-permute-start(bf16[128,2048]{1,0:T(8,128)(2,1)S(1)} %collective-permute-done.refs_3_.refs_2_), channel_id=1, source_target_pairs={{8,0},{12,4},{0,8},{4,12},{24,16},{28,20},{16,24},{20,28},{9,1},{1... | collective-permute-start | bytes 1572872 | tf_op jit(solution)/shard_map/ppermute | solution.py:180
  16.9 1.5 %collective-permute-start.8 = (bf16[128,2048]{1,0:T(8,128)(2,1)S(1)}, bf16[128,2048]{1,0:T(8,128)(2,1)S(1)}, u32[]{:S(2)}, u32[]{:S(2)}) collective-permute-start(bf16[128,2048]{1,0:T(8,128)(2,1)S(1)} %collective-permute-done.refs_3_.refs_2_), channel_id=1, source_target_pairs={{2,0},{3,1},{0,2},{1,3},{6,4},{7,5},{4,6},{5,7},{10,8},{11,9},{8,1... | collective-permute-start | bytes 1572872 | tf_op jit(solution)/shard_map/ppermute | solution.py:177
  18.5 1.2 slice_bitcast_fusion.1
  19.7 0.0 collective-permute-done.4.refs_7_.refs_6_
  19.7 11.3 %collective-permute-done.8.refs_11_.refs_10_ = bf16[128,2048]{1,0:T(8,128)(2,1)S(1)} collective-permute-done((bf16[128,2048]{1,0:T(8,128)(2,1)S(1)}, bf16[128,2048]{1,0:T(8,128)(2,1)S(1)}, u32[]{:S(2)}, u32[]{:S(2)}) %collective-permute-start.8) | collective-permute-done | bytes 524320 | tf_op jit(solution)/shard_map/ppermute | solution.py:177
  31.0 1.5 %collective-permute-start.14 = (bf16[2,128,2048]{2,1,0:T(8,128)(2,1)S(1)}, bf16[2,128,2048]{2,1,0:T(8,128)(2,1)S(1)}, u32[]{:S(2)}, u32[]{:S(2)}) collective-permute-start(bf16[2,128,2048]{2,1,0:T(8,128)(2,1)S(1)} %get-tuple-element.15), channel_id=1, source_target_pairs={{2,0},{3,1},{0,2},{1,3},{6,4},{7,5},{4,6},{5,7},{10,8},{11,9},{8,1... | collective-permute-start | bytes 3145736 | tf_op jit(solution)/shard_map/ppermute | solution.py:177
  32.5 0.0 collective-permute-start.5
  32.5 0.0 collective-permute-done.1.refs_4_.refs_3_
  32.5 0.5 collective-permute-start.6
  33.0 1.6 %collective-permute-start.10 = (bf16[128,2048]{1,0:T(8,128)(2,1)S(1)}, bf16[128,2048]{1,0:T(8,128)(2,1)}, u32[]{:S(2)}, u32[]{:S(2)}) collective-permute-start(bf16[128,2048]{1,0:T(8,128)(2,1)S(1)} %collective-permute-done.8.refs_11_.refs_10_), channel_id=1, source_target_pairs={{8,0},{12,4},{0,8},{4,12},{24,16},{28,20},{16,24},{20,28},{9,1},{1... | collective-permute-start | bytes 1572872 | tf_op jit(solution)/shard_map/ppermute | solution.py:180
  34.5 0.0 collective-permute-done.5.refs_8_.refs_7_
  34.6 0.0 collective-permute-start.3
  34.6 12.8 %collective-permute-done.6.refs_9_.refs_8_ = bf16[128,2048]{1,0:T(8,128)(2,1)} collective-permute-done((bf16[128,2048]{1,0:T(8,128)(2,1)S(1)}, bf16[128,2048]{1,0:T(8,128)(2,1)}, u32[]{:S(2)}, u32[]{:S(2)}) %collective-permute-start.6) | collective-permute-done | bytes 524320 | tf_op jit(solution)/shard_map/ppermute | solution.py:180
  47.3 0.0 collective-permute-start.9
  47.3 10.8 %collective-permute-done.10.refs_13_.refs_12_ = bf16[128,2048]{1,0:T(8,128)(2,1)} collective-permute-done((bf16[128,2048]{1,0:T(8,128)(2,1)S(1)}, bf16[128,2048]{1,0:T(8,128)(2,1)}, u32[]{:S(2)}, u32[]{:S(2)}) %collective-permute-start.10) | collective-permute-done | bytes 524320 | tf_op jit(solution)/shard_map/ppermute | solution.py:180
  58.2 0.0 collective-permute-start.7
  58.2 0.5 collective-permute-start.11
  58.7 1.7 %shard_map.47.refs_1_ = bf16[256,2048]{1,0:T(8,128)(2,1)} custom-call(s32[4,16]{1,0:T(4,128)S(1)} %bitcast.50, bf16[512,2048]{1,0:T(8,128)(2,1)S(1)} %bitcast.48), custom_call_target="tpu_custom_call" | custom-call | flops 524288 | bytes 2097152 | tf_op jit(solution)/shard_map/pallas_call | solution.py:35
  60.4 0.0 collective-permute-done.14.refs_4_
  60.4 1.0 copy-done.5
  61.4 1.5 %collective-permute-start.13 = (bf16[256,2048]{1,0:T(8,128)(2,1)}, bf16[256,2048]{1,0:T(8,128)(2,1)}, u32[]{:S(2)}, u32[]{:S(2)}) collective-permute-start(bf16[256,2048]{1,0:T(8,128)(2,1)} %shard_map.47.refs_1_), channel_id=1, source_target_pairs={{1,0},{0,1},{3,2},{2,3},{5,4},{4,5},{7,6},{6,7},{9,8},{8,9},{11,10... | collective-permute-start | bytes 3145736 | tf_op jit(solution)/shard_map/ppermute | solution.py:173
  62.9 0.1 stack.55.place_ref
  63.0 0.0 collective-permute-done.3.refs_6_.refs_5_
  63.0 0.6 collective-permute-start.19
  63.6 7.8 %shard_map.49.refs_1_ = bf16[256,2048]{1,0:T(8,128)(2,1)} custom-call(s32[13]{0:T(128)S(1)} %stack.55.place_ref, bf16[256,2048]{1,0:T(8,128)(2,1)} %copy-done.9, bf16[512,2048]{1,0:T(8,128)(2,1)} %refs_1_.3, bf16[128,2048]{1,0:T(8,128)(2,1)S(1)} %collective-permute-done.refs_3_.refs_2_, bf16[128,2048]{1,0:T(8,128)(2,1)S(1)} %collective-permute-done.1.refs_4_.refs_3_, ...), custom_call_target="tpu_custom_call" | custom-call | flops 2147483648 | bytes 10485760 | tf_op jit(solution)/shard_map/pallas_call | solution.py:89
  71.4 10.6 %shard_map.48.refs_0_ = bf16[512,2048]{1,0:T(8,128)(2,1)} custom-call(s32[13]{0:T(128)S(1)} %stack.55.place_ref, bf16[256,2048]{1,0:T(8,128)(2,1)} %copy-done.1, bf16[256,2048]{1,0:T(8,128)(2,1)} %shard_map.47.refs_1_, bf16[512,2048]{1,0:T(8,128)(2,1)} %refs_1_.3, bf16[128,2048]{1,0:T(8,128)(2,1)S(1)} %collective-permute-done.refs_3_.refs_2_, ...), custom_call_target="tpu_custom_call" | custom-call | flops 4294967296 | bytes 12582912 | tf_op jit(solution)/shard_map/pallas_call | solution.py:89
  82.0 4.9 %collective-permute-done.13.refs_0_ = bf16[256,2048]{1,0:T(8,128)(2,1)} collective-permute-done((bf16[256,2048]{1,0:T(8,128)(2,1)}, bf16[256,2048]{1,0:T(8,128)(2,1)}, u32[]{:S(2)}, u32[]{:S(2)}) %collective-permute-start.13) | collective-permute-done | bytes 1048608 | tf_op jit(solution)/shard_map/ppermute | solution.py:173
  86.8 7.7 %shard_map.50.refs_2_ = bf16[256,2048]{1,0:T(8,128)(2,1)} custom-call(s32[13]{0:T(128)S(1)} %stack.55.place_ref, bf16[256,2048]{1,0:T(8,128)(2,1)} %collective-permute-done.13.refs_0_, bf16[512,2048]{1,0:T(8,128)(2,1)} %refs_1_.3, bf16[128,2048]{1,0:T(8,128)(2,1)S(1)} %collective-permute-done.refs_3_.refs_2_, ...), custom_call_target="tpu_custom_call" | custom-call | flops 2147483648 | bytes 10485760 | tf_op jit(solution)/shard_map/pallas_call | solution.py:89
  94.6 1.2 copy-done.3
  95.8 5.2 %shard_map.51 = (f32[1024,256]{1,0:T(8,128)S(1)}, f32[1024,256]{1,0:T(8,128)}) custom-call(s32[1]{0:T(128)} %bitcast.side_ref, bf16[512,2048]{1,0:T(8,128)(2,1)} %shard_map.48.refs_0_, bf16[256,2048]{1,0:T(8,128)(2,1)S(1)} %copy-done.2, bf16[256,2048]{1,0:T(8,128)(2,1)S(1)} %copy-done.3, bf16[2,2,128,2048]{3,2,1,0:T(8,128)(2,1)} %bitcast.51, ...), custom_call_target="tpu_custom_call" | custom-call | flops 2147483648 | bytes 8388608 | tf_op jit(solution)/shard_map/pallas_call | solution.py:135
  101.1 0.0 collective-permute-start.15
  101.1 0.0 collective-permute-done.19.refs_4_
  101.1 4.2 %shard_map.52 = (f32[1024,256]{1,0:T(8,128)S(1)}, f32[1024,256]{1,0:T(8,128)S(1)}) custom-call(s32[1]{0:T(128)} %bitcast.side_ref, bf16[512,2048]{1,0:T(8,128)(2,1)} %shard_map.48.refs_0_, bf16[256,2048]{1,0:T(8,128)(2,1)S(1)} %copy-done.2, bf16[256,2048]{1,0:T(8,128)(2,1)S(1)} %copy-done.3, bf16[2,2,128,2048]{3,2,1,0:T(8,128)(2,1)} %bitcast.52, ...), custom_call_target="tpu_custom_call" | custom-call | flops 2147483648 | bytes 8388608 | tf_op jit(solution)/shard_map/pallas_call | solution.py:135
  105.3 0.6 collective-permute-start.20
  105.9 0.0 collective-permute-done.15
  105.9 2.3 %add.171 = f32[1024,256]{1,0:T(8,128)} add(f32[1024,256]{1,0:T(8,128)S(1)} %get-tuple-element.16, f32[1024,256]{1,0:T(8,128)} %collective-permute-done.15) | non-fusion elementwise | flops 262144 | bytes 3145728 | tf_op jit(solution)/shard_map/add | solution.py:251
  108.2 1.7 %reshape.14 = f32[2,512,2,128]{3,2,1,0:T(2,128)S(1)} reshape(f32[1024,256]{1,0:T(8,128)} %add.171) | data formatting | bytes 2097152 | tf_op jit(solution)/shard_map/reshape | solution.py:251
  109.9 0.2 constant_dynamic-slice_fusion.2
  110.1 0.7 copy.29
  110.9 0.4 collective-permute-start.16
  111.3 0.8 constant_dynamic-slice_fusion.3
  112.1 1.4 add.185
  113.5 0.5 reshape.15
  114.1 0.2 constant_dynamic-slice_fusion
  114.3 1.6 %collective-permute-start.21 = (bf16[512,2,128]{2,0,1:T(8,128)(2,1)S(1)}, bf16[512,2,128]{2,0,1:T(8,128)(2,1)S(1)}, u32[]{:S(2)}, u32[]{:S(2)}) collective-permute-start(bf16[512,2,128]{2,0,1:T(8,128)(2,1)S(1)} %bitcast.54), channel_id=1, source_target_pairs={{0,8},{4,12},{8,0},{12,4},{16,24},{20,28},{24,16},{28,20},{1,9},{5... | collective-permute-start | bytes 786440 | tf_op jit(solution)/shard_map/ppermute | solution.py:187
  116.0 4.3 %collective-permute-done.16 = bf16[512,2,128]{2,0,1:T(8,128)(2,1)S(1)} collective-permute-done((bf16[512,2,128]{2,0,1:T(8,128)(2,1)}, bf16[512,2,128]{2,0,1:T(8,128)(2,1)S(1)}, u32[]{:S(2)}, u32[]{:S(2)}) %collective-permute-start.16) | collective-permute-done | bytes 262176 | tf_op jit(solution)/shard_map/ppermute | solution.py:187
  120.3 2.6 %collective-permute-start.17 = (bf16[512,128]{1,0:T(8,128)(2,1)S(1)}, bf16[512,128]{1,0:T(8,128)(2,1)S(1)}, u32[]{:S(2)}, u32[]{:S(2)}) collective-permute-start(bf16[512,128]{1,0:T(8,128)(2,1)S(1)} %fusion.4), channel_id=1, source_target_pairs={{0,16},{4,20},{8,24},{12,28},{16,0},{20,4},{24,8},{28,12},{1,17},{... | collective-permute-start | bytes 393224 | tf_op jit(solution)/shard_map/ppermute | solution.py:194
  123.0 4.8 %collective-permute-done.21 = bf16[512,2,128]{2,0,1:T(8,128)(2,1)S(1)} collective-permute-done((bf16[512,2,128]{2,0,1:T(8,128)(2,1)S(1)}, bf16[512,2,128]{2,0,1:T(8,128)(2,1)S(1)}, u32[]{:S(2)}, u32[]{:S(2)}) %collective-permute-start.21) | collective-permute-done | bytes 262176 | tf_op jit(solution)/shard_map/ppermute | solution.py:187
  127.9 0.7 collective-permute-start.22
  128.6 4.8 %collective-permute-start.18 = (bf16[512,128]{1,0:T(8,128)(2,1)S(1)}, bf16[512,128]{1,0:T(8,128)(2,1)S(1)}, u32[]{:S(2)}, u32[]{:S(2)}) collective-permute-start(bf16[512,128]{1,0:T(8,128)(2,1)S(1)} %fusion.3), channel_id=1, source_target_pairs={{0,0},{1,8},{2,2},{3,10},{4,4},{5,12},{6,6},{7,14},{8,1},{9,9},{10... | collective-permute-start | bytes 393224 | tf_op jit(solution)/shard_map/ppermute | solution.py:201
  133.4 2.0 %collective-permute-done.22 = bf16[512,128]{1,0:T(8,128)(2,1)S(1)} collective-permute-done((bf16[512,128]{1,0:T(8,128)(2,1)S(1)}, bf16[512,128]{1,0:T(8,128)(2,1)S(1)}, u32[]{:S(2)}, u32[]{:S(2)}) %collective-permute-start.22) | collective-permute-done | bytes 131104 | tf_op jit(solution)/shard_map/ppermute | solution.py:194
  135.5 2.1 %collective-permute-start.23 = (bf16[512,128]{1,0:T(8,128)(2,1)S(1)}, bf16[512,128]{1,0:T(8,128)(2,1)S(1)}, u32[]{:S(2)}, u32[]{:S(2)}) collective-permute-start(bf16[512,128]{1,0:T(8,128)(2,1)S(1)} %fusion.2), channel_id=1, source_target_pairs={{0,0},{1,8},{2,2},{3,10},{4,4},{5,12},{6,6},{7,14},{8,1},{9,9},{10... | collective-permute-start | bytes 393224 | tf_op jit(solution)/shard_map/ppermute | solution.py:201
  137.6 1.2 collective-permute-done.18
  138.8 4.8 %collective-permute-done.23 = bf16[512,128]{1,0:T(8,128)(2,1)S(1)} collective-permute-done((bf16[512,128]{1,0:T(8,128)(2,1)S(1)}, bf16[512,128]{1,0:T(8,128)(2,1)S(1)}, u32[]{:S(2)}, u32[]{:S(2)}) %collective-permute-start.23) | collective-permute-done | bytes 131104 | tf_op jit(solution)/shard_map/ppermute | solution.py:201
  143.6 0.7 pad_maximum_fusion
  (31 shorter events, 0.3 us)
Async XLA Ops:
  1.1 13.7 %collective-permute-start = (bf16[128,2048]{1,0:T(8,128)(2,1)S(1)}, bf16[128,2048]{1,0:T(8,128)(2,1)S(1)}, u32[]{:S(2)}, u32[]{:S(2)}) collective-permute-start(bf16[128,2048]{1,0:T(8,128)(2,1)S(1)} %constant_dynamic-slice_fusion.4), channel_id=1, source_target_pairs={{1,0},{0,1},{3,2},{2,3},{5,4},{4,5},{7,6},{6,7},{9,8},{8,9},{11,10... | collective-permute-start | bytes 1572872 | tf_op jit(solution)/shard_map/ppermute | solution.py:173
  1.2 18.5 %collective-permute-start.4 = (bf16[128,2048]{1,0:T(8,128)(2,1)S(1)}, bf16[128,2048]{1,0:T(8,128)(2,1)S(1)}, u32[]{:S(2)}, u32[]{:S(2)}) collective-permute-start(bf16[128,2048]{1,0:T(8,128)(2,1)S(1)} %constant_dynamic-slice_fusion.4), channel_id=1, source_target_pairs={{2,0},{3,1},{0,2},{1,3},{6,4},{7,5},{4,6},{5,7},{10,8},{11,9},{8,1... | collective-permute-start | bytes 1572872 | tf_op jit(solution)/shard_map/ppermute | solution.py:177
  3.2 1.6 %copy-start = (bf16[1,512,2048]{2,1,0:T(8,128)(2,1)S(1)}, bf16[1,512,2048]{2,1,0:T(8,128)(2,1)}, u32[]{:S(2)}) copy-start(bf16[1,512,2048]{2,1,0:T(8,128)(2,1)} %param.5) | copy-start | bytes 6291460
  4.8 0.7 copy-start.4
  5.5 13.0 %copy-start.7 = (bf16[1,512,2048]{2,1,0:T(8,128)(2,1)S(1)}, bf16[1,512,2048]{2,1,0:T(8,128)(2,1)}, u32[]{:S(2)}) copy-start(bf16[1,512,2048]{2,1,0:T(8,128)(2,1)} %param.6) | copy-start | bytes 6291460
  6.4 13.3 %copy-start.1 = (bf16[256,2048]{1,0:T(8,128)(2,1)}, bf16[256,2048]{1,0:T(8,128)(2,1)S(1)}, u32[]{:S(2)}) copy-start(bf16[256,2048]{1,0:T(8,128)(2,1)S(1)} %shard_map.46.refs_0_) | copy-start | bytes 3145732
  14.8 43.4 %collective-permute-start.12 = (bf16[256,2048]{1,0:T(8,128)(2,1)S(1)}, bf16[256,2048]{1,0:T(8,128)(2,1)S(1)}, u32[]{:S(2)}, u32[]{:S(2)}) collective-permute-start(bf16[256,2048]{1,0:T(8,128)(2,1)S(1)} %shard_map.46.refs_0_), channel_id=1, source_target_pairs={{1,0},{0,1},{3,2},{2,3},{5,4},{4,5},{7,6},{6,7},{9,8},{8,9},{11,10... | collective-permute-start | bytes 3145736 | tf_op jit(solution)/shard_map/ppermute | solution.py:173
  15.1 17.4 %collective-permute-start.1 = (bf16[128,2048]{1,0:T(8,128)(2,1)S(1)}, bf16[128,2048]{1,0:T(8,128)(2,1)S(1)}, u32[]{:S(2)}, u32[]{:S(2)}) collective-permute-start(bf16[128,2048]{1,0:T(8,128)(2,1)S(1)} %collective-permute-done.refs_3_.refs_2_), channel_id=1, source_target_pairs={{4,0},{0,4},{12,8},{8,12},{20,16},{16,20},{28,24},{24,28},{5,1},{1... | collective-permute-start | bytes 1572872 | tf_op jit(solution)/shard_map/ppermute | solution.py:180
  15.1 17.9 %collective-permute-start.2 = (bf16[128,2048]{1,0:T(8,128)(2,1)S(1)}, bf16[128,2048]{1,0:T(8,128)(2,1)S(1)}, u32[]{:S(2)}, u32[]{:S(2)}) collective-permute-start(bf16[128,2048]{1,0:T(8,128)(2,1)S(1)} %collective-permute-done.refs_3_.refs_2_), channel_id=1, source_target_pairs={{8,0},{12,4},{0,8},{4,12},{24,16},{28,20},{16,24},{20,28},{9,1},{1... | collective-permute-start | bytes 1572872 | tf_op jit(solution)/shard_map/ppermute | solution.py:180
  16.9 14.1 %collective-permute-start.8 = (bf16[128,2048]{1,0:T(8,128)(2,1)S(1)}, bf16[128,2048]{1,0:T(8,128)(2,1)S(1)}, u32[]{:S(2)}, u32[]{:S(2)}) collective-permute-start(bf16[128,2048]{1,0:T(8,128)(2,1)S(1)} %collective-permute-done.refs_3_.refs_2_), channel_id=1, source_target_pairs={{2,0},{3,1},{0,2},{1,3},{6,4},{7,5},{4,6},{5,7},{10,8},{11,9},{8,1... | collective-permute-start | bytes 1572872 | tf_op jit(solution)/shard_map/ppermute | solution.py:177
  31.0 29.4 %collective-permute-start.14 = (bf16[2,128,2048]{2,1,0:T(8,128)(2,1)S(1)}, bf16[2,128,2048]{2,1,0:T(8,128)(2,1)S(1)}, u32[]{:S(2)}, u32[]{:S(2)}) collective-permute-start(bf16[2,128,2048]{2,1,0:T(8,128)(2,1)S(1)} %get-tuple-element.15), channel_id=1, source_target_pairs={{2,0},{3,1},{0,2},{1,3},{6,4},{7,5},{4,6},{5,7},{10,8},{11,9},{8,1... | collective-permute-start | bytes 3145736 | tf_op jit(solution)/shard_map/ppermute | solution.py:177
  32.5 2.0 %collective-permute-start.5 = (bf16[128,2048]{1,0:T(8,128)(2,1)S(1)}, bf16[128,2048]{1,0:T(8,128)(2,1)S(1)}, u32[]{:S(2)}, u32[]{:S(2)}) collective-permute-start(bf16[128,2048]{1,0:T(8,128)(2,1)S(1)} %collective-permute-done.4.refs_7_.refs_6_), channel_id=1, source_target_pairs={{4,0},{0,4},{12,8},{8,12},{20,16},{16,20},{28,24},{24,28},{5,1},{1... | collective-permute-start | bytes 1572872 | tf_op jit(solution)/shard_map/ppermute | solution.py:180
  32.5 14.8 %collective-permute-start.6 = (bf16[128,2048]{1,0:T(8,128)(2,1)S(1)}, bf16[128,2048]{1,0:T(8,128)(2,1)}, u32[]{:S(2)}, u32[]{:S(2)}) collective-permute-start(bf16[128,2048]{1,0:T(8,128)(2,1)S(1)} %collective-permute-done.4.refs_7_.refs_6_), channel_id=1, source_target_pairs={{8,0},{12,4},{0,8},{4,12},{24,16},{28,20},{16,24},{20,28},{9,1},{1... | collective-permute-start | bytes 1572872 | tf_op jit(solution)/shard_map/ppermute | solution.py:180
  33.0 25.2 %collective-permute-start.10 = (bf16[128,2048]{1,0:T(8,128)(2,1)S(1)}, bf16[128,2048]{1,0:T(8,128)(2,1)}, u32[]{:S(2)}, u32[]{:S(2)}) collective-permute-start(bf16[128,2048]{1,0:T(8,128)(2,1)S(1)} %collective-permute-done.8.refs_11_.refs_10_), channel_id=1, source_target_pairs={{8,0},{12,4},{0,8},{4,12},{24,16},{28,20},{16,24},{20,28},{9,1},{1... | collective-permute-start | bytes 1572872 | tf_op jit(solution)/shard_map/ppermute | solution.py:180
  34.6 28.4 %collective-permute-start.3 = (bf16[128,2048]{1,0:T(8,128)(2,1)S(1)}, bf16[128,2048]{1,0:T(8,128)(2,1)}, u32[]{:S(2)}, u32[]{:S(2)}) collective-permute-start(bf16[128,2048]{1,0:T(8,128)(2,1)S(1)} %collective-permute-done.2.refs_5_.refs_4_), channel_id=1, source_target_pairs={{4,0},{0,4},{12,8},{8,12},{20,16},{16,20},{28,24},{24,28},{5,1},{1... | collective-permute-start | bytes 1572872 | tf_op jit(solution)/shard_map/ppermute | solution.py:180
  47.3 16.2 %collective-permute-start.9 = (bf16[128,2048]{1,0:T(8,128)(2,1)S(1)}, bf16[128,2048]{1,0:T(8,128)(2,1)}, u32[]{:S(2)}, u32[]{:S(2)}) collective-permute-start(bf16[128,2048]{1,0:T(8,128)(2,1)S(1)} %collective-permute-done.8.refs_11_.refs_10_), channel_id=1, source_target_pairs={{4,0},{0,4},{12,8},{8,12},{20,16},{16,20},{28,24},{24,28},{5,1},{1... | collective-permute-start | bytes 1572872 | tf_op jit(solution)/shard_map/ppermute | solution.py:180
  58.2 5.4 %collective-permute-start.7 = (bf16[128,2048]{1,0:T(8,128)(2,1)}, bf16[128,2048]{1,0:T(8,128)(2,1)}, u32[]{:S(2)}, u32[]{:S(2)}) collective-permute-start(bf16[128,2048]{1,0:T(8,128)(2,1)} %collective-permute-done.6.refs_9_.refs_8_), channel_id=1, source_target_pairs={{4,0},{0,4},{12,8},{8,12},{20,16},{16,20},{28,24},{24,28},{5,1},{1... | collective-permute-start | bytes 1572872 | tf_op jit(solution)/shard_map/ppermute | solution.py:180
  58.2 2.2 %copy-start.9 = (bf16[256,2048]{1,0:T(8,128)(2,1)}, bf16[256,2048]{1,0:T(8,128)(2,1)S(1)}, u32[]{:S(2)}) copy-start(bf16[256,2048]{1,0:T(8,128)(2,1)S(1)} %collective-permute-done.12.refs_0_) | copy-start | bytes 3145732
  58.2 5.3 %collective-permute-start.11 = (bf16[128,2048]{1,0:T(8,128)(2,1)}, bf16[128,2048]{1,0:T(8,128)(2,1)}, u32[]{:S(2)}, u32[]{:S(2)}) collective-permute-start(bf16[128,2048]{1,0:T(8,128)(2,1)} %collective-permute-done.10.refs_13_.refs_12_), channel_id=1, source_target_pairs={{4,0},{0,4},{12,8},{8,12},{20,16},{16,20},{28,24},{24,28},{5,1},{1... | collective-permute-start | bytes 1572872 | tf_op jit(solution)/shard_map/ppermute | solution.py:180
  60.4 1.0 copy-start.5
  61.4 25.4 %collective-permute-start.13 = (bf16[256,2048]{1,0:T(8,128)(2,1)}, bf16[256,2048]{1,0:T(8,128)(2,1)}, u32[]{:S(2)}, u32[]{:S(2)}) collective-permute-start(bf16[256,2048]{1,0:T(8,128)(2,1)} %shard_map.47.refs_1_), channel_id=1, source_target_pairs={{1,0},{0,1},{3,2},{2,3},{5,4},{4,5},{7,6},{6,7},{9,8},{8,9},{11,10... | collective-permute-start | bytes 3145736 | tf_op jit(solution)/shard_map/ppermute | solution.py:173
  63.0 38.1 %collective-permute-start.19 = (bf16[2,128,2048]{2,1,0:T(8,128)(2,1)}, bf16[2,128,2048]{2,1,0:T(8,128)(2,1)S(1)}, u32[]{:S(2)}, u32[]{:S(2)}) collective-permute-start(bf16[2,128,2048]{2,1,0:T(8,128)(2,1)} %get-tuple-element.18), channel_id=1, source_target_pairs={{2,0},{3,1},{0,2},{1,3},{6,4},{7,5},{4,6},{5,7},{10,8},{11,9},{8,1... | collective-permute-start | bytes 3145736 | tf_op jit(solution)/shard_map/ppermute | solution.py:177
  82.0 12.6 %copy-start.2 = (bf16[256,2048]{1,0:T(8,128)(2,1)S(1)}, bf16[256,2048]{1,0:T(8,128)(2,1)}, u32[]{:S(2)}) copy-start(bf16[256,2048]{1,0:T(8,128)(2,1)} %shard_map.49.refs_1_) | copy-start | bytes 3145732
  82.0 12.6 %copy-start.6 = (bf16[2,128,2048]{2,1,0:T(8,128)(2,1)S(1)}, bf16[2,128,2048]{2,1,0:T(8,128)(2,1)}, u32[]{:S(2)}) copy-start(bf16[2,128,2048]{2,1,0:T(8,128)(2,1)} %copy-done.5) | copy-start | bytes 3145732
  94.6 1.2 copy-start.3
  101.1 4.8 %collective-permute-start.15 = (f32[1024,256]{1,0:T(8,128)}, f32[1024,256]{1,0:T(8,128)}, u32[]{:S(2)}, u32[]{:S(2)}) collective-permute-start(f32[1024,256]{1,0:T(8,128)} %get-tuple-element.17), channel_id=1, source_target_pairs={{4,0},{0,4},{12,8},{8,12},{20,16},{16,20},{28,24},{24,28},{5,1},{1... | collective-permute-start | bytes 3145736 | tf_op jit(solution)/shard_map/ppermute | solution.py:180
  105.3 6.9 %collective-permute-start.20 = (f32[1024,256]{1,0:T(8,128)S(1)}, f32[1024,256]{1,0:T(8,128)}, u32[]{:S(2)}, u32[]{:S(2)}) collective-permute-start(f32[1024,256]{1,0:T(8,128)S(1)} %get-tuple-element.20), channel_id=1, source_target_pairs={{4,0},{0,4},{12,8},{8,12},{20,16},{16,20},{28,24},{24,28},{5,1},{1... | collective-permute-start | bytes 3145736 | tf_op jit(solution)/shard_map/ppermute | solution.py:180
  110.9 9.4 %collective-permute-start.16 = (bf16[512,2,128]{2,0,1:T(8,128)(2,1)}, bf16[512,2,128]{2,0,1:T(8,128)(2,1)S(1)}, u32[]{:S(2)}, u32[]{:S(2)}) collective-permute-start(bf16[512,2,128]{2,0,1:T(8,128)(2,1)} %bitcast.45), channel_id=1, source_target_pairs={{0,8},{4,12},{8,0},{12,4},{16,24},{20,28},{24,16},{28,20},{1,9},{5... | collective-permute-start | bytes 786440 | tf_op jit(solution)/shard_map/ppermute | solution.py:187
  113.5 6.7 %copy-start.8 = (f32[1,512,2,128]{3,2,1,0:T(2,128)S(1)}, f32[1,512,2,128]{3,2,1,0:T(2,128)}, u32[]{:S(2)}) copy-start(f32[1,512,2,128]{3,2,1,0:T(2,128)} %constant_dynamic-slice_fusion.3) | copy-start | bytes 1572868
  114.3 13.5 %collective-permute-start.21 = (bf16[512,2,128]{2,0,1:T(8,128)(2,1)S(1)}, bf16[512,2,128]{2,0,1:T(8,128)(2,1)S(1)}, u32[]{:S(2)}, u32[]{:S(2)}) collective-permute-start(bf16[512,2,128]{2,0,1:T(8,128)(2,1)S(1)} %bitcast.54), channel_id=1, source_target_pairs={{0,8},{4,12},{8,0},{12,4},{16,24},{20,28},{24,16},{28,20},{1,9},{5... | collective-permute-start | bytes 786440 | tf_op jit(solution)/shard_map/ppermute | solution.py:187
  120.3 8.3 %collective-permute-start.17 = (bf16[512,128]{1,0:T(8,128)(2,1)S(1)}, bf16[512,128]{1,0:T(8,128)(2,1)S(1)}, u32[]{:S(2)}, u32[]{:S(2)}) collective-permute-start(bf16[512,128]{1,0:T(8,128)(2,1)S(1)} %fusion.4), channel_id=1, source_target_pairs={{0,16},{4,20},{8,24},{12,28},{16,0},{20,4},{24,8},{28,12},{1,17},{... | collective-permute-start | bytes 393224 | tf_op jit(solution)/shard_map/ppermute | solution.py:194
  127.9 7.6 %collective-permute-start.22 = (bf16[512,128]{1,0:T(8,128)(2,1)S(1)}, bf16[512,128]{1,0:T(8,128)(2,1)S(1)}, u32[]{:S(2)}, u32[]{:S(2)}) collective-permute-start(bf16[512,128]{1,0:T(8,128)(2,1)S(1)} %fusion.5), channel_id=1, source_target_pairs={{0,16},{4,20},{8,24},{12,28},{16,0},{20,4},{24,8},{28,12},{1,17},{... | collective-permute-start | bytes 393224 | tf_op jit(solution)/shard_map/ppermute | solution.py:194
  128.6 10.2 %collective-permute-start.18 = (bf16[512,128]{1,0:T(8,128)(2,1)S(1)}, bf16[512,128]{1,0:T(8,128)(2,1)S(1)}, u32[]{:S(2)}, u32[]{:S(2)}) collective-permute-start(bf16[512,128]{1,0:T(8,128)(2,1)S(1)} %fusion.3), channel_id=1, source_target_pairs={{0,0},{1,8},{2,2},{3,10},{4,4},{5,12},{6,6},{7,14},{8,1},{9,9},{10... | collective-permute-start | bytes 393224 | tf_op jit(solution)/shard_map/ppermute | solution.py:201
  135.5 8.1 %collective-permute-start.23 = (bf16[512,128]{1,0:T(8,128)(2,1)S(1)}, bf16[512,128]{1,0:T(8,128)(2,1)S(1)}, u32[]{:S(2)}, u32[]{:S(2)}) collective-permute-start(bf16[512,128]{1,0:T(8,128)(2,1)S(1)} %fusion.2), channel_id=1, source_target_pairs={{0,0},{1,8},{2,2},{3,10},{4,4},{5,12},{6,6},{7,14},{8,1},{9,9},{10... | collective-permute-start | bytes 393224 | tf_op jit(solution)/shard_map/ppermute | solution.py:201

commit v2 on v1

v2 whole, which is shorter than its diff:
```python
import functools
import math

import jax
import jax.numpy as jnp
from jax import lax
from jax.experimental import pallas as pl
from jax.experimental.pallas import tpu as pltpu
from jax.sharding import PartitionSpec as P

SHARE = 4
PIECES = 2
VMEM_BYTES = 20 * 1024 * 1024
COST = pl.CostEstimate(flops=1, bytes_accessed=1, transcendentals=0)
WHOLE = pl.BlockSpec(memory_space=pltpu.VMEM)
SCALARS = pl.BlockSpec(memory_space=pltpu.SMEM)
ANYWHERE = pl.BlockSpec(memory_space=pl.ANY)


def params():
    return pltpu.CompilerParams(vmem_limit_bytes=VMEM_BYTES)


def mask_kernel(blk, mask_ref, left_ref, out_ref):
    for j in range(left_ref.shape[1] // blk):
        keep = mask_ref[pl.program_id(0), j] != 0
        cols = pl.ds(j * blk, blk)
        tile = left_ref[:, cols]
        out_ref[:, cols] = jnp.where(keep, tile, jnp.zeros_like(tile))


def masked_rows(left, mask):
    rows, width = left.shape
    blk = width // mask.shape[1]
    spec = pl.BlockSpec((blk, width), lambda i: (i, 0))
    return pl.pallas_call(
        functools.partial(mask_kernel, blk),
        grid=(rows // blk,),
        in_specs=[SCALARS, spec],
        out_specs=spec,
        out_shape=jax.ShapeDtypeStruct((rows, width), left.dtype),
        compiler_params=params(),
        cost_estimate=COST,
    )(mask, left)


def stack_kernel(*refs):
    part_refs, (whole, sems) = refs[:-2], refs[-2:]
    copies, at = [], 0
    for p, part in enumerate(part_refs):
        size = part.shape[0]
        copies.append(pltpu.make_async_copy(part, whole.at[pl.ds(at, size)], sems.at[p]))
        at += size
    for copy in copies:
        copy.start()
    for copy in copies:
        copy.wait()


def stacked(parts):
    depth, width = sum(a.shape[0] for a in parts), parts[0].shape[1]
    return pl.pallas_call(
        stack_kernel,
        in_specs=[ANYWHERE] * len(parts),
        out_specs=ANYWHERE,
        out_shape=jax.ShapeDtypeStruct((depth, width), parts[0].dtype),
        scratch_shapes=[pltpu.SemaphoreType.DMA((len(parts),))],
        compiler_params=params(),
        cost_estimate=COST,
    )(*parts)


def inner_kernel(sizes, place_ref, rows_ref, *refs):
    part_refs, (out_ref, ordered) = refs[:-2], refs[-2:]

    @pl.when(pl.program_id(0) == 0)
    def _():
        at = 0
        for p, size in enumerate(sizes):
            cols = pl.ds(pl.multiple_of(place_ref[p], size), size)
            ordered[:, at : at + size] = rows_ref[:, cols]
            at += size

    psi = jnp.concatenate([ref[...] for ref in part_refs], 0)
    unit = math.gcd(rows_ref.shape[0], 256)
    for i in range(rows_ref.shape[0] // unit):
        rows = pl.ds(i * unit, unit)
        value = jnp.dot(ordered[rows, :], psi, preferred_element_type=jnp.float32)
        out_ref[rows, :] = value.astype(out_ref.dtype)


def inner_of(rows, parts, sizes, places):
    height, depth = rows.shape
    width = parts[0].shape[1]
    step = math.gcd(width, 512)
    return pl.pallas_call(
        functools.partial(inner_kernel, sizes),
        grid=(width // step,),
        in_specs=[SCALARS, pl.BlockSpec((height, depth), lambda j: (0, 0))]
        + [pl.BlockSpec((a.shape[0], step), lambda j: (0, j)) for a in parts],
        out_specs=pl.BlockSpec((height, step), lambda j: (0, j)),
        out_shape=jax.ShapeDtypeStruct((height, width), parts[0].dtype),
        scratch_shapes=[pltpu.VMEM((height, depth), rows.dtype)],
        compiler_params=params(),
        cost_estimate=COST,
    )(places, rows, *parts)


def outer_kernel(n_inner, n_right, side_ref, *refs):
    inner_refs = refs[:n_inner]
    right_refs = refs[n_inner : n_inner + n_right]
    keep_ref, give_ref = refs[n_inner + n_right :]
    side = side_ref[0]
    wide = keep_ref.shape[2]
    for half, out_ref in ((1 - side, give_ref), (side, keep_ref)):
        right = jnp.concatenate([ref[half] for ref in right_refs], 0)
        at = 0
        for ref in inner_refs:
            unit = math.gcd(ref.shape[0], 256)
            for i in range(ref.shape[0] // unit):
                value = lax.dot_general(
                    ref[i * unit : (i + 1) * unit, :],
                    right,
                    (((1,), (1,)), ((), ())),
                    preferred_element_type=jnp.float32,
                )
                for j in range(n_right):
                    out_ref[j, at : at + unit, :] = value[:, j * wide : (j + 1) * wide]
                at += unit


def outer_of(inners, piece, rights, side):
    height = sum(a.shape[0] for a in inners)
    halves, pieces, wide, depth = rights[0].shape
    n_right = len(rights)
    shape = jax.ShapeDtypeStruct((n_right, height, wide), jnp.float32)
    spec = pl.BlockSpec((halves, None, wide, depth), lambda i: (0, piece, 0, 0))
    return pl.pallas_call(
        functools.partial(outer_kernel, len(inners), n_right),
        grid=(1,),
        in_specs=[SCALARS] + [WHOLE] * len(inners) + [spec] * n_right,
        out_specs=[WHOLE, WHOLE],
        out_shape=[shape, shape],
        compiler_params=params(),
        cost_estimate=COST,
    )(side.astype(jnp.int32).reshape(1), *inners, *rights)


def cores_kernel(index_ref, keep_ref, got_ref, kept_ref, sent_ref):
    height = kept_ref.shape[1]
    for k in range(index_ref.shape[0]):
        rows = pl.ds(pl.multiple_of(index_ref[k] * height, height), height)
        for j in range(kept_ref.shape[0]):
            total = keep_ref[j, rows, :] + got_ref[j, rows, :]
            if k == 0:
                kept_ref[j] = total
            else:
                sent_ref[k - 1, j] = total.astype(sent_ref.dtype)


def cores_summed(keep, got, index, height):
    blocks, _, wide = keep.shape
    others = index.shape[0] - 1
    return pl.pallas_call(
        cores_kernel,
        in_specs=[SCALARS, WHOLE, WHOLE],
        out_specs=[WHOLE, WHOLE],
        out_shape=[
            jax.ShapeDtypeStruct((blocks, height, wide), jnp.float32),
            jax.ShapeDtypeStruct((others, blocks, height, wide), jnp.bfloat16),
        ],
        compiler_params=params(),
        cost_estimate=COST,
    )(index, keep, got)


def planes_kernel(n_got, index_ref, kept_ref, *refs):
    got_refs = refs[:n_got]
    final_ref, sent_ref = refs[n_got:]
    for k in range(index_ref.shape[0]):
        block = index_ref[k]
        total = kept_ref[block]
        for ref in got_refs:
            total = total + ref[block].astype(jnp.float32)
        if k == 0:
            final_ref[...] = total
        else:
            sent_ref[k - 1] = total.astype(sent_ref.dtype)


def planes_summed(kept, got, index):
    blocks, height, wide = kept.shape
    return pl.pallas_call(
        functools.partial(planes_kernel, len(got)),
        in_specs=[SCALARS] + [WHOLE] * (1 + len(got)),
        out_specs=[WHOLE, WHOLE],
        out_shape=[
            jax.ShapeDtypeStruct((height, wide), jnp.float32),
            jax.ShapeDtypeStruct((blocks - 1, height, wide), jnp.bfloat16),
        ],
        compiler_params=params(),
        cost_estimate=COST,
    )(index, kept, *got)


def after(value, *earlier):
    return lax.optimization_barrier((value, *earlier))[0]


def shards(psi, left_ops, right_ops, block_mask):
    terms, n = lax.axis_size("term"), lax.axis_size("row")
    s = math.isqrt(n)
    assert s * s == n and terms == 2 * n and left_ops.shape[0] == 1
    height, width = psi.shape
    term, row = lax.axis_index("term"), lax.axis_index("row")
    core, z = term % 2, term // 2
    zh, zl = z // s, z % s
    hi, lo = row // s, row % s

    def from_lo(value, j):
        pairs = [(a * s + (b + j) % s, a * s + b) for a in range(s) for b in range(s)]
        return lax.ppermute(value, "row", pairs)

    def from_hi(value, j):
        pairs = [(((a + j) % s) * s + b, a * s + b) for a in range(s) for b in range(s)]
        return lax.ppermute(value, "row", pairs)

    def from_term(value, bit):
        return lax.ppermute(value, "term", [(a ^ bit, a) for a in range(terms)])

    def to_zl(value, j):
        pairs = [
            ((a * s + b) * 2 + c, (a * s + (b + j) % s) * 2 + c)
            for a in range(s) for b in range(s) for c in range(2)
        ]
        return lax.ppermute(value, "term", pairs)

    def to_zh(value, j):
        pairs = [
            ((a * s + b) * 2 + c, (((a + j) % s) * s + b) * 2 + c)
            for a in range(s) for b in range(s) for c in range(2)
        ]
        return lax.ppermute(value, "term", pairs)

    def crossed(value):
        pairs = [
            (((a * s + b) * 2 + c) * n + y * s + x, ((a * s + x) * 2 + c) * n + y * s + b)
            for a in range(s) for b in range(s) for c in range(2) for y in range(s) for x in range(s)
        ]
        return lax.ppermute(value, ("term", "row"), pairs)

    sharing = min(SHARE, max(1, height // 128))
    share = height // sharing
    mine = term % sharing
    own_share = lax.dynamic_slice_in_dim(psi, mine * share, share, 0)
    depth = n * height

    def place(jy, jx, bits):
        return ((hi + jy) % s * s + (lo + jx) % s) * height + (mine ^ bits) * share

    near_x = [from_lo(own_share, j) for j in range(1, s)]
    near_y = [from_hi(own_share, j) for j in range(1, s)]
    near_x, near_y, own_left = lax.optimization_barrier(
        (near_x, near_y, masked_rows(left_ops[0], block_mask[0]))
    )
    far = [from_hi(v, jy) for jy in range(1, s) for v in near_x]
    at_near = [(0, j) for j in range(1, s)] + [(j, 0) for j in range(1, s)]
    at_far = [(jy, jx) for jy in range(1, s) for jx in range(1, s)]
    near = jnp.concatenate(near_x + near_y, 0)
    far = jnp.concatenate(far, 0)
    first, last = [(at_near, 0, near), (at_far, 0, far)], []
    if sharing > 1:
        near_core = from_term(near, 1)
        first += [(at_near, 1, near_core), (at_far, 1, from_term(far, 1))]
    early = stacked([psi] + [v for _, _, v in first])
    if sharing > 2:
        near_z, far_z = from_term(near, 2), from_term(far, 2)
        last = [(at_near, 2, near_z), (at_far, 2, far_z)]
        last += [(at_near, 3, from_term(after(near_z, early), 1)), (at_far, 3, from_term(far_z, 1))]
    parts = [early] + [v for _, _, v in last]
    held = [place(*at, bits) for group, bits, _ in first + last for at in group]
    sizes = [height] + [share] * len(held)
    places = jnp.stack([row * height] + held).astype(jnp.int32)

    near_left = [from_lo(own_left, j) for j in range(1, s)]
    own_right = after(right_ops[0], far if sharing == 1 else near_core)
    rights = [own_right] + [from_hi(own_right, j) for j in range(1, s)]
    rights = [a.reshape(2, PIECES, height // (2 * PIECES), width) for a in rights]

    inners = [inner_of(own_left, parts, sizes, places)]
    for rows in near_left:
        inners.append(inner_of(after(rows, inners[-1]), parts, sizes, places))

    def members(own, base):
        return jnp.stack([(own + j - base) % s for j in range(s)]).astype(jnp.int32)

    outs = []
    for p in range(PIECES):
        keep, give = outer_of(inners, p, rights, core)
        kept, sent = cores_summed(keep, from_term(give, 1), members(zl, lo), height)
        got = [to_zl(sent[j - 1], j) for j in range(1, s)]
        final, sent = planes_summed(kept, got, members(zh, hi))
        for j in range(1, s):
            final = final + to_zh(sent[j - 1], j).astype(jnp.float32)
        outs.append(crossed(final.astype(jnp.bfloat16)))
    return jnp.concatenate(outs, 1)


def solution(mesh):
    in_specs = (
        P("row", None),
        P("term", "row", None),
        P("term", "row", None),
        P("term", "row", None),
    )
    out_specs = P("row", "term")
    return jax.shard_map(shards, mesh=mesh, in_specs=in_specs, out_specs=out_specs, check_vma=False)
```

time: 145 us -> 121 us (0.83)
  Pallas kernels: 38.2 us -> 29.1 us
  waiting for transfers between devices: 65.4 us -> 58.1 us
  other arithmetic: 4.55 us -> 0.95 us
  local copies, waits for them, and re-layouts: 11.2 us -> 9.15 us
  starting transfers between devices: 24.8 us -> 22.8 us
    pallas_call x7 -> x10, Pallas kernels: 38.2 us -> 29.1 us  [the longest x2 15.1 us: inner_of(): pl.pallas_call(functools.partial(inner_kernel, sizes), grid=(width // ste...]
    ppermute x3 -> x2, waiting for transfers between devices: 13.3 us -> 8.63 us  [from_lo(): return lax.ppermute(value, 'row', pairs)]
    add x4 -> x0, other arithmetic: 3.76 us -> none  [the longest x2 3.67 us: shards(): total = (keep + from_term(give, 1)).reshape(s, height, s, wide)]
    unnamed x22 -> x17, local copies, waits for them, and re-layouts: 5.26 us -> 7.94 us
    ppermute x11 -> x8, waiting for transfers between devices: 23.7 us -> 21.2 us  [from_term(): return lax.ppermute(value, 'term', [(a ^ bit, a) for a in range(terms)])]
    reshape x2 -> x0, local copies, waits for them, and re-layouts: 2.28 us -> none  [shards(): total = (keep + from_term(give, 1)).reshape(s, height, s, wide)]
    ppermute x4 -> x3, starting transfers between devices: 5.65 us -> 4.31 us  [from_hi(): return lax.ppermute(value, 'row', pairs)]
    ppermute x4 -> x3, waiting for transfers between devices: 11.3 us -> 10.2 us  [from_hi(): return lax.ppermute(value, 'row', pairs)]
  transfers between devices with their start and end apart: 24 -> 19, of which waited for: 10 -> 14; matrix products, arithmetic and copies ran while one was open for 7% -> 0% of each run, Pallas kernels for 26% -> 21%
where the time goes in v2:
time: 121 us; the launch traced here: 120 us
  waiting for transfers between devices  58.1 us (48%)
  Pallas kernels  29.1 us (24%)
  starting transfers between devices  22.8 us (19%)
  local copies, waits for them, and re-layouts  9.15 us (8%)
    ppermute x8, waiting for transfers between devices, from_term(): return lax.ppermute(value, 'term', [(a ^ bit, a) for a in range(terms)])  21.2 us
    pallas_call x2, Pallas kernels, inner_of(): pl.pallas_call(functools.partial(inner_kernel, sizes), grid=(width // ste...  15.1 us
    ppermute x3, waiting for transfers between devices, from_hi(): return lax.ppermute(value, 'row', pairs)  10.2 us
    ppermute x2, waiting for transfers between devices, to_zl(): return lax.ppermute(value, 'term', pairs)  10.1 us
    ppermute x2, waiting for transfers between devices, from_lo(): return lax.ppermute(value, 'row', pairs)  8.63 us
    unnamed x17, local copies, waits for them, and re-layouts  7.94 us
    pallas_call x2, Pallas kernels, outer_of(): pl.pallas_call(functools.partial(outer_kernel, len(inners), n_right), gri...  7.82 us
    ppermute x2, starting transfers between devices, crossed(): return lax.ppermute(value, ('term', 'row'), pairs)  7.1 us
  transfers between devices with their start and end apart: 19, of which 14 were waited for; matrix products, arithmetic and copies ran while one was open for 0% of the time, Pallas kernels for 21%

profile of v2, /device:TPU:2, one launch (start us, length us, event | category | flops | bytes accessed | tf_op | source)
XLA Modules:
  0.0 120.2 jit_solution(2391113280430293015)
XLA Ops:
  0.0 1.1 constant_dynamic-slice_fusion
  1.1 0.1 collective-permute-start
  1.2 2.0 %collective-permute-start.1 = (bf16[128,2048]{1,0:T(8,128)(2,1)S(1)}, bf16[128,2048]{1,0:T(8,128)(2,1)S(1)}, u32[]{:S(2)}, u32[]{:S(2)}) collective-permute-start(bf16[128,2048]{1,0:T(8,128)(2,1)S(1)} %constant_dynamic-slice_fusion), channel_id=1, source_target_pairs={{2,0},{3,1},{0,2},{1,3},{6,4},{7,5},{4,6},{5,7},{10,8},{11,9},{8,1... | collective-permute-start | bytes 1572872 | tf_op jit(solution)/shard_map/ppermute | solution.py:226
  3.2 0.0 copy-start.4
  3.2 1.6 %copy-done.4 = bf16[1,512,2048]{2,1,0:T(8,128)(2,1)S(1)} copy-done((bf16[1,512,2048]{2,1,0:T(8,128)(2,1)S(1)}, bf16[1,512,2048]{2,1,0:T(8,128)(2,1)}, u32[]{:S(2)}) %copy-start.4) | copy-done | bytes 2097176
  4.8 0.7 copy-done.7
  5.5 1.2 %shard_map.46.rows_ref = bf16[512,2048]{1,0:T(8,128)(2,1)S(1)} custom-call(s32[4,16]{1,0:T(4,128)S(1)} %bitcast.28, bf16[512,2048]{1,0:T(8,128)(2,1)S(1)} %bitcast.27), custom_call_target="tpu_custom_call" | custom-call | flops 1 | bytes 1 | tf_op jit(solution)/shard_map/pallas_call | solution.py:36
  6.7 0.0 copy-start.3
  6.7 8.1 %collective-permute-done = bf16[128,2048]{1,0:T(8,128)(2,1)S(1)} collective-permute-done((bf16[128,2048]{1,0:T(8,128)(2,1)S(1)}, bf16[128,2048]{1,0:T(8,128)(2,1)S(1)}, u32[]{:S(2)}, u32[]{:S(2)}) %collective-permute-start) | collective-permute-done | bytes 524320 | tf_op jit(solution)/shard_map/ppermute | solution.py:222
  14.8 0.1 collective-permute-done.1
  15.0 0.1 collective-permute-start.3
  15.1 1.8 %collective-permute-start.2 = (bf16[128,2048]{1,0:T(8,128)(2,1)S(1)}, bf16[128,2048]{1,0:T(8,128)(2,1)S(1)}, u32[]{:S(2)}, u32[]{:S(2)}) collective-permute-start(bf16[128,2048]{1,0:T(8,128)(2,1)S(1)} %collective-permute-done), channel_id=1, source_target_pairs={{2,0},{3,1},{0,2},{1,3},{6,4},{7,5},{4,6},{5,7},{10,8},{11,9},{8,1... | collective-permute-start | bytes 1572872 | tf_op jit(solution)/shard_map/ppermute | solution.py:226
  16.8 1.6 %collective-permute-start.5 = (bf16[256,2048]{1,0:T(8,128)(2,1)S(1)}, bf16[256,2048]{1,0:T(8,128)(2,1)S(1)}, u32[]{:S(2)}, u32[]{:S(2)}) collective-permute-start(bf16[256,2048]{1,0:T(8,128)(2,1)S(1)} %constant_dynamic-update-slice_fusion.refs_1_), channel_id=1, source_target_pairs={{8,0},{12,4},{0,8},{4,12},{24,16},{28,20},{16,24},{20,28},{9,1},{1... | collective-permute-start | bytes 3145736 | tf_op jit(solution)/shard_map/ppermute | solution.py:229
  18.4 1.5 %collective-permute-start.9 = (bf16[512,2048]{1,0:T(8,128)(2,1)S(1)}, bf16[512,2048]{1,0:T(8,128)(2,1)}, u32[]{:S(2)}, u32[]{:S(2)}) collective-permute-start(bf16[512,2048]{1,0:T(8,128)(2,1)S(1)} %shard_map.46.rows_ref), channel_id=1, source_target_pairs={{1,0},{0,1},{3,2},{2,3},{5,4},{4,5},{7,6},{6,7},{9,8},{8,9},{11,10... | collective-permute-start | bytes 6291464 | tf_op jit(solution)/shard_map/ppermute | solution.py:222
  19.9 0.0 collective-permute-done.3.refs_3_
  19.9 0.5 collective-permute-start.10
  20.4 9.4 %collective-permute-done.2.refs_2_ = bf16[128,2048]{1,0:T(8,128)(2,1)S(1)} collective-permute-done((bf16[128,2048]{1,0:T(8,128)(2,1)S(1)}, bf16[128,2048]{1,0:T(8,128)(2,1)S(1)}, u32[]{:S(2)}, u32[]{:S(2)}) %collective-permute-start.2) | collective-permute-done | bytes 524320 | tf_op jit(solution)/shard_map/ppermute | solution.py:226
  29.9 0.0 collective-permute-start.4
  29.9 1.8 %collective-permute-start.6 = (bf16[128,2048]{1,0:T(8,128)(2,1)S(1)}, bf16[128,2048]{1,0:T(8,128)(2,1)}, u32[]{:S(2)}, u32[]{:S(2)}) collective-permute-start(bf16[128,2048]{1,0:T(8,128)(2,1)S(1)} %collective-permute-done.2.refs_2_), channel_id=1, source_target_pairs={{8,0},{12,4},{0,8},{4,12},{24,16},{28,20},{16,24},{20,28},{9,1},{1... | collective-permute-start | bytes 1572872 | tf_op jit(solution)/shard_map/ppermute | solution.py:229
  31.6 0.2 collective-permute-done.4.refs_4_
  31.8 0.0 copy-done.3
  31.8 0.4 shard_map.47.refs_0_
  32.2 0.0 copy-start
  32.2 2.3 %copy-done = bf16[1280,2048]{1,0:T(8,128)(2,1)} copy-done((bf16[1280,2048]{1,0:T(8,128)(2,1)}, bf16[1280,2048]{1,0:T(8,128)(2,1)S(1)}, u32[]{:S(2)}) %copy-start) | copy-done | bytes 5242904
  34.5 8.3 %collective-permute-done.5.refs_1_ = bf16[256,2048]{1,0:T(8,128)(2,1)S(1)} collective-permute-done((bf16[256,2048]{1,0:T(8,128)(2,1)S(1)}, bf16[256,2048]{1,0:T(8,128)(2,1)S(1)}, u32[]{:S(2)}, u32[]{:S(2)}) %collective-permute-start.5) | collective-permute-done | bytes 1048608 | tf_op jit(solution)/shard_map/ppermute | solution.py:229
  42.8 0.0 collective-permute-start.7
  42.8 10.6 %collective-permute-done.6.refs_2_ = bf16[128,2048]{1,0:T(8,128)(2,1)} collective-permute-done((bf16[128,2048]{1,0:T(8,128)(2,1)S(1)}, bf16[128,2048]{1,0:T(8,128)(2,1)}, u32[]{:S(2)}, u32[]{:S(2)}) %collective-permute-start.6) | collective-permute-done | bytes 524320 | tf_op jit(solution)/shard_map/ppermute | solution.py:229
  53.4 0.0 collective-permute-start.8
  53.4 0.1 stack.85.place_ref
  53.5 2.2 %collective-permute-done.8.refs_4_ = bf16[128,2048]{1,0:T(8,128)(2,1)} collective-permute-done((bf16[128,2048]{1,0:T(8,128)(2,1)}, bf16[128,2048]{1,0:T(8,128)(2,1)}, u32[]{:S(2)}, u32[]{:S(2)}) %collective-permute-start.8) | collective-permute-done | bytes 524320 | tf_op jit(solution)/shard_map/ppermute | solution.py:229
  55.7 0.0 collective-permute-done.7.refs_3_
  55.7 2.5 %copy-done.1 = bf16[1280,2048]{1,0:T(8,128)(2,1)S(1)} copy-done((bf16[1280,2048]{1,0:T(8,128)(2,1)S(1)}, bf16[1280,2048]{1,0:T(8,128)(2,1)}, u32[]{:S(2)}) %copy-start.1) | copy-done | bytes 5242904
  58.1 7.2 %shard_map.48.refs_0_ = bf16[512,2048]{1,0:T(8,128)(2,1)S(1)} custom-call(s32[13]{0:T(128)S(1)} %stack.85.place_ref, bf16[512,2048]{1,0:T(8,128)(2,1)S(1)} %shard_map.46.rows_ref, bf16[1280,2048]{1,0:T(8,128)(2,1)S(1)} %copy-done.1, bf16[256,2048]{1,0:T(8,128)(2,1)S(1)} %collective-permute-done.5.refs_1_, bf16[128,2048]{1,0:T(8,128)(2,1)} %collective-permute-done.6.refs_2_, ...), custom_call_target="tpu_custom_call" | custom-call | flops 1 | bytes 1 | tf_op jit(solution)/shard_map/pallas_call | solution.py:96
  65.4 0.5 collective-permute-done.9.rows_ref
  65.9 0.0 copy-done.2
  65.9 7.9 %shard_map.49.refs_1_ = bf16[512,2048]{1,0:T(8,128)(2,1)S(1)} custom-call(s32[13]{0:T(128)S(1)} %stack.85.place_ref, bf16[512,2048]{1,0:T(8,128)(2,1)} %collective-permute-done.9.rows_ref, bf16[1280,2048]{1,0:T(8,128)(2,1)S(1)} %copy-done.2, bf16[256,2048]{1,0:T(8,128)(2,1)S(1)} %collective-permute-done.5.refs_1_, ...), custom_call_target="tpu_custom_call" | custom-call | flops 1 | bytes 1 | tf_op jit(solution)/shard_map/pallas_call | solution.py:96
  73.8 0.6 collective-permute-done.10
  74.5 3.9 %shard_map.53 = (f32[2,1024,128]{2,1,0:T(8,128)S(1)}, f32[2,1024,128]{2,1,0:T(8,128)}) custom-call(s32[1]{0:T(128)} %bitcast.4.side_ref, bf16[512,2048]{1,0:T(8,128)(2,1)S(1)} %shard_map.48.refs_0_, bf16[512,2048]{1,0:T(8,128)(2,1)S(1)} %shard_map.49.refs_1_, bf16[2,2,128,2048]{3,2,1,0:T(8,128)(2,1)} %bitcast.21.refs_2_, ...), custom_call_target="tpu_custom_call" | custom-call | flops 1 | bytes 1 | tf_op jit(solution)/shard_map/pallas_call | solution.py:138
  78.4 0.1 collective-permute-start.15
  78.5 3.9 %shard_map.50 = (f32[2,1024,128]{2,1,0:T(8,128)S(1)}, f32[2,1024,128]{2,1,0:T(8,128)}) custom-call(s32[1]{0:T(128)} %bitcast.4.side_ref, bf16[512,2048]{1,0:T(8,128)(2,1)S(1)} %shard_map.48.refs_0_, bf16[512,2048]{1,0:T(8,128)(2,1)S(1)} %shard_map.49.refs_1_, bf16[2,2,128,2048]{3,2,1,0:T(8,128)(2,1)} %bitcast.21.refs_2_, ...), custom_call_target="tpu_custom_call" | custom-call | flops 1 | bytes 1 | tf_op jit(solution)/shard_map/pallas_call | solution.py:138
  82.4 0.6 collective-permute-start.11
  82.9 0.1 pad_add_fusion.1.index_ref
  83.0 0.0 collective-permute-done.15.got_ref
  83.0 2.0 %shard_map.54 = (f32[2,512,128]{2,1,0:T(8,128)S(1)}, bf16[1,2,512,128]{3,2,1,0:T(8,128)(2,1)}) custom-call(s32[2]{0:T(128)S(1)} %pad_add_fusion.1.index_ref, f32[2,1024,128]{2,1,0:T(8,128)S(1)} %get-tuple-element.35.keep_ref, f32[2,1024,128]{2,1,0:T(8,128)} %collective-permute-done.15.got_ref), custom_call_target="tpu_custom_call" | custom-call | flops 1 | bytes 1 | tf_op jit(solution)/shard_map/pallas_call | solution.py:164
  85.1 0.8 copy-done.5
  85.9 1.7 %collective-permute-start.16 = (bf16[2,512,128]{2,1,0:T(8,128)(2,1)}, bf16[2,512,128]{2,1,0:T(8,128)(2,1)S(1)}, u32[]{:S(2)}, u32[]{:S(2)}) collective-permute-start(bf16[2,512,128]{2,1,0:T(8,128)(2,1)} %bitcast.25), channel_id=1, source_target_pairs={{0,8},{4,12},{8,0},{12,4},{16,24},{20,28},{24,16},{28,20},{1,9},{5... | collective-permute-start | bytes 786440 | tf_op jit(solution)/shard_map/ppermute | solution.py:236
  87.6 0.0 collective-permute-done.11.got_ref
  87.6 1.3 %shard_map.51 = (f32[2,512,128]{2,1,0:T(8,128)S(1)}, bf16[1,2,512,128]{3,2,1,0:T(8,128)(2,1)}) custom-call(s32[2]{0:T(128)S(1)} %pad_add_fusion.1.index_ref, f32[2,1024,128]{2,1,0:T(8,128)S(1)} %get-tuple-element.29.keep_ref, f32[2,1024,128]{2,1,0:T(8,128)S(1)} %collective-permute-done.11.got_ref), custom_call_target="tpu_custom_call" | custom-call | flops 1 | bytes 1 | tf_op jit(solution)/shard_map/pallas_call | solution.py:164
  89.0 0.3 collective-permute-start.12
  89.2 0.1 pad_add_fusion.index_ref
  89.3 5.9 %collective-permute-done.16.refs_0_ = bf16[2,512,128]{2,1,0:T(8,128)(2,1)S(1)} collective-permute-done((bf16[2,512,128]{2,1,0:T(8,128)(2,1)}, bf16[2,512,128]{2,1,0:T(8,128)(2,1)S(1)}, u32[]{:S(2)}, u32[]{:S(2)}) %collective-permute-start.16) | collective-permute-done | bytes 262176 | tf_op jit(solution)/shard_map/ppermute | solution.py:236
  95.2 0.0 copy-done.6
  95.2 0.6 shard_map.55
  95.8 2.8 %collective-permute-start.17 = (bf16[512,128]{1,0:T(8,128)(2,1)S(1)}, bf16[512,128]{1,0:T(8,128)(2,1)S(1)}, u32[]{:S(2)}, u32[]{:S(2)}) collective-permute-start(bf16[512,128]{1,0:T(8,128)(2,1)S(1)} %bitcast.29), channel_id=1, source_target_pairs={{0,16},{4,20},{8,24},{12,28},{16,0},{20,4},{24,8},{28,12},{1,17},{... | collective-permute-start | bytes 393224 | tf_op jit(solution)/shard_map/ppermute | solution.py:243
  98.7 4.1 %collective-permute-done.12.refs_0_ = bf16[2,512,128]{2,1,0:T(8,128)(2,1)S(1)} collective-permute-done((bf16[2,512,128]{2,1,0:T(8,128)(2,1)}, bf16[2,512,128]{2,1,0:T(8,128)(2,1)S(1)}, u32[]{:S(2)}, u32[]{:S(2)}) %collective-permute-start.12) | collective-permute-done | bytes 262176 | tf_op jit(solution)/shard_map/ppermute | solution.py:236
  102.8 0.6 shard_map.52
  103.4 0.9 collective-permute-start.13
  104.3 0.0 collective-permute-done.17
  104.3 5.2 %collective-permute-start.18 = (bf16[512,128]{1,0:T(8,128)(2,1)S(1)}, bf16[512,128]{1,0:T(8,128)(2,1)S(1)}, u32[]{:S(2)}, u32[]{:S(2)}) collective-permute-start(bf16[512,128]{1,0:T(8,128)(2,1)S(1)} %add_convert_fusion), channel_id=1, source_target_pairs={{0,0},{1,8},{2,2},{3,10},{4,4},{5,12},{6,6},{7,14},{8,1},{9,9},{10... | collective-permute-start | bytes 393224 | tf_op jit(solution)/shard_map/ppermute | solution.py:250
  109.5 2.0 %collective-permute-done.13 = bf16[512,128]{1,0:T(8,128)(2,1)S(1)} collective-permute-done((bf16[512,128]{1,0:T(8,128)(2,1)S(1)}, bf16[512,128]{1,0:T(8,128)(2,1)S(1)}, u32[]{:S(2)}, u32[]{:S(2)}) %collective-permute-start.13) | collective-permute-done | bytes 131104 | tf_op jit(solution)/shard_map/ppermute | solution.py:243
  111.5 1.9 %collective-permute-start.14 = (bf16[512,128]{1,0:T(8,128)(2,1)S(1)}, bf16[512,128]{1,0:T(8,128)(2,1)S(1)}, u32[]{:S(2)}, u32[]{:S(2)}) collective-permute-start(bf16[512,128]{1,0:T(8,128)(2,1)S(1)} %add_convert_fusion.1), channel_id=1, source_target_pairs={{0,0},{1,8},{2,2},{3,10},{4,4},{5,12},{6,6},{7,14},{8,1},{9,9},{10... | collective-permute-start | bytes 393224 | tf_op jit(solution)/shard_map/ppermute | solution.py:250
  113.4 1.1 collective-permute-done.18
  114.5 4.9 %collective-permute-done.14 = bf16[512,128]{1,0:T(8,128)(2,1)S(1)} collective-permute-done((bf16[512,128]{1,0:T(8,128)(2,1)S(1)}, bf16[512,128]{1,0:T(8,128)(2,1)S(1)}, u32[]{:S(2)}, u32[]{:S(2)}) %collective-permute-start.14) | collective-permute-done | bytes 131104 | tf_op jit(solution)/shard_map/ppermute | solution.py:250
  119.5 0.7 pad_maximum_fusion
  (9 shorter events, 0.2 us)
Async XLA Ops:
  1.1 13.7 %collective-permute-start = (bf16[128,2048]{1,0:T(8,128)(2,1)S(1)}, bf16[128,2048]{1,0:T(8,128)(2,1)S(1)}, u32[]{:S(2)}, u32[]{:S(2)}) collective-permute-start(bf16[128,2048]{1,0:T(8,128)(2,1)S(1)} %constant_dynamic-slice_fusion), channel_id=1, source_target_pairs={{1,0},{0,1},{3,2},{2,3},{5,4},{4,5},{7,6},{6,7},{9,8},{8,9},{11,10... | collective-permute-start | bytes 1572872 | tf_op jit(solution)/shard_map/ppermute | solution.py:222
  1.2 13.7 %collective-permute-start.1 = (bf16[128,2048]{1,0:T(8,128)(2,1)S(1)}, bf16[128,2048]{1,0:T(8,128)(2,1)S(1)}, u32[]{:S(2)}, u32[]{:S(2)}) collective-permute-start(bf16[128,2048]{1,0:T(8,128)(2,1)S(1)} %constant_dynamic-slice_fusion), channel_id=1, source_target_pairs={{2,0},{3,1},{0,2},{1,3},{6,4},{7,5},{4,6},{5,7},{10,8},{11,9},{8,1... | collective-permute-start | bytes 1572872 | tf_op jit(solution)/shard_map/ppermute | solution.py:226
  3.2 1.6 %copy-start.4 = (bf16[1,512,2048]{2,1,0:T(8,128)(2,1)S(1)}, bf16[1,512,2048]{2,1,0:T(8,128)(2,1)}, u32[]{:S(2)}) copy-start(bf16[1,512,2048]{2,1,0:T(8,128)(2,1)} %param.5) | copy-start | bytes 6291460
  4.8 0.7 copy-start.7
  6.7 25.1 %copy-start.3 = (bf16[512,2048]{1,0:T(8,128)(2,1)S(1)}, bf16[512,2048]{1,0:T(8,128)(2,1)}, u32[]{:S(2)}) copy-start(bf16[512,2048]{1,0:T(8,128)(2,1)} %refs_0_.1) | copy-start | bytes 6291460
  15.0 4.9 %collective-permute-start.3 = (bf16[256,2048]{1,0:T(8,128)(2,1)S(1)}, bf16[256,2048]{1,0:T(8,128)(2,1)S(1)}, u32[]{:S(2)}, u32[]{:S(2)}) collective-permute-start(bf16[256,2048]{1,0:T(8,128)(2,1)S(1)} %constant_dynamic-update-slice_fusion.refs_1_), channel_id=1, source_target_pairs={{4,0},{0,4},{12,8},{8,12},{20,16},{16,20},{28,24},{24,28},{5,1},{1... | collective-permute-start | bytes 3145736 | tf_op jit(solution)/shard_map/ppermute | solution.py:229
  15.1 14.8 %collective-permute-start.2 = (bf16[128,2048]{1,0:T(8,128)(2,1)S(1)}, bf16[128,2048]{1,0:T(8,128)(2,1)S(1)}, u32[]{:S(2)}, u32[]{:S(2)}) collective-permute-start(bf16[128,2048]{1,0:T(8,128)(2,1)S(1)} %collective-permute-done), channel_id=1, source_target_pairs={{2,0},{3,1},{0,2},{1,3},{6,4},{7,5},{4,6},{5,7},{10,8},{11,9},{8,1... | collective-permute-start | bytes 1572872 | tf_op jit(solution)/shard_map/ppermute | solution.py:226
  16.8 26.0 %collective-permute-start.5 = (bf16[256,2048]{1,0:T(8,128)(2,1)S(1)}, bf16[256,2048]{1,0:T(8,128)(2,1)S(1)}, u32[]{:S(2)}, u32[]{:S(2)}) collective-permute-start(bf16[256,2048]{1,0:T(8,128)(2,1)S(1)} %constant_dynamic-update-slice_fusion.refs_1_), channel_id=1, source_target_pairs={{8,0},{12,4},{0,8},{4,12},{24,16},{28,20},{16,24},{20,28},{9,1},{1... | collective-permute-start | bytes 3145736 | tf_op jit(solution)/shard_map/ppermute | solution.py:229
  18.4 47.5 %collective-permute-start.9 = (bf16[512,2048]{1,0:T(8,128)(2,1)S(1)}, bf16[512,2048]{1,0:T(8,128)(2,1)}, u32[]{:S(2)}, u32[]{:S(2)}) collective-permute-start(bf16[512,2048]{1,0:T(8,128)(2,1)S(1)} %shard_map.46.rows_ref), channel_id=1, source_target_pairs={{1,0},{0,1},{3,2},{2,3},{5,4},{4,5},{7,6},{6,7},{9,8},{8,9},{11,10... | collective-permute-start | bytes 6291464 | tf_op jit(solution)/shard_map/ppermute | solution.py:222
  19.9 54.6 %collective-permute-start.10 = (bf16[512,2048]{1,0:T(8,128)(2,1)}, bf16[512,2048]{1,0:T(8,128)(2,1)}, u32[]{:S(2)}, u32[]{:S(2)}) collective-permute-start(bf16[512,2048]{1,0:T(8,128)(2,1)} %bitcast.20), channel_id=1, source_target_pairs={{2,0},{3,1},{0,2},{1,3},{6,4},{7,5},{4,6},{5,7},{10,8},{11,9},{8,1... | collective-permute-start | bytes 6291464 | tf_op jit(solution)/shard_map/ppermute | solution.py:226
  29.9 1.9 %collective-permute-start.4 = (bf16[128,2048]{1,0:T(8,128)(2,1)S(1)}, bf16[128,2048]{1,0:T(8,128)(2,1)S(1)}, u32[]{:S(2)}, u32[]{:S(2)}) collective-permute-start(bf16[128,2048]{1,0:T(8,128)(2,1)S(1)} %collective-permute-done.2.refs_2_), channel_id=1, source_target_pairs={{4,0},{0,4},{12,8},{8,12},{20,16},{16,20},{28,24},{24,28},{5,1},{1... | collective-permute-start | bytes 1572872 | tf_op jit(solution)/shard_map/ppermute | solution.py:229
  29.9 23.5 %collective-permute-start.6 = (bf16[128,2048]{1,0:T(8,128)(2,1)S(1)}, bf16[128,2048]{1,0:T(8,128)(2,1)}, u32[]{:S(2)}, u32[]{:S(2)}) collective-permute-start(bf16[128,2048]{1,0:T(8,128)(2,1)S(1)} %collective-permute-done.2.refs_2_), channel_id=1, source_target_pairs={{8,0},{12,4},{0,8},{4,12},{24,16},{28,20},{16,24},{20,28},{9,1},{1... | collective-permute-start | bytes 1572872 | tf_op jit(solution)/shard_map/ppermute | solution.py:229
  32.2 2.3 %copy-start = (bf16[1280,2048]{1,0:T(8,128)(2,1)}, bf16[1280,2048]{1,0:T(8,128)(2,1)S(1)}, u32[]{:S(2)}) copy-start(bf16[1280,2048]{1,0:T(8,128)(2,1)S(1)} %shard_map.47.refs_0_) | copy-start | bytes 15728644
  42.8 12.8 %collective-permute-start.7 = (bf16[256,2048]{1,0:T(8,128)(2,1)S(1)}, bf16[256,2048]{1,0:T(8,128)(2,1)}, u32[]{:S(2)}, u32[]{:S(2)}) collective-permute-start(bf16[256,2048]{1,0:T(8,128)(2,1)S(1)} %collective-permute-done.5.refs_1_), channel_id=1, source_target_pairs={{4,0},{0,4},{12,8},{8,12},{20,16},{16,20},{28,24},{24,28},{5,1},{1... | collective-permute-start | bytes 3145736 | tf_op jit(solution)/shard_map/ppermute | solution.py:229
  53.4 2.3 %collective-permute-start.8 = (bf16[128,2048]{1,0:T(8,128)(2,1)}, bf16[128,2048]{1,0:T(8,128)(2,1)}, u32[]{:S(2)}, u32[]{:S(2)}) collective-permute-start(bf16[128,2048]{1,0:T(8,128)(2,1)} %collective-permute-done.6.refs_2_), channel_id=1, source_target_pairs={{4,0},{0,4},{12,8},{8,12},{20,16},{16,20},{28,24},{24,28},{5,1},{1... | collective-permute-start | bytes 1572872 | tf_op jit(solution)/shard_map/ppermute | solution.py:229
  55.7 2.5 %copy-start.1 = (bf16[1280,2048]{1,0:T(8,128)(2,1)S(1)}, bf16[1280,2048]{1,0:T(8,128)(2,1)}, u32[]{:S(2)}) copy-start(bf16[1280,2048]{1,0:T(8,128)(2,1)} %copy-done) | copy-start | bytes 15728644
  58.1 7.8 %copy-start.2 = (bf16[1280,2048]{1,0:T(8,128)(2,1)S(1)}, bf16[1280,2048]{1,0:T(8,128)(2,1)}, u32[]{:S(2)}) copy-start(bf16[1280,2048]{1,0:T(8,128)(2,1)} %copy-done) | copy-start | bytes 15728644
  78.4 4.6 %collective-permute-start.15 = (f32[2,1024,128]{2,1,0:T(8,128)}, f32[2,1024,128]{2,1,0:T(8,128)}, u32[]{:S(2)}, u32[]{:S(2)}) collective-permute-start(f32[2,1024,128]{2,1,0:T(8,128)} %get-tuple-element.36), channel_id=1, source_target_pairs={{4,0},{0,4},{12,8},{8,12},{20,16},{16,20},{28,24},{24,28},{5,1},{1... | collective-permute-start | bytes 3145736 | tf_op jit(solution)/shard_map/ppermute | solution.py:229
  82.4 5.2 %collective-permute-start.11 = (f32[2,1024,128]{2,1,0:T(8,128)}, f32[2,1024,128]{2,1,0:T(8,128)S(1)}, u32[]{:S(2)}, u32[]{:S(2)}) collective-permute-start(f32[2,1024,128]{2,1,0:T(8,128)} %get-tuple-element.30), channel_id=1, source_target_pairs={{4,0},{0,4},{12,8},{8,12},{20,16},{16,20},{28,24},{24,28},{5,1},{1... | collective-permute-start | bytes 3145736 | tf_op jit(solution)/shard_map/ppermute | solution.py:229
  85.1 0.8 copy-start.5
  85.9 9.4 %copy-start.6 = (f32[2,512,128]{2,1,0:T(8,128)S(1)}, f32[2,512,128]{2,1,0:T(8,128)}, u32[]{:S(2)}) copy-start(f32[2,512,128]{2,1,0:T(8,128)} %copy-done.5) | copy-start | bytes 1572868
  85.9 9.4 %collective-permute-start.16 = (bf16[2,512,128]{2,1,0:T(8,128)(2,1)}, bf16[2,512,128]{2,1,0:T(8,128)(2,1)S(1)}, u32[]{:S(2)}, u32[]{:S(2)}) collective-permute-start(bf16[2,512,128]{2,1,0:T(8,128)(2,1)} %bitcast.25), channel_id=1, source_target_pairs={{0,8},{4,12},{8,0},{12,4},{16,24},{20,28},{24,16},{28,20},{1,9},{5... | collective-permute-start | bytes 786440 | tf_op jit(solution)/shard_map/ppermute | solution.py:236
  89.0 13.8 %collective-permute-start.12 = (bf16[2,512,128]{2,1,0:T(8,128)(2,1)}, bf16[2,512,128]{2,1,0:T(8,128)(2,1)S(1)}, u32[]{:S(2)}, u32[]{:S(2)}) collective-permute-start(bf16[2,512,128]{2,1,0:T(8,128)(2,1)} %bitcast.23), channel_id=1, source_target_pairs={{0,8},{4,12},{8,0},{12,4},{16,24},{20,28},{24,16},{28,20},{1,9},{5... | collective-permute-start | bytes 786440 | tf_op jit(solution)/shard_map/ppermute | solution.py:236
  95.8 8.4 %collective-permute-start.17 = (bf16[512,128]{1,0:T(8,128)(2,1)S(1)}, bf16[512,128]{1,0:T(8,128)(2,1)S(1)}, u32[]{:S(2)}, u32[]{:S(2)}) collective-permute-start(bf16[512,128]{1,0:T(8,128)(2,1)S(1)} %bitcast.29), channel_id=1, source_target_pairs={{0,16},{4,20},{8,24},{12,28},{16,0},{20,4},{24,8},{28,12},{1,17},{... | collective-permute-start | bytes 393224 | tf_op jit(solution)/shard_map/ppermute | solution.py:243
  103.4 8.1 %collective-permute-start.13 = (bf16[512,128]{1,0:T(8,128)(2,1)S(1)}, bf16[512,128]{1,0:T(8,128)(2,1)S(1)}, u32[]{:S(2)}, u32[]{:S(2)}) collective-permute-start(bf16[512,128]{1,0:T(8,128)(2,1)S(1)} %bitcast.30), channel_id=1, source_target_pairs={{0,16},{4,20},{8,24},{12,28},{16,0},{20,4},{24,8},{28,12},{1,17},{... | collective-permute-start | bytes 393224 | tf_op jit(solution)/shard_map/ppermute | solution.py:243
  104.3 10.2 %collective-permute-start.18 = (bf16[512,128]{1,0:T(8,128)(2,1)S(1)}, bf16[512,128]{1,0:T(8,128)(2,1)S(1)}, u32[]{:S(2)}, u32[]{:S(2)}) collective-permute-start(bf16[512,128]{1,0:T(8,128)(2,1)S(1)} %add_convert_fusion), channel_id=1, source_target_pairs={{0,0},{1,8},{2,2},{3,10},{4,4},{5,12},{6,6},{7,14},{8,1},{9,9},{10... | collective-permute-start | bytes 393224 | tf_op jit(solution)/shard_map/ppermute | solution.py:250
  111.5 8.0 %collective-permute-start.14 = (bf16[512,128]{1,0:T(8,128)(2,1)S(1)}, bf16[512,128]{1,0:T(8,128)(2,1)S(1)}, u32[]{:S(2)}, u32[]{:S(2)}) collective-permute-start(bf16[512,128]{1,0:T(8,128)(2,1)S(1)} %add_convert_fusion.1), channel_id=1, source_target_pairs={{0,0},{1,8},{2,2},{3,10},{4,4},{5,12},{6,6},{7,14},{8,1},{9,9},{10... | collective-permute-start | bytes 393224 | tf_op jit(solution)/shard_map/ppermute | solution.py:250

commit v3 on v2

--- a/solution.py
+++ b/solution.py
@@ -15,6 +15,14 @@
 WHOLE = pl.BlockSpec(memory_space=pltpu.VMEM)
 SCALARS = pl.BlockSpec(memory_space=pltpu.SMEM)
 ANYWHERE = pl.BlockSpec(memory_space=pl.ANY)
+
+
+def vmem(shape, kind):
+    return pltpu.VMEM(shape, kind)
+
+
+def held(values):
+    return [pltpu.with_memory_space_constraint(v, pltpu.VMEM) for v in values]
 
 
 def params():
@@ -63,87 +71,74 @@
         stack_kernel,
         in_specs=[ANYWHERE] * len(parts),
         out_specs=ANYWHERE,
-        out_shape=jax.ShapeDtypeStruct((depth, width), parts[0].dtype),
+        out_shape=vmem((depth, width), parts[0].dtype),
         scratch_shapes=[pltpu.SemaphoreType.DMA((len(parts),))],
         compiler_params=params(),
         cost_estimate=COST,
     )(*parts)
 
 
-def inner_kernel(sizes, place_ref, rows_ref, *refs):
-    part_refs, (out_ref, ordered) = refs[:-2], refs[-2:]
-
-    @pl.when(pl.program_id(0) == 0)
-    def _():
-        at = 0
-        for p, size in enumerate(sizes):
-            cols = pl.ds(pl.multiple_of(place_ref[p], size), size)
-            ordered[:, at : at + size] = rows_ref[:, cols]
-            at += size
-
-    psi = jnp.concatenate([ref[...] for ref in part_refs], 0)
-    unit = math.gcd(rows_ref.shape[0], 256)
-    for i in range(rows_ref.shape[0] // unit):
-        rows = pl.ds(i * unit, unit)
-        value = jnp.dot(ordered[rows, :], psi, preferred_element_type=jnp.float32)
-        out_ref[rows, :] = value.astype(out_ref.dtype)
+def inner_kernel(sizes, n_parts, place_ref, rows_ref, *refs):
+    part_refs, (out_ref, ordered) = refs[:n_parts], refs[n_parts:]
+    at = 0
+    for p, size in enumerate(sizes):
+        cols = pl.ds(pl.multiple_of(place_ref[p], size), size)
+        ordered[:, at : at + size] = rows_ref[:, cols]
+        at += size
+    step = math.gcd(out_ref.shape[1], 512)
+    for j in range(out_ref.shape[1] // step):
+        cols = pl.ds(j * step, step)
+        psi = jnp.concatenate([ref[:, cols] for ref in part_refs], 0)
+        value = jnp.dot(ordered[...], psi, preferred_element_type=jnp.float32)
+        out_ref[:, cols] = value.astype(out_ref.dtype)
 
 
 def inner_of(rows, parts, sizes, places):
     height, depth = rows.shape
     width = parts[0].shape[1]
-    step = math.gcd(width, 512)
-    return pl.pallas_call(
-        functools.partial(inner_kernel, sizes),
-        grid=(width // step,),
-        in_specs=[SCALARS, pl.BlockSpec((height, depth), lambda j: (0, 0))]
-        + [pl.BlockSpec((a.shape[0], step), lambda j: (0, j)) for a in parts],
-        out_specs=pl.BlockSpec((height, step), lambda j: (0, j)),
-        out_shape=jax.ShapeDtypeStruct((height, width), parts[0].dtype),
+    return pl.pallas_call(
+        functools.partial(inner_kernel, sizes, len(parts)),
+        in_specs=[SCALARS] + [WHOLE] * (1 + len(parts)),
+        out_specs=WHOLE,
+        out_shape=vmem((height, width), parts[0].dtype),
         scratch_shapes=[pltpu.VMEM((height, depth), rows.dtype)],
         compiler_params=params(),
         cost_estimate=COST,
-    )(places, rows, *parts)
-
-
-def outer_kernel(n_inner, n_right, side_ref, *refs):
-    inner_refs = refs[:n_inner]
-    right_refs = refs[n_inner : n_inner + n_right]
-    keep_ref, give_ref = refs[n_inner + n_right :]
-    side = side_ref[0]
-    wide = keep_ref.shape[2]
-    for half, out_ref in ((1 - side, give_ref), (side, keep_ref)):
-        right = jnp.concatenate([ref[half] for ref in right_refs], 0)
-        at = 0
-        for ref in inner_refs:
-            unit = math.gcd(ref.shape[0], 256)
-            for i in range(ref.shape[0] // unit):
-                value = lax.dot_general(
-                    ref[i * unit : (i + 1) * unit, :],
-                    right,
-                    (((1,), (1,)), ((), ())),
-                    preferred_element_type=jnp.float32,
-                )
-                for j in range(n_right):
-                    out_ref[j, at : at + unit, :] = value[:, j * wide : (j + 1) * wide]
-                at += unit
-
-
-def outer_of(inners, piece, rights, side):
+    )(places, *held([rows, *parts]))
+
+
+def outer_kernel(n_inner, pieces, half_ref, *refs):
+    inner_refs, right_refs, out_refs = refs[:n_inner], refs[n_inner:-pieces], refs[-pieces:]
+    blocks, _, wide = out_refs[0].shape
+    right = jnp.concatenate([ref[p] for p in range(pieces) for ref in right_refs], 0)
+    at = 0
+    for ref in inner_refs:
+        value = lax.dot_general(
+            ref[...], right, (((1,), (1,)), ((), ())), preferred_element_type=jnp.float32
+        )
+        for p, out_ref in enumerate(out_refs):
+            for j in range(blocks):
+                col = (p * blocks + j) * wide
+                out_ref[j, at : at + ref.shape[0], :] = value[:, col : col + wide].astype(out_ref.dtype)
+        at += ref.shape[0]
+
+
+def outer_of(inners, rights, half, kind, cost):
     height = sum(a.shape[0] for a in inners)
-    halves, pieces, wide, depth = rights[0].shape
-    n_right = len(rights)
-    shape = jax.ShapeDtypeStruct((n_right, height, wide), jnp.float32)
-    spec = pl.BlockSpec((halves, None, wide, depth), lambda i: (0, piece, 0, 0))
-    return pl.pallas_call(
-        functools.partial(outer_kernel, len(inners), n_right),
-        grid=(1,),
-        in_specs=[SCALARS] + [WHOLE] * len(inners) + [spec] * n_right,
-        out_specs=[WHOLE, WHOLE],
-        out_shape=[shape, shape],
-        compiler_params=params(),
-        cost_estimate=COST,
-    )(side.astype(jnp.int32).reshape(1), *inners, *rights)
+    _, pieces, wide, depth = rights[0].shape
+    spec = pl.BlockSpec((None, pieces, wide, depth), lambda i, half: (half[0], 0, 0, 0))
+    return pl.pallas_call(
+        functools.partial(outer_kernel, len(inners), pieces),
+        grid_spec=pltpu.PrefetchScalarGridSpec(
+            num_scalar_prefetch=1,
+            grid=(1,),
+            in_specs=[WHOLE] * len(inners) + [spec] * len(rights),
+            out_specs=[WHOLE] * pieces,
+        ),
+        out_shape=[vmem((len(rights), height, wide), kind)] * pieces,
+        compiler_params=params(),
+        cost_estimate=cost,
+    )(half.astype(jnp.int32).reshape(1), *held(inners), *rights)
 
 
 def cores_kernel(index_ref, keep_ref, got_ref, kept_ref, sent_ref):
@@ -166,12 +161,34 @@
         in_specs=[SCALARS, WHOLE, WHOLE],
         out_specs=[WHOLE, WHOLE],
         out_shape=[
-            jax.ShapeDtypeStruct((blocks, height, wide), jnp.float32),
-            jax.ShapeDtypeStruct((others, blocks, height, wide), jnp.bfloat16),
+            vmem((blocks, height, wide), jnp.float32),
+            vmem((others, blocks, height, wide), jnp.bfloat16),
         ],
         compiler_params=params(),
         cost_estimate=COST,
-    )(index, keep, got)
+    )(index, *held([keep, got]))
+
+
+def chosen_kernel(index_ref, *refs):
+    n = index_ref.shape[0]
+    for k, out_ref in enumerate(refs[n:]):
+        for j in range(out_ref.shape[0]):
+            value = refs[0][j].astype(jnp.float32)
+            for i in range(1, n):
+                value = jnp.where(index_ref[k] == i, refs[i][j].astype(jnp.float32), value)
+            out_ref[j] = value.astype(out_ref.dtype)
+
+
+def chosen_of(values, index):
+    kinds = [jnp.float32] + [jnp.bfloat16] * (len(values) - 1)
+    return pl.pallas_call(
+        chosen_kernel,
+        in_specs=[SCALARS] + [WHOLE] * len(values),
+        out_specs=[WHOLE] * len(values),
+        out_shape=[vmem(values[0].shape, kind) for kind in kinds],
+        compiler_params=params(),
+        cost_estimate=COST,
+    )(index, *held(values))
 
 
 def planes_kernel(n_got, index_ref, kept_ref, *refs):
@@ -195,12 +212,12 @@
         in_specs=[SCALARS] + [WHOLE] * (1 + len(got)),
         out_specs=[WHOLE, WHOLE],
         out_shape=[
-            jax.ShapeDtypeStruct((height, wide), jnp.float32),
-            jax.ShapeDtypeStruct((blocks - 1, height, wide), jnp.bfloat16),
+            vmem((height, wide), jnp.float32),
+            vmem((blocks - 1, height, wide), jnp.bfloat16),
         ],
         compiler_params=params(),
         cost_estimate=COST,
-    )(index, kept, *got)
+    )(index, *held([kept, *got]))
 
 
 def after(value, *earlier):
@@ -294,15 +311,24 @@
     def members(own, base):
         return jnp.stack([(own + j - base) % s for j in range(s)]).astype(jnp.int32)
 
+    give = outer_of(inners, rights, 1 - core, jnp.bfloat16, COST)
+    got = [from_term(v, 1) for v in give]
+    flops = 2 * len(inners) * height * len(rights) * (height // 2) * width
+    cost = pl.CostEstimate(flops=flops, bytes_accessed=1, transcendentals=0)
+    keep = outer_of(inners, rights, after(core, give), jnp.float32, cost)
     outs = []
     for p in range(PIECES):
-        keep, give = outer_of(inners, p, rights, core)
-        kept, sent = cores_summed(keep, from_term(give, 1), members(zl, lo), height)
-        got = [to_zl(sent[j - 1], j) for j in range(1, s)]
-        final, sent = planes_summed(kept, got, members(zh, hi))
+        home_first = p % 2 == 0
+        index = jnp.arange(s, dtype=jnp.int32) if home_first else members(zl, lo)
+        kept, sent = cores_summed(keep[p], got[p], index, height)
+        if home_first:
+            held_blocks = [kept] + [from_lo(sent[s - j - 1], j) for j in range(1, s)]
+            kept, *sent = chosen_of(held_blocks, members(zl, lo))
+        final, sent = planes_summed(kept, [to_zl(sent[j - 1], j) for j in range(1, s)], members(zh, hi))
         for j in range(1, s):
             final = final + to_zh(sent[j - 1], j).astype(jnp.float32)
-        outs.append(crossed(final.astype(jnp.bfloat16)))
+        final = final.astype(jnp.bfloat16)
+        outs.append(final if home_first else crossed(final))
     return jnp.concatenate(outs, 1)
 
 

time: 121 us -> 116 us (0.959)
  waiting for transfers between devices: 58.1 us -> 54.5 us
  Pallas kernels: 29.1 us -> 25.6 us
  starting transfers between devices: 22.8 us -> 24.9 us
    ppermute x2 -> x3, waiting for transfers between devices: 8.63 us -> 13.9 us  [from_lo(): return lax.ppermute(value, 'row', pairs)]
    ppermute x2, waiting for transfers between devices: 10.1 us -> 5.19 us  [to_zl(): return lax.ppermute(value, 'term', pairs)]
    ppermute x2 -> x1, waiting for transfers between devices: 6.04 us -> 2.84 us  [crossed(): return lax.ppermute(value, ('term', 'row'), pairs)]
    pallas_call x2, Pallas kernels: 3.37 us -> 1.27 us  [cores_summed(): pl.pallas_call(cores_kernel, in_specs=[SCALARS, WHOLE, WHOLE], out_specs=...]
    ppermute x2, waiting for transfers between devices: 1.96 us -> 0.05 us  [to_zh(): return lax.ppermute(value, 'term', pairs)]
    ppermute x2 -> x1, starting transfers between devices: 7.1 us -> 5.24 us  [crossed(): return lax.ppermute(value, ('term', 'row'), pairs)]
    ppermute x2 -> x3, starting transfers between devices: 1.56 us -> 3.3 us  [from_lo(): return lax.ppermute(value, 'row', pairs)]
    ppermute x2, starting transfers between devices: 2.03 us -> 3.46 us  [to_zl(): return lax.ppermute(value, 'term', pairs)]
  transfers between devices with their start and end apart: 19 -> 19, of which waited for: 14 -> 13; matrix products, arithmetic and copies ran while one was open for 0% -> 0% of each run, Pallas kernels for 21% -> 19%
where the time goes in v3:
time: 116 us; the launch traced here: 115 us
  waiting for transfers between devices  54.5 us (47%)
  Pallas kernels  25.6 us (22%)
  starting transfers between devices  24.9 us (21%)
  local copies, waits for them, and re-layouts  8.33 us (7%)
    ppermute x8, waiting for transfers between devices, from_term(): return lax.ppermute(value, 'term', [(a ^ bit, a) for a in range(terms)])  21.2 us
    ppermute x3, waiting for transfers between devices, from_lo(): return lax.ppermute(value, 'row', pairs)  13.9 us
    pallas_call x2, Pallas kernels, inner_of(): pl.pallas_call(functools.partial(inner_kernel, sizes, len(parts)), in_spe...  13 us
    ppermute x3, waiting for transfers between devices, from_hi(): return lax.ppermute(value, 'row', pairs)  11.3 us
    pallas_call x2, Pallas kernels, outer_of(): pl.pallas_call(functools.partial(outer_kernel, len(inners), pieces), grid...  7.94 us
    unnamed x13, local copies, waits for them, and re-layouts  7.12 us
    ppermute x1, starting transfers between devices, crossed(): return lax.ppermute(value, ('term', 'row'), pairs)  5.24 us
    ppermute x2, waiting for transfers between devices, to_zl(): return lax.ppermute(value, 'term', pairs)  5.19 us
  transfers between devices with their start and end apart: 19, of which 13 were waited for; matrix products, arithmetic and copies ran while one was open for 0% of the time, Pallas kernels for 19%

profile of v3, /device:TPU:2, one launch (start us, length us, event | category | flops | bytes accessed | tf_op | source)
XLA Modules:
  0.0 114.5 jit_solution(2717257545462005962)
XLA Ops:
  0.0 1.1 constant_dynamic-slice_fusion
  1.1 0.1 collective-permute-start
  1.2 2.0 %collective-permute-start.1 = (bf16[128,2048]{1,0:T(8,128)(2,1)S(1)}, bf16[128,2048]{1,0:T(8,128)(2,1)S(1)}, u32[]{:S(2)}, u32[]{:S(2)}) collective-permute-start(bf16[128,2048]{1,0:T(8,128)(2,1)S(1)} %constant_dynamic-slice_fusion), channel_id=1, source_target_pairs={{2,0},{3,1},{0,2},{1,3},{6,4},{7,5},{4,6},{5,7},{10,8},{11,9},{8,1... | collective-permute-start | bytes 1572872 | tf_op jit(solution)/shard_map/ppermute | solution.py:243
  3.2 1.6 %copy-done.4 = bf16[1,512,2048]{2,1,0:T(8,128)(2,1)S(1)} copy-done((bf16[1,512,2048]{2,1,0:T(8,128)(2,1)S(1)}, bf16[1,512,2048]{2,1,0:T(8,128)(2,1)}, u32[]{:S(2)}) %copy-start.4) | copy-done | bytes 2097176
  4.8 0.0 copy-start.5
  4.8 0.7 copy-done.5
  5.5 1.2 %shard_map.46.rows_ref = bf16[512,2048]{1,0:T(8,128)(2,1)S(1)} custom-call(s32[4,16]{1,0:T(4,128)S(1)} %bitcast.29, bf16[512,2048]{1,0:T(8,128)(2,1)S(1)} %bitcast.28), custom_call_target="tpu_custom_call" | custom-call | flops 1 | bytes 1 | tf_op jit(solution)/shard_map/pallas_call | solution.py:44
  6.7 0.0 copy-start.3
  6.7 8.1 %collective-permute-done = bf16[128,2048]{1,0:T(8,128)(2,1)S(1)} collective-permute-done((bf16[128,2048]{1,0:T(8,128)(2,1)S(1)}, bf16[128,2048]{1,0:T(8,128)(2,1)S(1)}, u32[]{:S(2)}, u32[]{:S(2)}) %collective-permute-start) | collective-permute-done | bytes 524320 | tf_op jit(solution)/shard_map/ppermute | solution.py:239
  14.8 0.1 collective-permute-done.1
  15.0 0.1 collective-permute-start.3
  15.1 1.8 %collective-permute-start.2 = (bf16[128,2048]{1,0:T(8,128)(2,1)S(1)}, bf16[128,2048]{1,0:T(8,128)(2,1)S(1)}, u32[]{:S(2)}, u32[]{:S(2)}) collective-permute-start(bf16[128,2048]{1,0:T(8,128)(2,1)S(1)} %collective-permute-done), channel_id=1, source_target_pairs={{2,0},{3,1},{0,2},{1,3},{6,4},{7,5},{4,6},{5,7},{10,8},{11,9},{8,1... | collective-permute-start | bytes 1572872 | tf_op jit(solution)/shard_map/ppermute | solution.py:243
  16.8 1.6 %collective-permute-start.5 = (bf16[256,2048]{1,0:T(8,128)(2,1)S(1)}, bf16[256,2048]{1,0:T(8,128)(2,1)S(1)}, u32[]{:S(2)}, u32[]{:S(2)}) collective-permute-start(bf16[256,2048]{1,0:T(8,128)(2,1)S(1)} %constant_dynamic-update-slice_fusion.refs_1_), channel_id=1, source_target_pairs={{8,0},{12,4},{0,8},{4,12},{24,16},{28,20},{16,24},{20,28},{9,1},{1... | collective-permute-start | bytes 3145736 | tf_op jit(solution)/shard_map/ppermute | solution.py:246
  18.4 1.5 %collective-permute-start.9 = (bf16[512,2048]{1,0:T(8,128)(2,1)S(1)}, bf16[512,2048]{1,0:T(8,128)(2,1)}, u32[]{:S(2)}, u32[]{:S(2)}) collective-permute-start(bf16[512,2048]{1,0:T(8,128)(2,1)S(1)} %shard_map.46.rows_ref), channel_id=1, source_target_pairs={{1,0},{0,1},{3,2},{2,3},{5,4},{4,5},{7,6},{6,7},{9,8},{8,9},{11,10... | collective-permute-start | bytes 6291464 | tf_op jit(solution)/shard_map/ppermute | solution.py:239
  19.9 0.0 collective-permute-done.3.refs_3_
  19.9 0.5 collective-permute-start.10
  20.4 9.4 %collective-permute-done.2.refs_2_ = bf16[128,2048]{1,0:T(8,128)(2,1)S(1)} collective-permute-done((bf16[128,2048]{1,0:T(8,128)(2,1)S(1)}, bf16[128,2048]{1,0:T(8,128)(2,1)S(1)}, u32[]{:S(2)}, u32[]{:S(2)}) %collective-permute-start.2) | collective-permute-done | bytes 524320 | tf_op jit(solution)/shard_map/ppermute | solution.py:243
  29.9 0.0 collective-permute-start.4
  29.9 1.8 %collective-permute-start.6 = (bf16[128,2048]{1,0:T(8,128)(2,1)S(1)}, bf16[128,2048]{1,0:T(8,128)(2,1)}, u32[]{:S(2)}, u32[]{:S(2)}) collective-permute-start(bf16[128,2048]{1,0:T(8,128)(2,1)S(1)} %collective-permute-done.2.refs_2_), channel_id=1, source_target_pairs={{8,0},{12,4},{0,8},{4,12},{24,16},{28,20},{16,24},{20,28},{9,1},{1... | collective-permute-start | bytes 1572872 | tf_op jit(solution)/shard_map/ppermute | solution.py:246
  31.6 0.2 collective-permute-done.4.refs_4_
  31.8 0.0 copy-done.3
  31.8 0.4 shard_map.47.refs_0_
  32.2 0.0 copy-start
  32.2 2.3 %copy-done = bf16[1280,2048]{1,0:T(8,128)(2,1)} copy-done((bf16[1280,2048]{1,0:T(8,128)(2,1)}, bf16[1280,2048]{1,0:T(8,128)(2,1)S(1)}, u32[]{:S(2)}) %copy-start) | copy-done | bytes 5242904
  34.5 8.3 %collective-permute-done.5.refs_1_ = bf16[256,2048]{1,0:T(8,128)(2,1)S(1)} collective-permute-done((bf16[256,2048]{1,0:T(8,128)(2,1)S(1)}, bf16[256,2048]{1,0:T(8,128)(2,1)S(1)}, u32[]{:S(2)}, u32[]{:S(2)}) %collective-permute-start.5) | collective-permute-done | bytes 1048608 | tf_op jit(solution)/shard_map/ppermute | solution.py:246
  42.8 0.0 collective-permute-start.7
  42.8 10.6 %collective-permute-done.6.refs_2_ = bf16[128,2048]{1,0:T(8,128)(2,1)} collective-permute-done((bf16[128,2048]{1,0:T(8,128)(2,1)S(1)}, bf16[128,2048]{1,0:T(8,128)(2,1)}, u32[]{:S(2)}, u32[]{:S(2)}) %collective-permute-start.6) | collective-permute-done | bytes 524320 | tf_op jit(solution)/shard_map/ppermute | solution.py:246
  53.4 0.0 collective-permute-start.8
  53.4 0.1 stack.85.place_ref
  53.5 2.2 %collective-permute-done.8.refs_4_ = bf16[128,2048]{1,0:T(8,128)(2,1)} collective-permute-done((bf16[128,2048]{1,0:T(8,128)(2,1)}, bf16[128,2048]{1,0:T(8,128)(2,1)}, u32[]{:S(2)}, u32[]{:S(2)}) %collective-permute-start.8) | collective-permute-done | bytes 524320 | tf_op jit(solution)/shard_map/ppermute | solution.py:246
  55.7 0.0 collective-permute-done.7.refs_3_
  55.7 2.5 %copy-done.1 = bf16[1280,2048]{1,0:T(8,128)(2,1)S(1)} copy-done((bf16[1280,2048]{1,0:T(8,128)(2,1)S(1)}, bf16[1280,2048]{1,0:T(8,128)(2,1)}, u32[]{:S(2)}) %copy-start.1) | copy-done | bytes 5242904
  58.1 0.0 copy-start.2
  58.1 6.2 %shard_map.48.refs_0_ = bf16[512,2048]{1,0:T(8,128)(2,1)S(1)} custom-call(s32[13]{0:T(128)S(1)} %stack.85.place_ref, bf16[512,2048]{1,0:T(8,128)(2,1)S(1)} %shard_map.46.rows_ref, bf16[1280,2048]{1,0:T(8,128)(2,1)S(1)} %copy-done.1, bf16[256,2048]{1,0:T(8,128)(2,1)S(1)} %collective-permute-done.5.refs_1_, bf16[128,2048]{1,0:T(8,128)(2,1)} %collective-permute-done.6.refs_2_, ...), custom_call_target="tpu_custom_call" | custom-call | flops 1 | bytes 1 | tf_op jit(solution)/shard_map/pallas_call | solution.py:99
  64.4 1.6 %collective-permute-done.9.rows_ref = bf16[512,2048]{1,0:T(8,128)(2,1)} collective-permute-done((bf16[512,2048]{1,0:T(8,128)(2,1)S(1)}, bf16[512,2048]{1,0:T(8,128)(2,1)}, u32[]{:S(2)}, u32[]{:S(2)}) %collective-permute-start.9) | collective-permute-done | bytes 2097184 | tf_op jit(solution)/shard_map/ppermute | solution.py:239
  65.9 0.0 copy-done.2
  65.9 6.8 %shard_map.49.refs_1_ = bf16[512,2048]{1,0:T(8,128)(2,1)S(1)} custom-call(s32[13]{0:T(128)S(1)} %stack.85.place_ref, bf16[512,2048]{1,0:T(8,128)(2,1)} %collective-permute-done.9.rows_ref, bf16[1280,2048]{1,0:T(8,128)(2,1)S(1)} %copy-done.2, bf16[256,2048]{1,0:T(8,128)(2,1)S(1)} %collective-permute-done.5.refs_1_, ...), custom_call_target="tpu_custom_call" | custom-call | flops 1 | bytes 1 | tf_op jit(solution)/shard_map/pallas_call | solution.py:99
  72.7 1.8 %collective-permute-done.10 = bf16[512,2048]{1,0:T(8,128)(2,1)} collective-permute-done((bf16[512,2048]{1,0:T(8,128)(2,1)}, bf16[512,2048]{1,0:T(8,128)(2,1)}, u32[]{:S(2)}, u32[]{:S(2)}) %collective-permute-start.10) | collective-permute-done | bytes 2097184 | tf_op jit(solution)/shard_map/ppermute | solution.py:243
  74.5 4.0 %shard_map.50 = (bf16[2,1024,128]{2,1,0:T(8,128)(2,1)S(1)}, bf16[2,1024,128]{2,1,0:T(8,128)(2,1)S(1)}) custom-call(s32[1]{0:T(128)} %bitcast.4.half_ref, bf16[512,2048]{1,0:T(8,128)(2,1)S(1)} %shard_map.48.refs_0_, bf16[512,2048]{1,0:T(8,128)(2,1)S(1)} %shard_map.49.refs_1_, bf16[2,2,128,2048]{3,2,1,0:T(8,128)(2,1)} %bitcast.21.refs_2_, ...), custom_call_target="tpu_custom_call" | custom-call | flops 1 | bytes 1 | tf_op jit(solution)/shard_map/pallas_call | solution.py:130
  78.4 0.1 collective-permute-start.11
  78.5 0.5 collective-permute-start.15
  79.0 4.0 %shard_map.51 = (f32[2,1024,128]{2,1,0:T(8,128)S(1)}, f32[2,1024,128]{2,1,0:T(8,128)S(1)}) custom-call(s32[1]{0:T(128)} %bitcast.23.half_ref, bf16[512,2048]{1,0:T(8,128)(2,1)S(1)} %shard_map.48.refs_0_, bf16[512,2048]{1,0:T(8,128)(2,1)S(1)} %shard_map.49.refs_1_, bf16[2,2,128,2048]{3,2,1,0:T(8,128)(2,1)} %bitcast.21.refs_2_, ...), custom_call_target="tpu_custom_call" | custom-call | flops 2147483648 | bytes 1 | tf_op jit(solution)/shard_map/pallas_call | solution.py:130
  83.0 0.0 collective-permute-done.11.got_ref
  83.0 0.6 shard_map.52
  83.7 1.7 %collective-permute-start.12 = (bf16[2,512,128]{2,1,0:T(8,128)(2,1)S(1)}, bf16[2,512,128]{2,1,0:T(8,128)(2,1)S(1)}, u32[]{:S(2)}, u32[]{:S(2)}) collective-permute-start(bf16[2,512,128]{2,1,0:T(8,128)(2,1)S(1)} %bitcast.30), channel_id=1, source_target_pairs={{1,0},{0,1},{3,2},{2,3},{5,4},{4,5},{7,6},{6,7},{9,8},{8,9},{11,10... | collective-permute-start | bytes 786440 | tf_op jit(solution)/shard_map/ppermute | solution.py:239
  85.4 0.1 pad_add_fusion.1.index_ref
  85.5 0.0 collective-permute-done.15.got_ref
  85.5 0.6 shard_map.55
  86.1 1.6 %collective-permute-start.16 = (bf16[2,512,128]{2,1,0:T(8,128)(2,1)S(1)}, bf16[2,512,128]{2,1,0:T(8,128)(2,1)S(1)}, u32[]{:S(2)}, u32[]{:S(2)}) collective-permute-start(bf16[2,512,128]{2,1,0:T(8,128)(2,1)S(1)} %bitcast.31), channel_id=1, source_target_pairs={{0,8},{4,12},{8,0},{12,4},{16,24},{20,28},{24,16},{28,20},{1,9},{5... | collective-permute-start | bytes 786440 | tf_op jit(solution)/shard_map/ppermute | solution.py:253
  87.7 4.3 %collective-permute-done.12.refs_1_ = bf16[2,512,128]{2,1,0:T(8,128)(2,1)S(1)} collective-permute-done((bf16[2,512,128]{2,1,0:T(8,128)(2,1)S(1)}, bf16[2,512,128]{2,1,0:T(8,128)(2,1)S(1)}, u32[]{:S(2)}, u32[]{:S(2)}) %collective-permute-start.12) | collective-permute-done | bytes 262176 | tf_op jit(solution)/shard_map/ppermute | solution.py:239
  92.0 0.6 shard_map.53
  92.6 1.8 %collective-permute-start.13 = (bf16[2,512,128]{2,1,0:T(8,128)(2,1)S(1)}, bf16[2,512,128]{2,1,0:T(8,128)(2,1)S(1)}, u32[]{:S(2)}, u32[]{:S(2)}) collective-permute-start(bf16[2,512,128]{2,1,0:T(8,128)(2,1)S(1)} %get-tuple-element.39), channel_id=1, source_target_pairs={{0,8},{4,12},{8,0},{12,4},{16,24},{20,28},{24,16},{28,20},{1,9},{5... | collective-permute-start | bytes 786440 | tf_op jit(solution)/shard_map/ppermute | solution.py:253
  94.5 0.1 pad_add_fusion.index_ref
  94.5 0.0 collective-permute-done.16.refs_0_
  94.5 0.6 shard_map.56
  95.1 2.7 %collective-permute-start.17 = (bf16[512,128]{1,0:T(8,128)(2,1)S(1)}, bf16[512,128]{1,0:T(8,128)(2,1)S(1)}, u32[]{:S(2)}, u32[]{:S(2)}) collective-permute-start(bf16[512,128]{1,0:T(8,128)(2,1)S(1)} %bitcast.32), channel_id=1, source_target_pairs={{0,16},{4,20},{8,24},{12,28},{16,0},{20,4},{24,8},{28,12},{1,17},{... | collective-permute-start | bytes 393224 | tf_op jit(solution)/shard_map/ppermute | solution.py:260
  97.8 5.2 %collective-permute-done.13.refs_0_ = bf16[2,512,128]{2,1,0:T(8,128)(2,1)S(1)} collective-permute-done((bf16[2,512,128]{2,1,0:T(8,128)(2,1)S(1)}, bf16[2,512,128]{2,1,0:T(8,128)(2,1)S(1)}, u32[]{:S(2)}, u32[]{:S(2)}) %collective-permute-start.13) | collective-permute-done | bytes 262176 | tf_op jit(solution)/shard_map/ppermute | solution.py:253
  103.0 0.6 shard_map.54
  103.6 2.0 %collective-permute-start.14 = (bf16[512,128]{1,0:T(8,128)(2,1)S(1)}, bf16[512,128]{1,0:T(8,128)(2,1)S(1)}, u32[]{:S(2)}, u32[]{:S(2)}) collective-permute-start(bf16[512,128]{1,0:T(8,128)(2,1)S(1)} %bitcast.33), channel_id=1, source_target_pairs={{0,16},{4,20},{8,24},{12,28},{16,0},{20,4},{24,8},{28,12},{1,17},{... | collective-permute-start | bytes 393224 | tf_op jit(solution)/shard_map/ppermute | solution.py:260
  105.6 0.0 collective-permute-done.17
  105.6 5.2 %collective-permute-start.18 = (bf16[512,128]{1,0:T(8,128)(2,1)S(1)}, bf16[512,128]{1,0:T(8,128)(2,1)S(1)}, u32[]{:S(2)}, u32[]{:S(2)}) collective-permute-start(bf16[512,128]{1,0:T(8,128)(2,1)S(1)} %add_convert_fusion), channel_id=1, source_target_pairs={{0,0},{1,8},{2,2},{3,10},{4,4},{5,12},{6,6},{7,14},{8,1},{9,9},{10... | collective-permute-start | bytes 393224 | tf_op jit(solution)/shard_map/ppermute | solution.py:267
  110.9 0.1 collective-permute-done.14
  111.0 2.8 %collective-permute-done.18 = bf16[512,128]{1,0:T(8,128)(2,1)S(1)} collective-permute-done((bf16[512,128]{1,0:T(8,128)(2,1)S(1)}, bf16[512,128]{1,0:T(8,128)(2,1)S(1)}, u32[]{:S(2)}, u32[]{:S(2)}) %collective-permute-start.18) | collective-permute-done | bytes 131104 | tf_op jit(solution)/shard_map/ppermute | solution.py:267
  113.8 0.7 pad_maximum_fusion
  (7 shorter events, 0.2 us)
Async XLA Ops:
  1.1 13.7 %collective-permute-start = (bf16[128,2048]{1,0:T(8,128)(2,1)S(1)}, bf16[128,2048]{1,0:T(8,128)(2,1)S(1)}, u32[]{:S(2)}, u32[]{:S(2)}) collective-permute-start(bf16[128,2048]{1,0:T(8,128)(2,1)S(1)} %constant_dynamic-slice_fusion), channel_id=1, source_target_pairs={{1,0},{0,1},{3,2},{2,3},{5,4},{4,5},{7,6},{6,7},{9,8},{8,9},{11,10... | collective-permute-start | bytes 1572872 | tf_op jit(solution)/shard_map/ppermute | solution.py:239
  1.2 13.7 %collective-permute-start.1 = (bf16[128,2048]{1,0:T(8,128)(2,1)S(1)}, bf16[128,2048]{1,0:T(8,128)(2,1)S(1)}, u32[]{:S(2)}, u32[]{:S(2)}) collective-permute-start(bf16[128,2048]{1,0:T(8,128)(2,1)S(1)} %constant_dynamic-slice_fusion), channel_id=1, source_target_pairs={{2,0},{3,1},{0,2},{1,3},{6,4},{7,5},{4,6},{5,7},{10,8},{11,9},{8,1... | collective-permute-start | bytes 1572872 | tf_op jit(solution)/shard_map/ppermute | solution.py:243
  3.2 1.6 %copy-start.4 = (bf16[1,512,2048]{2,1,0:T(8,128)(2,1)S(1)}, bf16[1,512,2048]{2,1,0:T(8,128)(2,1)}, u32[]{:S(2)}) copy-start(bf16[1,512,2048]{2,1,0:T(8,128)(2,1)} %param.5) | copy-start | bytes 6291460
  4.8 0.7 copy-start.5
  6.7 25.1 %copy-start.3 = (bf16[512,2048]{1,0:T(8,128)(2,1)S(1)}, bf16[512,2048]{1,0:T(8,128)(2,1)}, u32[]{:S(2)}) copy-start(bf16[512,2048]{1,0:T(8,128)(2,1)} %refs_0_.1) | copy-start | bytes 6291460
  15.0 4.9 %collective-permute-start.3 = (bf16[256,2048]{1,0:T(8,128)(2,1)S(1)}, bf16[256,2048]{1,0:T(8,128)(2,1)S(1)}, u32[]{:S(2)}, u32[]{:S(2)}) collective-permute-start(bf16[256,2048]{1,0:T(8,128)(2,1)S(1)} %constant_dynamic-update-slice_fusion.refs_1_), channel_id=1, source_target_pairs={{4,0},{0,4},{12,8},{8,12},{20,16},{16,20},{28,24},{24,28},{5,1},{1... | collective-permute-start | bytes 3145736 | tf_op jit(solution)/shard_map/ppermute | solution.py:246
  15.1 14.8 %collective-permute-start.2 = (bf16[128,2048]{1,0:T(8,128)(2,1)S(1)}, bf16[128,2048]{1,0:T(8,128)(2,1)S(1)}, u32[]{:S(2)}, u32[]{:S(2)}) collective-permute-start(bf16[128,2048]{1,0:T(8,128)(2,1)S(1)} %collective-permute-done), channel_id=1, source_target_pairs={{2,0},{3,1},{0,2},{1,3},{6,4},{7,5},{4,6},{5,7},{10,8},{11,9},{8,1... | collective-permute-start | bytes 1572872 | tf_op jit(solution)/shard_map/ppermute | solution.py:243
  16.8 26.0 %collective-permute-start.5 = (bf16[256,2048]{1,0:T(8,128)(2,1)S(1)}, bf16[256,2048]{1,0:T(8,128)(2,1)S(1)}, u32[]{:S(2)}, u32[]{:S(2)}) collective-permute-start(bf16[256,2048]{1,0:T(8,128)(2,1)S(1)} %constant_dynamic-update-slice_fusion.refs_1_), channel_id=1, source_target_pairs={{8,0},{12,4},{0,8},{4,12},{24,16},{28,20},{16,24},{20,28},{9,1},{1... | collective-permute-start | bytes 3145736 | tf_op jit(solution)/shard_map/ppermute | solution.py:246
  18.4 47.5 %collective-permute-start.9 = (bf16[512,2048]{1,0:T(8,128)(2,1)S(1)}, bf16[512,2048]{1,0:T(8,128)(2,1)}, u32[]{:S(2)}, u32[]{:S(2)}) collective-permute-start(bf16[512,2048]{1,0:T(8,128)(2,1)S(1)} %shard_map.46.rows_ref), channel_id=1, source_target_pairs={{1,0},{0,1},{3,2},{2,3},{5,4},{4,5},{7,6},{6,7},{9,8},{8,9},{11,10... | collective-permute-start | bytes 6291464 | tf_op jit(solution)/shard_map/ppermute | solution.py:239
  19.9 54.6 %collective-permute-start.10 = (bf16[512,2048]{1,0:T(8,128)(2,1)}, bf16[512,2048]{1,0:T(8,128)(2,1)}, u32[]{:S(2)}, u32[]{:S(2)}) collective-permute-start(bf16[512,2048]{1,0:T(8,128)(2,1)} %bitcast.20), channel_id=1, source_target_pairs={{2,0},{3,1},{0,2},{1,3},{6,4},{7,5},{4,6},{5,7},{10,8},{11,9},{8,1... | collective-permute-start | bytes 6291464 | tf_op jit(solution)/shard_map/ppermute | solution.py:243
  29.9 1.9 %collective-permute-start.4 = (bf16[128,2048]{1,0:T(8,128)(2,1)S(1)}, bf16[128,2048]{1,0:T(8,128)(2,1)S(1)}, u32[]{:S(2)}, u32[]{:S(2)}) collective-permute-start(bf16[128,2048]{1,0:T(8,128)(2,1)S(1)} %collective-permute-done.2.refs_2_), channel_id=1, source_target_pairs={{4,0},{0,4},{12,8},{8,12},{20,16},{16,20},{28,24},{24,28},{5,1},{1... | collective-permute-start | bytes 1572872 | tf_op jit(solution)/shard_map/ppermute | solution.py:246
  29.9 23.5 %collective-permute-start.6 = (bf16[128,2048]{1,0:T(8,128)(2,1)S(1)}, bf16[128,2048]{1,0:T(8,128)(2,1)}, u32[]{:S(2)}, u32[]{:S(2)}) collective-permute-start(bf16[128,2048]{1,0:T(8,128)(2,1)S(1)} %collective-permute-done.2.refs_2_), channel_id=1, source_target_pairs={{8,0},{12,4},{0,8},{4,12},{24,16},{28,20},{16,24},{20,28},{9,1},{1... | collective-permute-start | bytes 1572872 | tf_op jit(solution)/shard_map/ppermute | solution.py:246
  32.2 2.3 %copy-start = (bf16[1280,2048]{1,0:T(8,128)(2,1)}, bf16[1280,2048]{1,0:T(8,128)(2,1)S(1)}, u32[]{:S(2)}) copy-start(bf16[1280,2048]{1,0:T(8,128)(2,1)S(1)} %shard_map.47.refs_0_) | copy-start | bytes 15728644
  42.8 12.8 %collective-permute-start.7 = (bf16[256,2048]{1,0:T(8,128)(2,1)S(1)}, bf16[256,2048]{1,0:T(8,128)(2,1)}, u32[]{:S(2)}, u32[]{:S(2)}) collective-permute-start(bf16[256,2048]{1,0:T(8,128)(2,1)S(1)} %collective-permute-done.5.refs_1_), channel_id=1, source_target_pairs={{4,0},{0,4},{12,8},{8,12},{20,16},{16,20},{28,24},{24,28},{5,1},{1... | collective-permute-start | bytes 3145736 | tf_op jit(solution)/shard_map/ppermute | solution.py:246
  53.4 2.3 %collective-permute-start.8 = (bf16[128,2048]{1,0:T(8,128)(2,1)}, bf16[128,2048]{1,0:T(8,128)(2,1)}, u32[]{:S(2)}, u32[]{:S(2)}) collective-permute-start(bf16[128,2048]{1,0:T(8,128)(2,1)} %collective-permute-done.6.refs_2_), channel_id=1, source_target_pairs={{4,0},{0,4},{12,8},{8,12},{20,16},{16,20},{28,24},{24,28},{5,1},{1... | collective-permute-start | bytes 1572872 | tf_op jit(solution)/shard_map/ppermute | solution.py:246
  55.7 2.5 %copy-start.1 = (bf16[1280,2048]{1,0:T(8,128)(2,1)S(1)}, bf16[1280,2048]{1,0:T(8,128)(2,1)}, u32[]{:S(2)}) copy-start(bf16[1280,2048]{1,0:T(8,128)(2,1)} %copy-done) | copy-start | bytes 15728644
  58.1 7.8 %copy-start.2 = (bf16[1280,2048]{1,0:T(8,128)(2,1)S(1)}, bf16[1280,2048]{1,0:T(8,128)(2,1)}, u32[]{:S(2)}) copy-start(bf16[1280,2048]{1,0:T(8,128)(2,1)} %copy-done) | copy-start | bytes 15728644
  78.4 4.6 %collective-permute-start.11 = (bf16[2,1024,128]{2,1,0:T(8,128)(2,1)S(1)}, bf16[2,1024,128]{2,1,0:T(8,128)(2,1)S(1)}, u32[]{:S(2)}, u32[]{:S(2)}) collective-permute-start(bf16[2,1024,128]{2,1,0:T(8,128)(2,1)S(1)} %get-tuple-element.32), channel_id=1, source_target_pairs={{4,0},{0,4},{12,8},{8,12},{20,16},{16,20},{28,24},{24,28},{5,1},{1... | collective-permute-start | bytes 1572872 | tf_op jit(solution)/shard_map/ppermute | solution.py:246
  78.5 6.9 %collective-permute-start.15 = (bf16[2,1024,128]{2,1,0:T(8,128)(2,1)S(1)}, bf16[2,1024,128]{2,1,0:T(8,128)(2,1)S(1)}, u32[]{:S(2)}, u32[]{:S(2)}) collective-permute-start(bf16[2,1024,128]{2,1,0:T(8,128)(2,1)S(1)} %get-tuple-element.33), channel_id=1, source_target_pairs={{4,0},{0,4},{12,8},{8,12},{20,16},{16,20},{28,24},{24,28},{5,1},{1... | collective-permute-start | bytes 1572872 | tf_op jit(solution)/shard_map/ppermute | solution.py:246
  83.7 8.4 %collective-permute-start.12 = (bf16[2,512,128]{2,1,0:T(8,128)(2,1)S(1)}, bf16[2,512,128]{2,1,0:T(8,128)(2,1)S(1)}, u32[]{:S(2)}, u32[]{:S(2)}) collective-permute-start(bf16[2,512,128]{2,1,0:T(8,128)(2,1)S(1)} %bitcast.30), channel_id=1, source_target_pairs={{1,0},{0,1},{3,2},{2,3},{5,4},{4,5},{7,6},{6,7},{9,8},{8,9},{11,10... | collective-permute-start | bytes 786440 | tf_op jit(solution)/shard_map/ppermute | solution.py:239
  86.1 8.4 %collective-permute-start.16 = (bf16[2,512,128]{2,1,0:T(8,128)(2,1)S(1)}, bf16[2,512,128]{2,1,0:T(8,128)(2,1)S(1)}, u32[]{:S(2)}, u32[]{:S(2)}) collective-permute-start(bf16[2,512,128]{2,1,0:T(8,128)(2,1)S(1)} %bitcast.31), channel_id=1, source_target_pairs={{0,8},{4,12},{8,0},{12,4},{16,24},{20,28},{24,16},{28,20},{1,9},{5... | collective-permute-start | bytes 786440 | tf_op jit(solution)/shard_map/ppermute | solution.py:253
  92.6 10.3 %collective-permute-start.13 = (bf16[2,512,128]{2,1,0:T(8,128)(2,1)S(1)}, bf16[2,512,128]{2,1,0:T(8,128)(2,1)S(1)}, u32[]{:S(2)}, u32[]{:S(2)}) collective-permute-start(bf16[2,512,128]{2,1,0:T(8,128)(2,1)S(1)} %get-tuple-element.39), channel_id=1, source_target_pairs={{0,8},{4,12},{8,0},{12,4},{16,24},{20,28},{24,16},{28,20},{1,9},{5... | collective-permute-start | bytes 786440 | tf_op jit(solution)/shard_map/ppermute | solution.py:253
  95.1 10.4 %collective-permute-start.17 = (bf16[512,128]{1,0:T(8,128)(2,1)S(1)}, bf16[512,128]{1,0:T(8,128)(2,1)S(1)}, u32[]{:S(2)}, u32[]{:S(2)}) collective-permute-start(bf16[512,128]{1,0:T(8,128)(2,1)S(1)} %bitcast.32), channel_id=1, source_target_pairs={{0,16},{4,20},{8,24},{12,28},{16,0},{20,4},{24,8},{28,12},{1,17},{... | collective-permute-start | bytes 393224 | tf_op jit(solution)/shard_map/ppermute | solution.py:260
  103.6 7.3 %collective-permute-start.14 = (bf16[512,128]{1,0:T(8,128)(2,1)S(1)}, bf16[512,128]{1,0:T(8,128)(2,1)S(1)}, u32[]{:S(2)}, u32[]{:S(2)}) collective-permute-start(bf16[512,128]{1,0:T(8,128)(2,1)S(1)} %bitcast.33), channel_id=1, source_target_pairs={{0,16},{4,20},{8,24},{12,28},{16,0},{20,4},{24,8},{28,12},{1,17},{... | collective-permute-start | bytes 393224 | tf_op jit(solution)/shard_map/ppermute | solution.py:260
  105.6 8.2 %collective-permute-start.18 = (bf16[512,128]{1,0:T(8,128)(2,1)S(1)}, bf16[512,128]{1,0:T(8,128)(2,1)S(1)}, u32[]{:S(2)}, u32[]{:S(2)}) collective-permute-start(bf16[512,128]{1,0:T(8,128)(2,1)S(1)} %add_convert_fusion), channel_id=1, source_target_pairs={{0,0},{1,8},{2,2},{3,10},{4,4},{5,12},{6,6},{7,14},{8,1},{9,9},{10... | collective-permute-start | bytes 393224 | tf_op jit(solution)/shard_map/ppermute | solution.py:267

commit v4 on v3

--- a/solution.py
+++ b/solution.py
@@ -10,6 +10,7 @@
 
 SHARE = 4
 PIECES = 2
+FIRST = (1, 2)
 VMEM_BYTES = 20 * 1024 * 1024
 COST = pl.CostEstimate(flops=1, bytes_accessed=1, transcendentals=0)
 WHOLE = pl.BlockSpec(memory_space=pltpu.VMEM)
@@ -79,7 +80,16 @@
 
 
 def inner_kernel(sizes, n_parts, place_ref, rows_ref, *refs):
-    part_refs, (out_ref, ordered) = refs[:n_parts], refs[n_parts:]
+    part_refs, refs = refs[:n_parts], refs[n_parts:]
+    copies = []
+    if len(refs) > 2:
+        half_ref, right_ref, out_ref, right_out, ordered, sems = refs
+        for k in range(2):
+            half = half_ref[0] if k == 0 else 1 - half_ref[0]
+            copies.append(pltpu.make_async_copy(right_ref.at[half], right_out.at[k], sems.at[k]))
+            copies[-1].start()
+    else:
+        out_ref, ordered = refs
     at = 0
     for p, size in enumerate(sizes):
         cols = pl.ds(pl.multiple_of(place_ref[p], size), size)
@@ -91,70 +101,112 @@
         psi = jnp.concatenate([ref[:, cols] for ref in part_refs], 0)
         value = jnp.dot(ordered[...], psi, preferred_element_type=jnp.float32)
         out_ref[:, cols] = value.astype(out_ref.dtype)
-
-
-def inner_of(rows, parts, sizes, places):
+    for copy in copies:
+        copy.wait()
+
+
+def inner_of(rows, parts, sizes, places, right=None, half=None):
     height, depth = rows.shape
-    width = parts[0].shape[1]
+    kind = parts[0].dtype
+    shape, extra, scratch = [vmem((height, parts[0].shape[1]), kind)], [], [pltpu.VMEM((height, depth), kind)]
+    if right is not None:
+        shape.append(vmem(right.shape, kind))
+        extra = [half.astype(jnp.int32).reshape(1), right]
+        scratch.append(pltpu.SemaphoreType.DMA((2,)))
     return pl.pallas_call(
         functools.partial(inner_kernel, sizes, len(parts)),
-        in_specs=[SCALARS] + [WHOLE] * (1 + len(parts)),
-        out_specs=WHOLE,
-        out_shape=vmem((height, width), parts[0].dtype),
-        scratch_shapes=[pltpu.VMEM((height, depth), rows.dtype)],
-        compiler_params=params(),
-        cost_estimate=COST,
-    )(places, *held([rows, *parts]))
-
-
-def outer_kernel(n_inner, pieces, half_ref, *refs):
-    inner_refs, right_refs, out_refs = refs[:n_inner], refs[n_inner:-pieces], refs[-pieces:]
-    blocks, _, wide = out_refs[0].shape
-    right = jnp.concatenate([ref[p] for p in range(pieces) for ref in right_refs], 0)
-    at = 0
-    for ref in inner_refs:
+        in_specs=[SCALARS] + [WHOLE] * (1 + len(parts)) + [SCALARS, ANYWHERE][: len(extra)],
+        out_specs=[WHOLE] * len(shape),
+        out_shape=shape,
+        scratch_shapes=scratch,
+        compiler_params=params(),
+        cost_estimate=COST,
+    )(places, *held([rows, *parts]), *extra)
+
+
+def products(inner_refs, right, outs, j):
+    for e, ref in enumerate(inner_refs):
         value = lax.dot_general(
             ref[...], right, (((1,), (1,)), ((), ())), preferred_element_type=jnp.float32
         )
-        for p, out_ref in enumerate(out_refs):
-            for j in range(blocks):
-                col = (p * blocks + j) * wide
-                out_ref[j, at : at + ref.shape[0], :] = value[:, col : col + wide].astype(out_ref.dtype)
-        at += ref.shape[0]
-
-
-def outer_of(inners, rights, half, kind, cost):
+        at = 0
+        for out_ref in outs:
+            size = out_ref.shape[2]
+            out_ref[j, e] = value[at : at + size, :].astype(out_ref.dtype)
+            at += size
+
+
+def give_kernel(n_inner, n_near, half_ref, *refs):
+    inner_refs, own_ref, near_refs = refs[:n_inner], refs[n_inner], refs[n_inner + 1 : n_inner + 1 + n_near]
+    outs, kept_refs = refs[n_inner + 1 + n_near :][:PIECES], refs[n_inner + 1 + n_near + PIECES : -2]
+    held_ref, sems = refs[-2:]
+    copies = []
+    for k, targets in enumerate(([held_ref.at[j] for j in range(n_near)], kept_refs)):
+        half = half_ref[0] if k == 0 else 1 - half_ref[0]
+        for j, (ref, target) in enumerate(zip(near_refs, targets)):
+            copies.append(pltpu.make_async_copy(ref.at[half], target, sems.at[k, j]))
+            copies[-1].start()
+    products(inner_refs, own_ref[0], outs, 0)
+    for j in range(n_near):
+        copies[j].wait()
+        products(inner_refs, held_ref[j], outs, 1 + j)
+    for copy in copies[n_near:]:
+        copy.wait()
+
+
+def give_of(inners, own, nears, half, sizes):
+    _, rows, depth = own.shape
+    made = pl.pallas_call(
+        functools.partial(give_kernel, len(inners), len(nears)),
+        in_specs=[SCALARS] + [WHOLE] * (len(inners) + 1) + [ANYWHERE] * len(nears),
+        out_specs=[WHOLE] * (PIECES + len(nears)),
+        out_shape=[vmem((1 + len(nears), len(inners), size, rows), jnp.bfloat16) for size in sizes]
+        + [vmem((rows, depth), own.dtype)] * len(nears),
+        scratch_shapes=[
+            pltpu.VMEM((len(nears), rows, depth), own.dtype),
+            pltpu.SemaphoreType.DMA((2, len(nears))),
+        ],
+        compiler_params=params(),
+        cost_estimate=COST,
+    )(half.astype(jnp.int32).reshape(1), *held([*inners, own]), *nears)
+    return made[:PIECES], made[PIECES:]
+
+
+def keep_kernel(n_inner, *refs):
+    inner_refs, own_ref, rest = refs[:n_inner], refs[n_inner], refs[n_inner + 1 :]
+    near_refs, outs = rest[:-PIECES], rest[-PIECES:]
+    products(inner_refs, own_ref[1], outs, 0)
+    for j, ref in enumerate(near_refs):
+        products(inner_refs, ref[...], outs, 1 + j)
+
+
+def keep_of(inners, own, nears, sizes):
     height = sum(a.shape[0] for a in inners)
-    _, pieces, wide, depth = rights[0].shape
-    spec = pl.BlockSpec((None, pieces, wide, depth), lambda i, half: (half[0], 0, 0, 0))
-    return pl.pallas_call(
-        functools.partial(outer_kernel, len(inners), pieces),
-        grid_spec=pltpu.PrefetchScalarGridSpec(
-            num_scalar_prefetch=1,
-            grid=(1,),
-            in_specs=[WHOLE] * len(inners) + [spec] * len(rights),
-            out_specs=[WHOLE] * pieces,
-        ),
-        out_shape=[vmem((len(rights), height, wide), kind)] * pieces,
-        compiler_params=params(),
-        cost_estimate=cost,
-    )(half.astype(jnp.int32).reshape(1), *held(inners), *rights)
+    _, rows, depth = own.shape
+    flops = 2 * height * (1 + len(nears)) * rows * depth
+    return pl.pallas_call(
+        functools.partial(keep_kernel, len(inners)),
+        in_specs=[WHOLE] * (len(inners) + 1 + len(nears)),
+        out_specs=[WHOLE] * PIECES,
+        out_shape=[vmem((1 + len(nears), len(inners), size, rows), jnp.float32) for size in sizes],
+        compiler_params=params(),
+        cost_estimate=pl.CostEstimate(flops=flops, bytes_accessed=1, transcendentals=0),
+    )(*held([*inners, own, *nears]))
 
 
 def cores_kernel(index_ref, keep_ref, got_ref, kept_ref, sent_ref):
-    height = kept_ref.shape[1]
     for k in range(index_ref.shape[0]):
-        rows = pl.ds(pl.multiple_of(index_ref[k] * height, height), height)
+        block = index_ref[k]
         for j in range(kept_ref.shape[0]):
-            total = keep_ref[j, rows, :] + got_ref[j, rows, :]
+            total = keep_ref[j, block] + got_ref[j, block]
             if k == 0:
                 kept_ref[j] = total
             else:
                 sent_ref[k - 1, j] = total.astype(sent_ref.dtype)
 
 
-def cores_summed(keep, got, index, height):
-    blocks, _, wide = keep.shape
+def cores_summed(keep, got, index):
+    blocks, _, height, wide = keep.shape
     others = index.shape[0] - 1
     return pl.pallas_call(
         cores_kernel,
@@ -302,25 +354,27 @@
     near_left = [from_lo(own_left, j) for j in range(1, s)]
     own_right = after(right_ops[0], far if sharing == 1 else near_core)
     rights = [own_right] + [from_hi(own_right, j) for j in range(1, s)]
-    rights = [a.reshape(2, PIECES, height // (2 * PIECES), width) for a in rights]
-
-    inners = [inner_of(own_left, parts, sizes, places)]
+    rights = [a.reshape(2, height // 2, width) for a in rights]
+
+    inners = list(inner_of(own_left, parts, sizes, places))
     for rows in near_left:
-        inners.append(inner_of(after(rows, inners[-1]), parts, sizes, places))
+        rows = after(rows, inners[-1])
+        inner, own_halves = inner_of(rows, parts, sizes, places, rights[0], 1 - core)
+        inners.append(inner)
 
     def members(own, base):
         return jnp.stack([(own + j - base) % s for j in range(s)]).astype(jnp.int32)
 
-    give = outer_of(inners, rights, 1 - core, jnp.bfloat16, COST)
+    cut = height * FIRST[0] // FIRST[1] // 32 * 32
+    row_sizes = [cut, height - cut]
+    give, near_halves = give_of(inners, own_halves, rights[1:], 1 - core, row_sizes)
     got = [from_term(v, 1) for v in give]
-    flops = 2 * len(inners) * height * len(rights) * (height // 2) * width
-    cost = pl.CostEstimate(flops=flops, bytes_accessed=1, transcendentals=0)
-    keep = outer_of(inners, rights, after(core, give), jnp.float32, cost)
+    keep = keep_of(inners, own_halves, near_halves, row_sizes)
     outs = []
     for p in range(PIECES):
         home_first = p % 2 == 0
         index = jnp.arange(s, dtype=jnp.int32) if home_first else members(zl, lo)
-        kept, sent = cores_summed(keep[p], got[p], index, height)
+        kept, sent = cores_summed(keep[p], got[p], index)
         if home_first:
             held_blocks = [kept] + [from_lo(sent[s - j - 1], j) for j in range(1, s)]
             kept, *sent = chosen_of(held_blocks, members(zl, lo))
@@ -329,7 +383,7 @@
             final = final + to_zh(sent[j - 1], j).astype(jnp.float32)
         final = final.astype(jnp.bfloat16)
         outs.append(final if home_first else crossed(final))
-    return jnp.concatenate(outs, 1)
+    return jnp.concatenate(outs, 0)
 
 
 def solution(mesh):

time: 116 us -> 113 us (0.974)
  Pallas kernels: 25.6 us -> 22.7 us
    pallas_call x2, Pallas kernels: 7.94 us -> 4.98 us  [the longest x1 2.6 us: give_of(): pl.pallas_call(functools.partial(give_kernel, len(inners), len(nears)), i...]
  transfers between devices with their start and end apart: 19 -> 19, of which waited for: 13 -> 13; matrix products, arithmetic and copies ran while one was open for 0% -> 0% of each run, Pallas kernels for 19% -> 18%
where the time goes in v4:
time: 113 us; the launch traced here: 112 us
  waiting for transfers between devices  54.5 us (48%)
  starting transfers between devices  24.9 us (22%)
  Pallas kernels  22.7 us (20%)
  local copies, waits for them, and re-layouts  8.34 us (7%)
    ppermute x8, waiting for transfers between devices, from_term(): return lax.ppermute(value, 'term', [(a ^ bit, a) for a in range(terms)])  21.2 us
    ppermute x3, waiting for transfers between devices, from_lo(): return lax.ppermute(value, 'row', pairs)  13.9 us
    pallas_call x2, Pallas kernels, inner_of(): pl.pallas_call(functools.partial(inner_kernel, sizes, len(parts)), in_spe...  13 us
    ppermute x3, waiting for transfers between devices, from_hi(): return lax.ppermute(value, 'row', pairs)  11.3 us
    unnamed x13, local copies, waits for them, and re-layouts  7.13 us
    ppermute x1, starting transfers between devices, crossed(): return lax.ppermute(value, ('term', 'row'), pairs)  5.24 us
    ppermute x2, waiting for transfers between devices, to_zl(): return lax.ppermute(value, 'term', pairs)  5.18 us
    ppermute x2, starting transfers between devices, to_zh(): return lax.ppermute(value, 'term', pairs)  4.65 us
  transfers between devices with their start and end apart: 19, of which 13 were waited for; matrix products, arithmetic and copies ran while one was open for 0% of the time, Pallas kernels for 18%

profile of v4, /device:TPU:2, one launch (start us, length us, event | category | flops | bytes accessed | tf_op | source)
XLA Modules:
  0.0 111.5 jit_solution(5383607560924229538)
XLA Ops:
  0.0 1.1 constant_dynamic-slice_fusion
  1.1 0.1 collective-permute-start
  1.2 2.0 %collective-permute-start.1 = (bf16[128,2048]{1,0:T(8,128)(2,1)S(1)}, bf16[128,2048]{1,0:T(8,128)(2,1)S(1)}, u32[]{:S(2)}, u32[]{:S(2)}) collective-permute-start(bf16[128,2048]{1,0:T(8,128)(2,1)S(1)} %constant_dynamic-slice_fusion), channel_id=1, source_target_pairs={{2,0},{3,1},{0,2},{1,3},{6,4},{7,5},{4,6},{5,7},{10,8},{11,9},{8,1... | collective-permute-start | bytes 1572872 | tf_op jit(solution)/shard_map/ppermute | solution.py:295
  3.2 0.0 copy-start.4
  3.2 1.6 %copy-done.4 = bf16[1,512,2048]{2,1,0:T(8,128)(2,1)S(1)} copy-done((bf16[1,512,2048]{2,1,0:T(8,128)(2,1)S(1)}, bf16[1,512,2048]{2,1,0:T(8,128)(2,1)}, u32[]{:S(2)}) %copy-start.4) | copy-done | bytes 2097176
  4.8 0.0 copy-start.5
  4.8 0.7 copy-done.5
  5.5 1.2 %shard_map.46.rows_ref = bf16[512,2048]{1,0:T(8,128)(2,1)S(1)} custom-call(s32[4,16]{1,0:T(4,128)S(1)} %bitcast.28, bf16[512,2048]{1,0:T(8,128)(2,1)S(1)} %bitcast.27), custom_call_target="tpu_custom_call" | custom-call | flops 1 | bytes 1 | tf_op jit(solution)/shard_map/pallas_call | solution.py:45
  6.7 0.0 copy-start.3
  6.7 8.1 %collective-permute-done = bf16[128,2048]{1,0:T(8,128)(2,1)S(1)} collective-permute-done((bf16[128,2048]{1,0:T(8,128)(2,1)S(1)}, bf16[128,2048]{1,0:T(8,128)(2,1)S(1)}, u32[]{:S(2)}, u32[]{:S(2)}) %collective-permute-start) | collective-permute-done | bytes 524320 | tf_op jit(solution)/shard_map/ppermute | solution.py:291
  14.8 0.1 collective-permute-done.1
  15.0 0.1 collective-permute-start.3
  15.1 1.8 %collective-permute-start.2 = (bf16[128,2048]{1,0:T(8,128)(2,1)S(1)}, bf16[128,2048]{1,0:T(8,128)(2,1)S(1)}, u32[]{:S(2)}, u32[]{:S(2)}) collective-permute-start(bf16[128,2048]{1,0:T(8,128)(2,1)S(1)} %collective-permute-done), channel_id=1, source_target_pairs={{2,0},{3,1},{0,2},{1,3},{6,4},{7,5},{4,6},{5,7},{10,8},{11,9},{8,1... | collective-permute-start | bytes 1572872 | tf_op jit(solution)/shard_map/ppermute | solution.py:295
  16.8 1.6 %collective-permute-start.5 = (bf16[256,2048]{1,0:T(8,128)(2,1)S(1)}, bf16[256,2048]{1,0:T(8,128)(2,1)S(1)}, u32[]{:S(2)}, u32[]{:S(2)}) collective-permute-start(bf16[256,2048]{1,0:T(8,128)(2,1)S(1)} %constant_dynamic-update-slice_fusion.refs_1_), channel_id=1, source_target_pairs={{8,0},{12,4},{0,8},{4,12},{24,16},{28,20},{16,24},{20,28},{9,1},{1... | collective-permute-start | bytes 3145736 | tf_op jit(solution)/shard_map/ppermute | solution.py:298
  18.4 1.5 %collective-permute-start.9 = (bf16[512,2048]{1,0:T(8,128)(2,1)S(1)}, bf16[512,2048]{1,0:T(8,128)(2,1)}, u32[]{:S(2)}, u32[]{:S(2)}) collective-permute-start(bf16[512,2048]{1,0:T(8,128)(2,1)S(1)} %shard_map.46.rows_ref), channel_id=1, source_target_pairs={{1,0},{0,1},{3,2},{2,3},{5,4},{4,5},{7,6},{6,7},{9,8},{8,9},{11,10... | collective-permute-start | bytes 6291464 | tf_op jit(solution)/shard_map/ppermute | solution.py:291
  19.9 0.0 collective-permute-done.3.refs_3_
  19.9 0.5 collective-permute-start.10
  20.4 9.4 %collective-permute-done.2.refs_2_ = bf16[128,2048]{1,0:T(8,128)(2,1)S(1)} collective-permute-done((bf16[128,2048]{1,0:T(8,128)(2,1)S(1)}, bf16[128,2048]{1,0:T(8,128)(2,1)S(1)}, u32[]{:S(2)}, u32[]{:S(2)}) %collective-permute-start.2) | collective-permute-done | bytes 524320 | tf_op jit(solution)/shard_map/ppermute | solution.py:295
  29.9 0.0 collective-permute-start.4
  29.9 1.8 %collective-permute-start.6 = (bf16[128,2048]{1,0:T(8,128)(2,1)S(1)}, bf16[128,2048]{1,0:T(8,128)(2,1)}, u32[]{:S(2)}, u32[]{:S(2)}) collective-permute-start(bf16[128,2048]{1,0:T(8,128)(2,1)S(1)} %collective-permute-done.2.refs_2_), channel_id=1, source_target_pairs={{8,0},{12,4},{0,8},{4,12},{24,16},{28,20},{16,24},{20,28},{9,1},{1... | collective-permute-start | bytes 1572872 | tf_op jit(solution)/shard_map/ppermute | solution.py:298
  31.6 0.2 collective-permute-done.4.refs_4_
  31.8 0.0 copy-done.3
  31.8 0.4 shard_map.47.refs_0_
  32.2 0.0 copy-start
  32.2 2.3 %copy-done = bf16[1280,2048]{1,0:T(8,128)(2,1)} copy-done((bf16[1280,2048]{1,0:T(8,128)(2,1)}, bf16[1280,2048]{1,0:T(8,128)(2,1)S(1)}, u32[]{:S(2)}) %copy-start) | copy-done | bytes 5242904
  34.5 8.3 %collective-permute-done.5.refs_1_ = bf16[256,2048]{1,0:T(8,128)(2,1)S(1)} collective-permute-done((bf16[256,2048]{1,0:T(8,128)(2,1)S(1)}, bf16[256,2048]{1,0:T(8,128)(2,1)S(1)}, u32[]{:S(2)}, u32[]{:S(2)}) %collective-permute-start.5) | collective-permute-done | bytes 1048608 | tf_op jit(solution)/shard_map/ppermute | solution.py:298
  42.8 0.0 collective-permute-start.7
  42.8 10.6 %collective-permute-done.6.refs_2_ = bf16[128,2048]{1,0:T(8,128)(2,1)} collective-permute-done((bf16[128,2048]{1,0:T(8,128)(2,1)S(1)}, bf16[128,2048]{1,0:T(8,128)(2,1)}, u32[]{:S(2)}, u32[]{:S(2)}) %collective-permute-start.6) | collective-permute-done | bytes 524320 | tf_op jit(solution)/shard_map/ppermute | solution.py:298
  53.4 0.0 collective-permute-start.8
  53.4 0.1 stack.85.place_ref
  53.5 2.2 %collective-permute-done.8.refs_4_ = bf16[128,2048]{1,0:T(8,128)(2,1)} collective-permute-done((bf16[128,2048]{1,0:T(8,128)(2,1)}, bf16[128,2048]{1,0:T(8,128)(2,1)}, u32[]{:S(2)}, u32[]{:S(2)}) %collective-permute-start.8) | collective-permute-done | bytes 524320 | tf_op jit(solution)/shard_map/ppermute | solution.py:298
  55.7 0.0 collective-permute-done.7.refs_3_
  55.7 2.5 %copy-done.1 = bf16[1280,2048]{1,0:T(8,128)(2,1)S(1)} copy-done((bf16[1280,2048]{1,0:T(8,128)(2,1)S(1)}, bf16[1280,2048]{1,0:T(8,128)(2,1)}, u32[]{:S(2)}) %copy-start.1) | copy-done | bytes 5242904
  58.1 6.2 %shard_map.48.refs_0_ = bf16[512,2048]{1,0:T(8,128)(2,1)S(1)} custom-call(s32[13]{0:T(128)S(1)} %stack.85.place_ref, bf16[512,2048]{1,0:T(8,128)(2,1)S(1)} %shard_map.46.rows_ref, bf16[1280,2048]{1,0:T(8,128)(2,1)S(1)} %copy-done.1, bf16[256,2048]{1,0:T(8,128)(2,1)S(1)} %collective-permute-done.5.refs_1_, bf16[128,2048]{1,0:T(8,128)(2,1)} %collective-permute-done.6.refs_2_, ...), custom_call_target="tpu_custom_call" | custom-call | flops 1 | bytes 1 | tf_op jit(solution)/shard_map/pallas_call | solution.py:116
  64.4 1.6 %collective-permute-done.9.rows_ref = bf16[512,2048]{1,0:T(8,128)(2,1)} collective-permute-done((bf16[512,2048]{1,0:T(8,128)(2,1)S(1)}, bf16[512,2048]{1,0:T(8,128)(2,1)}, u32[]{:S(2)}, u32[]{:S(2)}) %collective-permute-start.9) | collective-permute-done | bytes 2097184 | tf_op jit(solution)/shard_map/ppermute | solution.py:291
  65.9 0.0 copy-done.2
  65.9 6.8 %shard_map.49 = (bf16[512,2048]{1,0:T(8,128)(2,1)S(1)}, bf16[2,256,2048]{2,1,0:T(8,128)(2,1)S(1)}) custom-call(s32[13]{0:T(128)S(1)} %stack.85.place_ref, bf16[512,2048]{1,0:T(8,128)(2,1)} %collective-permute-done.9.rows_ref, bf16[1280,2048]{1,0:T(8,128)(2,1)S(1)} %copy-done.2, bf16[256,2048]{1,0:T(8,128)(2,1)S(1)} %collective-permute-done.5.refs_1_, ...), custom_call_target="tpu_custom_call" | custom-call | flops 1 | bytes 1 | tf_op jit(solution)/shard_map/pallas_call | solution.py:116
  72.7 1.7 %collective-permute-done.10 = bf16[512,2048]{1,0:T(8,128)(2,1)} collective-permute-done((bf16[512,2048]{1,0:T(8,128)(2,1)}, bf16[512,2048]{1,0:T(8,128)(2,1)}, u32[]{:S(2)}, u32[]{:S(2)}) %collective-permute-start.10) | collective-permute-done | bytes 2097184 | tf_op jit(solution)/shard_map/ppermute | solution.py:295
  74.5 2.6 %shard_map.50 = (bf16[2,2,256,256]{3,2,1,0:T(8,128)(2,1)S(1)}, bf16[2,2,256,256]{3,2,1,0:T(8,128)(2,1)S(1)}, bf16[256,2048]{1,0:T(8,128)(2,1)S(1)}) custom-call(s32[1]{0:T(128)} %bitcast.19.refs_5_.half_ref, bf16[512,2048]{1,0:T(8,128)(2,1)S(1)} %shard_map.48.refs_0_, bf16[512,2048]{1,0:T(8,128)(2,1)S(1)} %get-tuple-element.34.refs_1_, ...), custom_call_target="tpu_custom_call" | custom-call | flops 1 | bytes 1 | tf_op jit(solution)/shard_map/pallas_call | solution.py:159
  77.1 0.1 collective-permute-start.11
  77.1 0.5 collective-permute-start.15
  77.6 2.4 %shard_map.51 = (f32[2,2,256,256]{3,2,1,0:T(8,128)S(1)}, f32[2,2,256,256]{3,2,1,0:T(8,128)S(1)}) custom-call(bf16[512,2048]{1,0:T(8,128)(2,1)S(1)} %shard_map.48.refs_0_, bf16[512,2048]{1,0:T(8,128)(2,1)S(1)} %get-tuple-element.34.refs_1_, bf16[2,256,2048]{2,1,0:T(8,128)(2,1)S(1)} %get-tuple-element.35.refs_2_, bf16[256,2048]{1,0:T(8,128)(2,1)S(1)} %get-tuple-element.36.refs_3_), custom_call_target="tpu_custom_call" | custom-call | flops 2147483648 | bytes 1 | tf_op jit(solution)/shard_map/pallas_call | solution.py:187
  80.0 0.0 collective-permute-done.11.got_ref
  80.0 0.6 shard_map.52
  80.7 1.7 %collective-permute-start.12 = (bf16[2,256,256]{2,1,0:T(8,128)(2,1)S(1)}, bf16[2,256,256]{2,1,0:T(8,128)(2,1)S(1)}, u32[]{:S(2)}, u32[]{:S(2)}) collective-permute-start(bf16[2,256,256]{2,1,0:T(8,128)(2,1)S(1)} %bitcast.29), channel_id=1, source_target_pairs={{1,0},{0,1},{3,2},{2,3},{5,4},{4,5},{7,6},{6,7},{9,8},{8,9},{11,10... | collective-permute-start | bytes 786440 | tf_op jit(solution)/shard_map/ppermute | solution.py:291
  82.4 0.1 pad_add_fusion.1.index_ref
  82.5 0.0 collective-permute-done.15.got_ref
  82.5 0.6 shard_map.55
  83.1 1.6 %collective-permute-start.16 = (bf16[2,256,256]{2,1,0:T(8,128)(2,1)S(1)}, bf16[2,256,256]{2,1,0:T(8,128)(2,1)S(1)}, u32[]{:S(2)}, u32[]{:S(2)}) collective-permute-start(bf16[2,256,256]{2,1,0:T(8,128)(2,1)S(1)} %bitcast.30), channel_id=1, source_target_pairs={{0,8},{4,12},{8,0},{12,4},{16,24},{20,28},{24,16},{28,20},{1,9},{5... | collective-permute-start | bytes 786440 | tf_op jit(solution)/shard_map/ppermute | solution.py:305
  84.8 4.3 %collective-permute-done.12.refs_1_ = bf16[2,256,256]{2,1,0:T(8,128)(2,1)S(1)} collective-permute-done((bf16[2,256,256]{2,1,0:T(8,128)(2,1)S(1)}, bf16[2,256,256]{2,1,0:T(8,128)(2,1)S(1)}, u32[]{:S(2)}, u32[]{:S(2)}) %collective-permute-start.12) | collective-permute-done | bytes 262176 | tf_op jit(solution)/shard_map/ppermute | solution.py:291
  89.0 0.6 shard_map.53
  89.7 1.8 %collective-permute-start.13 = (bf16[2,256,256]{2,1,0:T(8,128)(2,1)S(1)}, bf16[2,256,256]{2,1,0:T(8,128)(2,1)S(1)}, u32[]{:S(2)}, u32[]{:S(2)}) collective-permute-start(bf16[2,256,256]{2,1,0:T(8,128)(2,1)S(1)} %get-tuple-element.42), channel_id=1, source_target_pairs={{0,8},{4,12},{8,0},{12,4},{16,24},{20,28},{24,16},{28,20},{1,9},{5... | collective-permute-start | bytes 786440 | tf_op jit(solution)/shard_map/ppermute | solution.py:305
  91.5 0.1 pad_add_fusion.index_ref
  91.6 0.0 collective-permute-done.16.refs_0_
  91.6 0.6 shard_map.56
  92.2 2.7 %collective-permute-start.17 = (bf16[256,256]{1,0:T(8,128)(2,1)S(1)}, bf16[256,256]{1,0:T(8,128)(2,1)S(1)}, u32[]{:S(2)}, u32[]{:S(2)}) collective-permute-start(bf16[256,256]{1,0:T(8,128)(2,1)S(1)} %bitcast.31), channel_id=1, source_target_pairs={{0,16},{4,20},{8,24},{12,28},{16,0},{20,4},{24,8},{28,12},{1,17},{... | collective-permute-start | bytes 393224 | tf_op jit(solution)/shard_map/ppermute | solution.py:312
  94.8 5.2 %collective-permute-done.13.refs_0_ = bf16[2,256,256]{2,1,0:T(8,128)(2,1)S(1)} collective-permute-done((bf16[2,256,256]{2,1,0:T(8,128)(2,1)S(1)}, bf16[2,256,256]{2,1,0:T(8,128)(2,1)S(1)}, u32[]{:S(2)}, u32[]{:S(2)}) %collective-permute-start.13) | collective-permute-done | bytes 262176 | tf_op jit(solution)/shard_map/ppermute | solution.py:305
  100.0 0.6 shard_map.54
  100.6 2.0 %collective-permute-start.14 = (bf16[256,256]{1,0:T(8,128)(2,1)S(1)}, bf16[256,256]{1,0:T(8,128)(2,1)S(1)}, u32[]{:S(2)}, u32[]{:S(2)}) collective-permute-start(bf16[256,256]{1,0:T(8,128)(2,1)S(1)} %bitcast.32), channel_id=1, source_target_pairs={{0,16},{4,20},{8,24},{12,28},{16,0},{20,4},{24,8},{28,12},{1,17},{... | collective-permute-start | bytes 393224 | tf_op jit(solution)/shard_map/ppermute | solution.py:312
  102.6 0.0 collective-permute-done.17
  102.6 5.2 %collective-permute-start.18 = (bf16[256,256]{1,0:T(8,128)(2,1)S(1)}, bf16[256,256]{1,0:T(8,128)(2,1)S(1)}, u32[]{:S(2)}, u32[]{:S(2)}) collective-permute-start(bf16[256,256]{1,0:T(8,128)(2,1)S(1)} %add_convert_fusion), channel_id=1, source_target_pairs={{0,0},{1,8},{2,2},{3,10},{4,4},{5,12},{6,6},{7,14},{8,1},{9,9},{10... | collective-permute-start | bytes 393224 | tf_op jit(solution)/shard_map/ppermute | solution.py:319
  107.9 0.1 collective-permute-done.14
  108.0 2.8 %collective-permute-done.18 = bf16[256,256]{1,0:T(8,128)(2,1)S(1)} collective-permute-done((bf16[256,256]{1,0:T(8,128)(2,1)S(1)}, bf16[256,256]{1,0:T(8,128)(2,1)S(1)}, u32[]{:S(2)}, u32[]{:S(2)}) %collective-permute-start.18) | collective-permute-done | bytes 131104 | tf_op jit(solution)/shard_map/ppermute | solution.py:319
  110.8 0.7 pad_maximum_fusion
  (7 shorter events, 0.1 us)
Async XLA Ops:
  1.1 13.7 %collective-permute-start = (bf16[128,2048]{1,0:T(8,128)(2,1)S(1)}, bf16[128,2048]{1,0:T(8,128)(2,1)S(1)}, u32[]{:S(2)}, u32[]{:S(2)}) collective-permute-start(bf16[128,2048]{1,0:T(8,128)(2,1)S(1)} %constant_dynamic-slice_fusion), channel_id=1, source_target_pairs={{1,0},{0,1},{3,2},{2,3},{5,4},{4,5},{7,6},{6,7},{9,8},{8,9},{11,10... | collective-permute-start | bytes 1572872 | tf_op jit(solution)/shard_map/ppermute | solution.py:291
  1.2 13.7 %collective-permute-start.1 = (bf16[128,2048]{1,0:T(8,128)(2,1)S(1)}, bf16[128,2048]{1,0:T(8,128)(2,1)S(1)}, u32[]{:S(2)}, u32[]{:S(2)}) collective-permute-start(bf16[128,2048]{1,0:T(8,128)(2,1)S(1)} %constant_dynamic-slice_fusion), channel_id=1, source_target_pairs={{2,0},{3,1},{0,2},{1,3},{6,4},{7,5},{4,6},{5,7},{10,8},{11,9},{8,1... | collective-permute-start | bytes 1572872 | tf_op jit(solution)/shard_map/ppermute | solution.py:295
  3.2 1.6 %copy-start.4 = (bf16[1,512,2048]{2,1,0:T(8,128)(2,1)S(1)}, bf16[1,512,2048]{2,1,0:T(8,128)(2,1)}, u32[]{:S(2)}) copy-start(bf16[1,512,2048]{2,1,0:T(8,128)(2,1)} %param.5) | copy-start | bytes 6291460
  4.8 0.7 copy-start.5
  6.7 25.1 %copy-start.3 = (bf16[512,2048]{1,0:T(8,128)(2,1)S(1)}, bf16[512,2048]{1,0:T(8,128)(2,1)}, u32[]{:S(2)}) copy-start(bf16[512,2048]{1,0:T(8,128)(2,1)} %refs_0_.1) | copy-start | bytes 6291460
  15.0 4.9 %collective-permute-start.3 = (bf16[256,2048]{1,0:T(8,128)(2,1)S(1)}, bf16[256,2048]{1,0:T(8,128)(2,1)S(1)}, u32[]{:S(2)}, u32[]{:S(2)}) collective-permute-start(bf16[256,2048]{1,0:T(8,128)(2,1)S(1)} %constant_dynamic-update-slice_fusion.refs_1_), channel_id=1, source_target_pairs={{4,0},{0,4},{12,8},{8,12},{20,16},{16,20},{28,24},{24,28},{5,1},{1... | collective-permute-start | bytes 3145736 | tf_op jit(solution)/shard_map/ppermute | solution.py:298
  15.1 14.8 %collective-permute-start.2 = (bf16[128,2048]{1,0:T(8,128)(2,1)S(1)}, bf16[128,2048]{1,0:T(8,128)(2,1)S(1)}, u32[]{:S(2)}, u32[]{:S(2)}) collective-permute-start(bf16[128,2048]{1,0:T(8,128)(2,1)S(1)} %collective-permute-done), channel_id=1, source_target_pairs={{2,0},{3,1},{0,2},{1,3},{6,4},{7,5},{4,6},{5,7},{10,8},{11,9},{8,1... | collective-permute-start | bytes 1572872 | tf_op jit(solution)/shard_map/ppermute | solution.py:295
  16.8 26.0 %collective-permute-start.5 = (bf16[256,2048]{1,0:T(8,128)(2,1)S(1)}, bf16[256,2048]{1,0:T(8,128)(2,1)S(1)}, u32[]{:S(2)}, u32[]{:S(2)}) collective-permute-start(bf16[256,2048]{1,0:T(8,128)(2,1)S(1)} %constant_dynamic-update-slice_fusion.refs_1_), channel_id=1, source_target_pairs={{8,0},{12,4},{0,8},{4,12},{24,16},{28,20},{16,24},{20,28},{9,1},{1... | collective-permute-start | bytes 3145736 | tf_op jit(solution)/shard_map/ppermute | solution.py:298
  18.4 47.5 %collective-permute-start.9 = (bf16[512,2048]{1,0:T(8,128)(2,1)S(1)}, bf16[512,2048]{1,0:T(8,128)(2,1)}, u32[]{:S(2)}, u32[]{:S(2)}) collective-permute-start(bf16[512,2048]{1,0:T(8,128)(2,1)S(1)} %shard_map.46.rows_ref), channel_id=1, source_target_pairs={{1,0},{0,1},{3,2},{2,3},{5,4},{4,5},{7,6},{6,7},{9,8},{8,9},{11,10... | collective-permute-start | bytes 6291464 | tf_op jit(solution)/shard_map/ppermute | solution.py:291
  19.9 54.6 %collective-permute-start.10 = (bf16[512,2048]{1,0:T(8,128)(2,1)}, bf16[512,2048]{1,0:T(8,128)(2,1)}, u32[]{:S(2)}, u32[]{:S(2)}) collective-permute-start(bf16[512,2048]{1,0:T(8,128)(2,1)} %bitcast.20), channel_id=1, source_target_pairs={{2,0},{3,1},{0,2},{1,3},{6,4},{7,5},{4,6},{5,7},{10,8},{11,9},{8,1... | collective-permute-start | bytes 6291464 | tf_op jit(solution)/shard_map/ppermute | solution.py:295
  29.9 1.9 %collective-permute-start.4 = (bf16[128,2048]{1,0:T(8,128)(2,1)S(1)}, bf16[128,2048]{1,0:T(8,128)(2,1)S(1)}, u32[]{:S(2)}, u32[]{:S(2)}) collective-permute-start(bf16[128,2048]{1,0:T(8,128)(2,1)S(1)} %collective-permute-done.2.refs_2_), channel_id=1, source_target_pairs={{4,0},{0,4},{12,8},{8,12},{20,16},{16,20},{28,24},{24,28},{5,1},{1... | collective-permute-start | bytes 1572872 | tf_op jit(solution)/shard_map/ppermute | solution.py:298
  29.9 23.5 %collective-permute-start.6 = (bf16[128,2048]{1,0:T(8,128)(2,1)S(1)}, bf16[128,2048]{1,0:T(8,128)(2,1)}, u32[]{:S(2)}, u32[]{:S(2)}) collective-permute-start(bf16[128,2048]{1,0:T(8,128)(2,1)S(1)} %collective-permute-done.2.refs_2_), channel_id=1, source_target_pairs={{8,0},{12,4},{0,8},{4,12},{24,16},{28,20},{16,24},{20,28},{9,1},{1... | collective-permute-start | bytes 1572872 | tf_op jit(solution)/shard_map/ppermute | solution.py:298
  32.2 2.3 %copy-start = (bf16[1280,2048]{1,0:T(8,128)(2,1)}, bf16[1280,2048]{1,0:T(8,128)(2,1)S(1)}, u32[]{:S(2)}) copy-start(bf16[1280,2048]{1,0:T(8,128)(2,1)S(1)} %shard_map.47.refs_0_) | copy-start | bytes 15728644
  42.8 12.8 %collective-permute-start.7 = (bf16[256,2048]{1,0:T(8,128)(2,1)S(1)}, bf16[256,2048]{1,0:T(8,128)(2,1)}, u32[]{:S(2)}, u32[]{:S(2)}) collective-permute-start(bf16[256,2048]{1,0:T(8,128)(2,1)S(1)} %collective-permute-done.5.refs_1_), channel_id=1, source_target_pairs={{4,0},{0,4},{12,8},{8,12},{20,16},{16,20},{28,24},{24,28},{5,1},{1... | collective-permute-start | bytes 3145736 | tf_op jit(solution)/shard_map/ppermute | solution.py:298
  53.4 2.3 %collective-permute-start.8 = (bf16[128,2048]{1,0:T(8,128)(2,1)}, bf16[128,2048]{1,0:T(8,128)(2,1)}, u32[]{:S(2)}, u32[]{:S(2)}) collective-permute-start(bf16[128,2048]{1,0:T(8,128)(2,1)} %collective-permute-done.6.refs_2_), channel_id=1, source_target_pairs={{4,0},{0,4},{12,8},{8,12},{20,16},{16,20},{28,24},{24,28},{5,1},{1... | collective-permute-start | bytes 1572872 | tf_op jit(solution)/shard_map/ppermute | solution.py:298
  55.7 2.5 %copy-start.1 = (bf16[1280,2048]{1,0:T(8,128)(2,1)S(1)}, bf16[1280,2048]{1,0:T(8,128)(2,1)}, u32[]{:S(2)}) copy-start(bf16[1280,2048]{1,0:T(8,128)(2,1)} %copy-done) | copy-start | bytes 15728644
  58.1 7.8 %copy-start.2 = (bf16[1280,2048]{1,0:T(8,128)(2,1)S(1)}, bf16[1280,2048]{1,0:T(8,128)(2,1)}, u32[]{:S(2)}) copy-start(bf16[1280,2048]{1,0:T(8,128)(2,1)} %copy-done) | copy-start | bytes 15728644
  77.1 3.0 %collective-permute-start.11 = (bf16[2,2,256,256]{3,2,1,0:T(8,128)(2,1)S(1)}, bf16[2,2,256,256]{3,2,1,0:T(8,128)(2,1)S(1)}, u32[]{:S(2)}, u32[]{:S(2)}) collective-permute-start(bf16[2,2,256,256]{3,2,1,0:T(8,128)(2,1)S(1)} %get-tuple-element.38), channel_id=1, source_target_pairs={{4,0},{0,4},{12,8},{8,12},{20,16},{16,20},{28,24},{24,28},{5,1},{1... | collective-permute-start | bytes 1572872 | tf_op jit(solution)/shard_map/ppermute | solution.py:298
  77.1 5.3 %collective-permute-start.15 = (bf16[2,2,256,256]{3,2,1,0:T(8,128)(2,1)S(1)}, bf16[2,2,256,256]{3,2,1,0:T(8,128)(2,1)S(1)}, u32[]{:S(2)}, u32[]{:S(2)}) collective-permute-start(bf16[2,2,256,256]{3,2,1,0:T(8,128)(2,1)S(1)} %get-tuple-element.46), channel_id=1, source_target_pairs={{4,0},{0,4},{12,8},{8,12},{20,16},{16,20},{28,24},{24,28},{5,1},{1... | collective-permute-start | bytes 1572872 | tf_op jit(solution)/shard_map/ppermute | solution.py:298
  80.7 8.4 %collective-permute-start.12 = (bf16[2,256,256]{2,1,0:T(8,128)(2,1)S(1)}, bf16[2,256,256]{2,1,0:T(8,128)(2,1)S(1)}, u32[]{:S(2)}, u32[]{:S(2)}) collective-permute-start(bf16[2,256,256]{2,1,0:T(8,128)(2,1)S(1)} %bitcast.29), channel_id=1, source_target_pairs={{1,0},{0,1},{3,2},{2,3},{5,4},{4,5},{7,6},{6,7},{9,8},{8,9},{11,10... | collective-permute-start | bytes 786440 | tf_op jit(solution)/shard_map/ppermute | solution.py:291
  83.1 8.4 %collective-permute-start.16 = (bf16[2,256,256]{2,1,0:T(8,128)(2,1)S(1)}, bf16[2,256,256]{2,1,0:T(8,128)(2,1)S(1)}, u32[]{:S(2)}, u32[]{:S(2)}) collective-permute-start(bf16[2,256,256]{2,1,0:T(8,128)(2,1)S(1)} %bitcast.30), channel_id=1, source_target_pairs={{0,8},{4,12},{8,0},{12,4},{16,24},{20,28},{24,16},{28,20},{1,9},{5... | collective-permute-start | bytes 786440 | tf_op jit(solution)/shard_map/ppermute | solution.py:305
  89.7 10.3 %collective-permute-start.13 = (bf16[2,256,256]{2,1,0:T(8,128)(2,1)S(1)}, bf16[2,256,256]{2,1,0:T(8,128)(2,1)S(1)}, u32[]{:S(2)}, u32[]{:S(2)}) collective-permute-start(bf16[2,256,256]{2,1,0:T(8,128)(2,1)S(1)} %get-tuple-element.42), channel_id=1, source_target_pairs={{0,8},{4,12},{8,0},{12,4},{16,24},{20,28},{24,16},{28,20},{1,9},{5... | collective-permute-start | bytes 786440 | tf_op jit(solution)/shard_map/ppermute | solution.py:305
  92.2 10.4 %collective-permute-start.17 = (bf16[256,256]{1,0:T(8,128)(2,1)S(1)}, bf16[256,256]{1,0:T(8,128)(2,1)S(1)}, u32[]{:S(2)}, u32[]{:S(2)}) collective-permute-start(bf16[256,256]{1,0:T(8,128)(2,1)S(1)} %bitcast.31), channel_id=1, source_target_pairs={{0,16},{4,20},{8,24},{12,28},{16,0},{20,4},{24,8},{28,12},{1,17},{... | collective-permute-start | bytes 393224 | tf_op jit(solution)/shard_map/ppermute | solution.py:312
  100.6 7.3 %collective-permute-start.14 = (bf16[256,256]{1,0:T(8,128)(2,1)S(1)}, bf16[256,256]{1,0:T(8,128)(2,1)S(1)}, u32[]{:S(2)}, u32[]{:S(2)}) collective-permute-start(bf16[256,256]{1,0:T(8,128)(2,1)S(1)} %bitcast.32), channel_id=1, source_target_pairs={{0,16},{4,20},{8,24},{12,28},{16,0},{20,4},{24,8},{28,12},{1,17},{... | collective-permute-start | bytes 393224 | tf_op jit(solution)/shard_map/ppermute | solution.py:312
  102.6 8.2 %collective-permute-start.18 = (bf16[256,256]{1,0:T(8,128)(2,1)S(1)}, bf16[256,256]{1,0:T(8,128)(2,1)S(1)}, u32[]{:S(2)}, u32[]{:S(2)}) collective-permute-start(bf16[256,256]{1,0:T(8,128)(2,1)S(1)} %add_convert_fusion), channel_id=1, source_target_pairs={{0,0},{1,8},{2,2},{3,10},{4,4},{5,12},{6,6},{7,14},{8,1},{9,9},{10... | collective-permute-start | bytes 393224 | tf_op jit(solution)/shard_map/ppermute | solution.py:319

commit v5 on v4

--- a/solution.py
+++ b/solution.py
@@ -10,7 +10,7 @@
 
 SHARE = 4
 PIECES = 2
-FIRST = (1, 2)
+FIRST = (9, 16)
 VMEM_BYTES = 20 * 1024 * 1024
 COST = pl.CostEstimate(flops=1, bytes_accessed=1, transcendentals=0)
 WHOLE = pl.BlockSpec(memory_space=pltpu.VMEM)
@@ -51,6 +51,26 @@
         compiler_params=params(),
         cost_estimate=COST,
     )(mask, left)
+
+
+def share_kernel(start_ref, whole_ref, out_ref, sem):
+    size = out_ref.shape[0]
+    where = pl.ds(pl.multiple_of(start_ref[0], size), size)
+    copy = pltpu.make_async_copy(whole_ref.at[where], out_ref, sem)
+    copy.start()
+    copy.wait()
+
+
+def share_of(whole, start, size):
+    return pl.pallas_call(
+        share_kernel,
+        in_specs=[SCALARS, ANYWHERE],
+        out_specs=WHOLE,
+        out_shape=vmem((size, whole.shape[1]), whole.dtype),
+        scratch_shapes=[pltpu.SemaphoreType.DMA],
+        compiler_params=params(),
+        cost_estimate=COST,
+    )(start.astype(jnp.int32).reshape(1), pltpu.with_memory_space_constraint(whole, pltpu.HBM))
 
 
 def stack_kernel(*refs):
@@ -111,7 +131,7 @@
     shape, extra, scratch = [vmem((height, parts[0].shape[1]), kind)], [], [pltpu.VMEM((height, depth), kind)]
     if right is not None:
         shape.append(vmem(right.shape, kind))
-        extra = [half.astype(jnp.int32).reshape(1), right]
+        extra = [half, right]
         scratch.append(pltpu.SemaphoreType.DMA((2,)))
     return pl.pallas_call(
         functools.partial(inner_kernel, sizes, len(parts)),
@@ -136,69 +156,82 @@
             at += size
 
 
+def own_kernel(n_inner, *refs):
+    inner_refs, own_ref, outs = refs[:n_inner], refs[n_inner], refs[n_inner + 1 :]
+    products(inner_refs, own_ref[0], outs[:PIECES], 0)
+    products(inner_refs, own_ref[1], outs[PIECES:], 0)
+
+
 def give_kernel(n_inner, n_near, half_ref, *refs):
-    inner_refs, own_ref, near_refs = refs[:n_inner], refs[n_inner], refs[n_inner + 1 : n_inner + 1 + n_near]
-    outs, kept_refs = refs[n_inner + 1 + n_near :][:PIECES], refs[n_inner + 1 + n_near + PIECES : -2]
-    held_ref, sems = refs[-2:]
+    inner_refs, near_refs, refs = refs[:n_inner], refs[n_inner : n_inner + n_near], refs[n_inner + n_near :]
+    outs, kept_refs, (held_ref, sems) = refs[:PIECES], refs[PIECES:-2], refs[-2:]
     copies = []
     for k, targets in enumerate(([held_ref.at[j] for j in range(n_near)], kept_refs)):
         half = half_ref[0] if k == 0 else 1 - half_ref[0]
         for j, (ref, target) in enumerate(zip(near_refs, targets)):
             copies.append(pltpu.make_async_copy(ref.at[half], target, sems.at[k, j]))
             copies[-1].start()
-    products(inner_refs, own_ref[0], outs, 0)
     for j in range(n_near):
         copies[j].wait()
-        products(inner_refs, held_ref[j], outs, 1 + j)
+        products(inner_refs, held_ref[j], outs, j)
     for copy in copies[n_near:]:
         copy.wait()
 
 
-def give_of(inners, own, nears, half, sizes):
+def keep_kernel(n_inner, *refs):
+    inner_refs, near_refs, outs = refs[:n_inner], refs[n_inner:-PIECES], refs[-PIECES:]
+    for j, ref in enumerate(near_refs):
+        products(inner_refs, ref[...], outs, j)
+
+
+def outer_of(inners, own, nears, half, sizes):
     _, rows, depth = own.shape
+    n = len(nears)
+
+    def shapes(blocks, kind):
+        return [vmem((blocks, len(inners), size, rows), kind) for size in sizes]
+
     made = pl.pallas_call(
-        functools.partial(give_kernel, len(inners), len(nears)),
-        in_specs=[SCALARS] + [WHOLE] * (len(inners) + 1) + [ANYWHERE] * len(nears),
-        out_specs=[WHOLE] * (PIECES + len(nears)),
-        out_shape=[vmem((1 + len(nears), len(inners), size, rows), jnp.bfloat16) for size in sizes]
-        + [vmem((rows, depth), own.dtype)] * len(nears),
-        scratch_shapes=[
-            pltpu.VMEM((len(nears), rows, depth), own.dtype),
-            pltpu.SemaphoreType.DMA((2, len(nears))),
-        ],
-        compiler_params=params(),
-        cost_estimate=COST,
-    )(half.astype(jnp.int32).reshape(1), *held([*inners, own]), *nears)
-    return made[:PIECES], made[PIECES:]
-
-
-def keep_kernel(n_inner, *refs):
-    inner_refs, own_ref, rest = refs[:n_inner], refs[n_inner], refs[n_inner + 1 :]
-    near_refs, outs = rest[:-PIECES], rest[-PIECES:]
-    products(inner_refs, own_ref[1], outs, 0)
-    for j, ref in enumerate(near_refs):
-        products(inner_refs, ref[...], outs, 1 + j)
-
-
-def keep_of(inners, own, nears, sizes):
-    height = sum(a.shape[0] for a in inners)
-    _, rows, depth = own.shape
-    flops = 2 * height * (1 + len(nears)) * rows * depth
-    return pl.pallas_call(
+        functools.partial(own_kernel, len(inners)),
+        in_specs=[WHOLE] * (len(inners) + 1),
+        out_specs=[WHOLE] * (2 * PIECES),
+        out_shape=shapes(1, jnp.bfloat16) + shapes(1, jnp.float32),
+        compiler_params=params(),
+        cost_estimate=COST,
+    )(*held([*inners, own]))
+    give, keep = [list(made[:PIECES])], [list(made[PIECES:])]
+    made = pl.pallas_call(
+        functools.partial(give_kernel, len(inners), n),
+        in_specs=[SCALARS] + [WHOLE] * len(inners) + [ANYWHERE] * n,
+        out_specs=[WHOLE] * (PIECES + n),
+        out_shape=shapes(n, jnp.bfloat16) + [vmem((rows, depth), own.dtype)] * n,
+        scratch_shapes=[pltpu.VMEM((n, rows, depth), own.dtype), pltpu.SemaphoreType.DMA((2, n))],
+        compiler_params=params(),
+        cost_estimate=COST,
+    )(half, *held(inners), *after(nears, made))
+    give.append(list(made[:PIECES]))
+    flops = 2 * sum(sizes) * len(inners) * n * rows * depth
+    made = pl.pallas_call(
         functools.partial(keep_kernel, len(inners)),
-        in_specs=[WHOLE] * (len(inners) + 1 + len(nears)),
+        in_specs=[WHOLE] * (len(inners) + n),
         out_specs=[WHOLE] * PIECES,
-        out_shape=[vmem((1 + len(nears), len(inners), size, rows), jnp.float32) for size in sizes],
+        out_shape=shapes(n, jnp.float32),
         compiler_params=params(),
         cost_estimate=pl.CostEstimate(flops=flops, bytes_accessed=1, transcendentals=0),
-    )(*held([*inners, own, *nears]))
-
-
-def cores_kernel(index_ref, keep_ref, got_ref, kept_ref, sent_ref):
+    )(*held([*inners, *made[PIECES:]]))
+    keep.append(list(made))
+    return give, keep
+
+
+def cores_kernel(index_ref, *refs):
+    (own_ref, near_ref), (got_own_ref, got_near_ref), (kept_ref, sent_ref) = refs[:2], refs[2:4], refs[4:]
     for k in range(index_ref.shape[0]):
         block = index_ref[k]
         for j in range(kept_ref.shape[0]):
-            total = keep_ref[j, block] + got_ref[j, block]
+            if j == 0:
+                total = own_ref[0, block] + got_own_ref[0, block]
+            else:
+                total = near_ref[j - 1, block] + got_near_ref[j - 1, block]
             if k == 0:
                 kept_ref[j] = total
             else:
@@ -206,19 +239,19 @@
 
 
 def cores_summed(keep, got, index):
-    blocks, _, height, wide = keep.shape
+    near, _, height, wide = keep[1].shape
     others = index.shape[0] - 1
     return pl.pallas_call(
         cores_kernel,
-        in_specs=[SCALARS, WHOLE, WHOLE],
+        in_specs=[SCALARS] + [WHOLE] * 4,
         out_specs=[WHOLE, WHOLE],
         out_shape=[
-            vmem((blocks, height, wide), jnp.float32),
-            vmem((others, blocks, height, wide), jnp.bfloat16),
+            vmem((1 + near, height, wide), jnp.float32),
+            vmem((others, 1 + near, height, wide), jnp.bfloat16),
         ],
         compiler_params=params(),
         cost_estimate=COST,
-    )(index, *held([keep, got]))
+    )(index, *held([*keep, *got]))
 
 
 def chosen_kernel(index_ref, *refs):
@@ -321,22 +354,34 @@
     sharing = min(SHARE, max(1, height // 128))
     share = height // sharing
     mine = term % sharing
-    own_share = lax.dynamic_slice_in_dim(psi, mine * share, share, 0)
+    own_share = share_of(psi, mine * share, share)
     depth = n * height
+
+    near_x = [from_lo(own_share, j) for j in range(1, s)]
+    near_y = [from_hi(own_share, j) for j in range(1, s)]
+    own_share, term, row = lax.optimization_barrier((own_share, term, row))
+    core, z, mine = term % 2, term // 2, term % sharing
+    zh, zl, hi, lo = z // s, z % s, row // s, row % s
 
     def place(jy, jx, bits):
         return ((hi + jy) % s * s + (lo + jx) % s) * height + (mine ^ bits) * share
 
-    near_x = [from_lo(own_share, j) for j in range(1, s)]
-    near_y = [from_hi(own_share, j) for j in range(1, s)]
-    near_x, near_y, own_left = lax.optimization_barrier(
-        (near_x, near_y, masked_rows(left_ops[0], block_mask[0]))
+    def members(own, base):
+        return jnp.stack([(own + j - base) % s for j in range(s)]).astype(jnp.int32)
+
+    at_near = [(0, j) for j in range(1, s)] + [(j, 0) for j in range(1, s)]
+    at_far = [(jy, jx) for jy in range(1, s) for jx in range(1, s)]
+    held = [place(*at, bits) for bits in range(sharing) for at in at_near + at_far]
+    sizes = [height] + [share] * len(held)
+    places = jnp.stack([row * height] + held).astype(jnp.int32)
+    half = (1 - core).astype(jnp.int32).reshape(1)
+    counted = jnp.arange(s, dtype=jnp.int32)
+    near_x, near_y, own_left, places, half, by_zl, by_zh, counted = lax.optimization_barrier(
+        (near_x, near_y, masked_rows(left_ops[0], block_mask[0]), places, half, members(zl, lo), members(zh, hi), counted)
     )
     far = [from_hi(v, jy) for jy in range(1, s) for v in near_x]
-    at_near = [(0, j) for j in range(1, s)] + [(j, 0) for j in range(1, s)]
-    at_far = [(jy, jx) for jy in range(1, s) for jx in range(1, s)]
     near = jnp.concatenate(near_x + near_y, 0)
-    far = jnp.concatenate(far, 0)
+    far = stacked(far) if len(far) > 1 else far[0]
     first, last = [(at_near, 0, near), (at_far, 0, far)], []
     if sharing > 1:
         near_core = from_term(near, 1)
@@ -347,9 +392,6 @@
         last = [(at_near, 2, near_z), (at_far, 2, far_z)]
         last += [(at_near, 3, from_term(after(near_z, early), 1)), (at_far, 3, from_term(far_z, 1))]
     parts = [early] + [v for _, _, v in last]
-    held = [place(*at, bits) for group, bits, _ in first + last for at in group]
-    sizes = [height] + [share] * len(held)
-    places = jnp.stack([row * height] + held).astype(jnp.int32)
 
     near_left = [from_lo(own_left, j) for j in range(1, s)]
     own_right = after(right_ops[0], far if sharing == 1 else near_core)
@@ -359,26 +401,22 @@
     inners = list(inner_of(own_left, parts, sizes, places))
     for rows in near_left:
         rows = after(rows, inners[-1])
-        inner, own_halves = inner_of(rows, parts, sizes, places, rights[0], 1 - core)
+        inner, own_halves = inner_of(rows, parts, sizes, places, rights[0], half)
         inners.append(inner)
-
-    def members(own, base):
-        return jnp.stack([(own + j - base) % s for j in range(s)]).astype(jnp.int32)
 
     cut = height * FIRST[0] // FIRST[1] // 32 * 32
     row_sizes = [cut, height - cut]
-    give, near_halves = give_of(inners, own_halves, rights[1:], 1 - core, row_sizes)
-    got = [from_term(v, 1) for v in give]
-    keep = keep_of(inners, own_halves, near_halves, row_sizes)
+    give, keep = outer_of(inners, own_halves, rights[1:], half, row_sizes)
+    got = [[from_term(v, 1) for v in group] for group in give]
     outs = []
     for p in range(PIECES):
-        home_first = p % 2 == 0
-        index = jnp.arange(s, dtype=jnp.int32) if home_first else members(zl, lo)
-        kept, sent = cores_summed(keep[p], got[p], index)
+        home_first = p % 2 == 1
+        index = counted if home_first else by_zl
+        kept, sent = cores_summed([v[p] for v in keep], [v[p] for v in got], index)
         if home_first:
             held_blocks = [kept] + [from_lo(sent[s - j - 1], j) for j in range(1, s)]
-            kept, *sent = chosen_of(held_blocks, members(zl, lo))
-        final, sent = planes_summed(kept, [to_zl(sent[j - 1], j) for j in range(1, s)], members(zh, hi))
+            kept, *sent = chosen_of(held_blocks, by_zl)
+        final, sent = planes_summed(kept, [to_zl(sent[j - 1], j) for j in range(1, s)], by_zh)
         for j in range(1, s):
             final = final + to_zh(sent[j - 1], j).astype(jnp.float32)
         final = final.astype(jnp.bfloat16)

time: 113 us -> 113 us (level)
  waiting for transfers between devices: 54.5 us -> 65.8 us
  local copies, waits for them, and re-layouts: 8.34 us -> 2.56 us
  starting transfers between devices: 24.9 us -> 21.3 us
    unnamed x13, local copies, waits for them, and re-layouts: 7.13 us -> 1.39 us
    ppermute x3, waiting for transfers between devices: 13.9 us -> 18.2 us  [from_lo(): return lax.ppermute(value, 'row', pairs)]
    ppermute x2, waiting for transfers between devices: 0.06 us -> 4.32 us  [to_zh(): return lax.ppermute(value, 'term', pairs)]
    ppermute x1, starting transfers between devices: 5.24 us -> 2.09 us  [crossed(): return lax.ppermute(value, ('term', 'row'), pairs)]
    pallas_call x2, Pallas kernels: 13 us -> 10.5 us  [inner_of(): pl.pallas_call(functools.partial(inner_kernel, sizes, len(parts)), in_spe...]
    ppermute x8 -> x10, waiting for transfers between devices: 21.2 us -> 23.5 us  [from_term(): return lax.ppermute(value, 'term', [(a ^ bit, a) for a in range(terms)])]
    ppermute x1, waiting for transfers between devices: 2.84 us -> 4.68 us  [crossed(): return lax.ppermute(value, ('term', 'row'), pairs)]
    pallas_call x4 -> x6, Pallas kernels: 6.24 us -> 7.8 us  [the longest x1 2.4 us: outer_of(): pl.pallas_call(functools.partial(own_kernel, len(inners)), in_specs=[WHOL...]
  transfers between devices with their start and end apart: 19 -> 21, of which waited for: 13 -> 16; matrix products, arithmetic and copies ran while one was open for 0% -> 0% of each run, Pallas kernels for 18% -> 18%
where the time goes in v5:
time: 113 us; the launch traced here: 112 us
  waiting for transfers between devices  65.8 us (58%)
  Pallas kernels  21.8 us (19%)
  starting transfers between devices  21.3 us (19%)
  local copies, waits for them, and re-layouts  2.56 us (2%)
    ppermute x10, waiting for transfers between devices, from_term(): return lax.ppermute(value, 'term', [(a ^ bit, a) for a in range(terms)])  23.5 us
    ppermute x3, waiting for transfers between devices, from_lo(): return lax.ppermute(value, 'row', pairs)  18.2 us
    pallas_call x2, Pallas kernels, inner_of(): pl.pallas_call(functools.partial(inner_kernel, sizes, len(parts)), in_spe...  10.5 us
    ppermute x3, waiting for transfers between devices, from_hi(): return lax.ppermute(value, 'row', pairs)  10.1 us
    ppermute x2, waiting for transfers between devices, to_zl(): return lax.ppermute(value, 'term', pairs)  4.98 us
    ppermute x1, waiting for transfers between devices, crossed(): return lax.ppermute(value, ('term', 'row'), pairs)  4.68 us
    ppermute x2, waiting for transfers between devices, to_zh(): return lax.ppermute(value, 'term', pairs)  4.32 us
    ppermute x3, starting transfers between devices, from_hi(): return lax.ppermute(value, 'row', pairs)  4.31 us
  transfers between devices with their start and end apart: 21, of which 16 were waited for; matrix products, arithmetic and copies ran while one was open for 0% of the time, Pallas kernels for 18%

profile of v5, /device:TPU:2, one launch (start us, length us, event | category | flops | bytes accessed | tf_op | source)
XLA Modules:
  0.0 112.4 jit_solution(40088666421743985)
XLA Ops:
  0.0 1.2 %shard_map.46 = bf16[128,2048]{1,0:T(8,128)(2,1)S(1)} custom-call(s32[1]{0:T(128)} %bitcast.start_ref, bf16[512,2048]{1,0:T(8,128)(2,1)} %refs_0_.1), custom_call_target="tpu_custom_call" | custom-call | flops 1 | bytes 1 | tf_op jit(solution)/shard_map/pallas_call | solution.py:65
  1.2 0.1 collective-permute-start
  1.3 2.0 %collective-permute-start.1 = (bf16[128,2048]{1,0:T(8,128)(2,1)S(1)}, bf16[128,2048]{1,0:T(8,128)(2,1)}, u32[]{:S(2)}, u32[]{:S(2)}) collective-permute-start(bf16[128,2048]{1,0:T(8,128)(2,1)S(1)} %shard_map.46), channel_id=1, source_target_pairs={{2,0},{3,1},{0,2},{1,3},{6,4},{7,5},{4,6},{5,7},{10,8},{11,9},{8,1... | collective-permute-start | bytes 1572872 | tf_op jit(solution)/shard_map/ppermute | solution.py:328
  3.3 0.0 copy-done.5
  3.3 1.2 %shard_map.47.rows_ref = bf16[512,2048]{1,0:T(8,128)(2,1)S(1)} custom-call(s32[4,16]{1,0:T(4,128)S(1)} %bitcast.32, bf16[512,2048]{1,0:T(8,128)(2,1)S(1)} %bitcast.31), custom_call_target="tpu_custom_call" | custom-call | flops 1 | bytes 1 | tf_op jit(solution)/shard_map/pallas_call | solution.py:45
  4.6 1.3 %copy-done.1 = bf16[512,2048]{1,0:T(8,128)(2,1)} copy-done((bf16[512,2048]{1,0:T(8,128)(2,1)}, bf16[512,2048]{1,0:T(8,128)(2,1)S(1)}, u32[]{:S(2)}) %copy-start.1) | copy-done | bytes 2097176
  5.9 0.1 stack.73.place_ref
  6.0 0.1 pad_add_fusion
  6.1 8.9 %collective-permute-done = bf16[128,2048]{1,0:T(8,128)(2,1)S(1)} collective-permute-done((bf16[128,2048]{1,0:T(8,128)(2,1)S(1)}, bf16[128,2048]{1,0:T(8,128)(2,1)S(1)}, u32[]{:S(2)}, u32[]{:S(2)}) %collective-permute-start) | collective-permute-done | bytes 524320 | tf_op jit(solution)/shard_map/ppermute | solution.py:324
  14.9 0.2 collective-permute-done.1
  15.2 1.1 constant_dynamic-update-slice_fusion.refs_1_
  16.2 0.1 collective-permute-start.3
  16.3 1.8 %collective-permute-start.2 = (bf16[128,2048]{1,0:T(8,128)(2,1)S(1)}, bf16[128,2048]{1,0:T(8,128)(2,1)S(1)}, u32[]{:S(2)}, u32[]{:S(2)}) collective-permute-start(bf16[128,2048]{1,0:T(8,128)(2,1)S(1)} %collective-permute-done), channel_id=1, source_target_pairs={{2,0},{3,1},{0,2},{1,3},{6,4},{7,5},{4,6},{5,7},{10,8},{11,9},{8,1... | collective-permute-start | bytes 1572872 | tf_op jit(solution)/shard_map/ppermute | solution.py:328
  18.1 1.6 %collective-permute-start.5 = (bf16[256,2048]{1,0:T(8,128)(2,1)S(1)}, bf16[256,2048]{1,0:T(8,128)(2,1)S(1)}, u32[]{:S(2)}, u32[]{:S(2)}) collective-permute-start(bf16[256,2048]{1,0:T(8,128)(2,1)S(1)} %constant_dynamic-update-slice_fusion.refs_1_), channel_id=1, source_target_pairs={{8,0},{12,4},{0,8},{4,12},{24,16},{28,20},{16,24},{20,28},{9,1},{1... | collective-permute-start | bytes 3145736 | tf_op jit(solution)/shard_map/ppermute | solution.py:331
  19.7 1.5 %collective-permute-start.9 = (bf16[512,2048]{1,0:T(8,128)(2,1)}, bf16[512,2048]{1,0:T(8,128)(2,1)S(1)}, u32[]{:S(2)}, u32[]{:S(2)}) collective-permute-start(bf16[512,2048]{1,0:T(8,128)(2,1)} %copy-done.1), channel_id=1, source_target_pairs={{1,0},{0,1},{3,2},{2,3},{5,4},{4,5},{7,6},{6,7},{9,8},{8,9},{11,10... | collective-permute-start | bytes 6291464 | tf_op jit(solution)/shard_map/ppermute | solution.py:324
  21.2 0.0 collective-permute-done.3.refs_3_
  21.2 0.5 collective-permute-start.10
  21.7 9.4 %collective-permute-done.2.refs_2_ = bf16[128,2048]{1,0:T(8,128)(2,1)S(1)} collective-permute-done((bf16[128,2048]{1,0:T(8,128)(2,1)S(1)}, bf16[128,2048]{1,0:T(8,128)(2,1)S(1)}, u32[]{:S(2)}, u32[]{:S(2)}) %collective-permute-start.2) | collective-permute-done | bytes 524320 | tf_op jit(solution)/shard_map/ppermute | solution.py:328
  31.1 0.0 collective-permute-start.4
  31.1 1.8 %collective-permute-start.6 = (bf16[128,2048]{1,0:T(8,128)(2,1)S(1)}, bf16[128,2048]{1,0:T(8,128)(2,1)S(1)}, u32[]{:S(2)}, u32[]{:S(2)}) collective-permute-start(bf16[128,2048]{1,0:T(8,128)(2,1)S(1)} %collective-permute-done.2.refs_2_), channel_id=1, source_target_pairs={{8,0},{12,4},{0,8},{4,12},{24,16},{28,20},{16,24},{20,28},{9,1},{1... | collective-permute-start | bytes 1572872 | tf_op jit(solution)/shard_map/ppermute | solution.py:331
  32.9 0.2 collective-permute-done.4.refs_4_
  33.0 0.4 shard_map.48.refs_0_
  33.4 0.0 copy-start.3
  33.5 10.6 %collective-permute-done.5.refs_1_ = bf16[256,2048]{1,0:T(8,128)(2,1)S(1)} collective-permute-done((bf16[256,2048]{1,0:T(8,128)(2,1)S(1)}, bf16[256,2048]{1,0:T(8,128)(2,1)S(1)}, u32[]{:S(2)}, u32[]{:S(2)}) %collective-permute-start.5) | collective-permute-done | bytes 1048608 | tf_op jit(solution)/shard_map/ppermute | solution.py:331
  44.1 0.0 collective-permute-start.7
  44.1 10.5 %collective-permute-done.6.refs_2_ = bf16[128,2048]{1,0:T(8,128)(2,1)S(1)} collective-permute-done((bf16[128,2048]{1,0:T(8,128)(2,1)S(1)}, bf16[128,2048]{1,0:T(8,128)(2,1)S(1)}, u32[]{:S(2)}, u32[]{:S(2)}) %collective-permute-start.6) | collective-permute-done | bytes 524320 | tf_op jit(solution)/shard_map/ppermute | solution.py:331
  54.6 0.0 collective-permute-start.8
  54.6 1.9 %collective-permute-done.8.refs_4_ = bf16[128,2048]{1,0:T(8,128)(2,1)S(1)} collective-permute-done((bf16[128,2048]{1,0:T(8,128)(2,1)S(1)}, bf16[128,2048]{1,0:T(8,128)(2,1)S(1)}, u32[]{:S(2)}, u32[]{:S(2)}) %collective-permute-start.8) | collective-permute-done | bytes 524320 | tf_op jit(solution)/shard_map/ppermute | solution.py:331
  56.5 0.0 collective-permute-done.7.refs_3_
  56.5 0.0 copy-done.2
  56.5 5.2 %shard_map.49.refs_0_ = bf16[512,2048]{1,0:T(8,128)(2,1)S(1)} custom-call(s32[13]{0:T(128)S(1)} %stack.73.place_ref, bf16[512,2048]{1,0:T(8,128)(2,1)S(1)} %copy-done.2, bf16[1280,2048]{1,0:T(8,128)(2,1)S(1)} %shard_map.48.refs_0_, bf16[256,2048]{1,0:T(8,128)(2,1)S(1)} %collective-permute-done.5.refs_1_, ...), custom_call_target="tpu_custom_call" | custom-call | flops 1 | bytes 1 | tf_op jit(solution)/shard_map/pallas_call | solution.py:136
  61.7 5.6 %collective-permute-done.9.rows_ref = bf16[512,2048]{1,0:T(8,128)(2,1)S(1)} collective-permute-done((bf16[512,2048]{1,0:T(8,128)(2,1)}, bf16[512,2048]{1,0:T(8,128)(2,1)S(1)}, u32[]{:S(2)}, u32[]{:S(2)}) %collective-permute-start.9) | collective-permute-done | bytes 2097184 | tf_op jit(solution)/shard_map/ppermute | solution.py:324
  67.3 0.0 copy-done.3
  67.3 5.3 %shard_map.50 = (bf16[512,2048]{1,0:T(8,128)(2,1)S(1)}, bf16[2,256,2048]{2,1,0:T(8,128)(2,1)S(1)}) custom-call(s32[13]{0:T(128)S(1)} %stack.73.place_ref, bf16[512,2048]{1,0:T(8,128)(2,1)S(1)} %collective-permute-done.9.rows_ref, bf16[1280,2048]{1,0:T(8,128)(2,1)S(1)} %shard_map.48.refs_0_, bf16[256,2048]{1,0:T(8,128)(2,1)S(1)} %collective-permute-done.5.refs_1_, ...), custom_call_target="tpu_custom_call" | custom-call | flops 1 | bytes 1 | tf_op jit(solution)/shard_map/pallas_call | solution.py:136
  72.7 2.4 %shard_map.51 = (bf16[1,2,288,256]{3,2,1,0:T(8,128)(2,1)S(1)}, bf16[1,2,224,256]{3,2,1,0:T(8,128)(2,1)S(1)}, f32[1,2,288,256]{3,2,1,0:T(8,128)S(1)}, f32[1,2,224,256]{3,2,1,0:T(8,128)S(1)}) custom-call(bf16[512,2048]{1,0:T(8,128)(2,1)S(1)} %shard_map.49.refs_0_, bf16[512,2048]{1,0:T(8,128)(2,1)S(1)} %get-tuple-element.52.refs_1_, ...), custom_call_target="tpu_custom_call" | custom-call | flops 1 | bytes 1 | tf_op jit(solution)/shard_map/pallas_call | solution.py:194
  75.1 0.1 collective-permute-start.11
  75.1 0.5 collective-permute-done.10
  75.6 1.6 %shard_map.52 = (bf16[1,2,288,256]{3,2,1,0:T(8,128)(2,1)S(1)}, bf16[1,2,224,256]{3,2,1,0:T(8,128)(2,1)S(1)}, bf16[256,2048]{1,0:T(8,128)(2,1)S(1)}) custom-call(s32[1]{0:T(128)} %bitcast.16.refs_5_.half_ref, bf16[512,2048]{1,0:T(8,128)(2,1)S(1)} %shard_map.49.refs_0_, bf16[512,2048]{1,0:T(8,128)(2,1)S(1)} %get-tuple-element.52.refs_1_, ...), custom_call_target="tpu_custom_call" | custom-call | flops 1 | bytes 1 | tf_op jit(solution)/shard_map/pallas_call | solution.py:203
  77.3 0.1 collective-permute-start.12
  77.3 0.5 collective-permute-start.16
  77.8 0.1 collective-permute-start.17
  77.9 1.3 %shard_map.53 = (f32[1,2,288,256]{3,2,1,0:T(8,128)S(1)}, f32[1,2,224,256]{3,2,1,0:T(8,128)S(1)}) custom-call(bf16[512,2048]{1,0:T(8,128)(2,1)S(1)} %shard_map.49.refs_0_, bf16[512,2048]{1,0:T(8,128)(2,1)S(1)} %get-tuple-element.52.refs_1_, bf16[256,2048]{1,0:T(8,128)(2,1)S(1)} %get-tuple-element.59.refs_2_), custom_call_target="tpu_custom_call" | custom-call | flops 1073741824 | bytes 1 | tf_op jit(solution)/shard_map/pallas_call | solution.py:214
  79.2 0.0 collective-permute-done.16.refs_2_
  79.2 0.3 collective-permute-done.17.refs_3_
  79.6 0.6 shard_map.56
  80.2 1.7 %collective-permute-start.18 = (bf16[2,224,256]{2,1,0:T(8,128)(2,1)S(1)}, bf16[2,224,256]{2,1,0:T(8,128)(2,1)S(1)}, u32[]{:S(2)}, u32[]{:S(2)}) collective-permute-start(bf16[2,224,256]{2,1,0:T(8,128)(2,1)S(1)} %bitcast.34), channel_id=1, source_target_pairs={{1,0},{0,1},{3,2},{2,3},{5,4},{4,5},{7,6},{6,7},{9,8},{8,9},{11,10... | collective-permute-start | bytes 688136 | tf_op jit(solution)/shard_map/ppermute | solution.py:324
  81.9 0.0 collective-permute-done.11.refs_2_
  81.9 0.0 collective-permute-done.12.refs_3_
  81.9 0.6 shard_map.54
  82.6 1.6 %collective-permute-start.13 = (bf16[2,288,256]{2,1,0:T(8,128)(2,1)S(1)}, bf16[2,288,256]{2,1,0:T(8,128)(2,1)S(1)}, u32[]{:S(2)}, u32[]{:S(2)}) collective-permute-start(bf16[2,288,256]{2,1,0:T(8,128)(2,1)S(1)} %bitcast.33), channel_id=1, source_target_pairs={{0,8},{4,12},{8,0},{12,4},{16,24},{20,28},{24,16},{28,20},{1,9},{5... | collective-permute-start | bytes 884744 | tf_op jit(solution)/shard_map/ppermute | solution.py:338
  84.2 3.7 %collective-permute-done.18.refs_1_ = bf16[2,224,256]{2,1,0:T(8,128)(2,1)S(1)} collective-permute-done((bf16[2,224,256]{2,1,0:T(8,128)(2,1)S(1)}, bf16[2,224,256]{2,1,0:T(8,128)(2,1)S(1)}, u32[]{:S(2)}, u32[]{:S(2)}) %collective-permute-start.18) | collective-permute-done | bytes 229408 | tf_op jit(solution)/shard_map/ppermute | solution.py:324
  87.9 0.6 shard_map.57
  88.5 1.8 %collective-permute-start.19 = (bf16[2,224,256]{2,1,0:T(8,128)(2,1)S(1)}, bf16[2,224,256]{2,1,0:T(8,128)(2,1)S(1)}, u32[]{:S(2)}, u32[]{:S(2)}) collective-permute-start(bf16[2,224,256]{2,1,0:T(8,128)(2,1)S(1)} %get-tuple-element.72), channel_id=1, source_target_pairs={{0,8},{4,12},{8,0},{12,4},{16,24},{20,28},{24,16},{28,20},{1,9},{5... | collective-permute-start | bytes 688136 | tf_op jit(solution)/shard_map/ppermute | solution.py:338
  90.4 1.9 %collective-permute-done.13.refs_0_ = bf16[2,288,256]{2,1,0:T(8,128)(2,1)S(1)} collective-permute-done((bf16[2,288,256]{2,1,0:T(8,128)(2,1)S(1)}, bf16[2,288,256]{2,1,0:T(8,128)(2,1)S(1)}, u32[]{:S(2)}, u32[]{:S(2)}) %collective-permute-start.13) | collective-permute-done | bytes 294944 | tf_op jit(solution)/shard_map/ppermute | solution.py:338
  92.2 0.6 shard_map.55
  92.8 2.5 %collective-permute-start.14 = (bf16[288,256]{1,0:T(8,128)(2,1)S(1)}, bf16[288,256]{1,0:T(8,128)(2,1)S(1)}, u32[]{:S(2)}, u32[]{:S(2)}) collective-permute-start(bf16[288,256]{1,0:T(8,128)(2,1)S(1)} %bitcast.35), channel_id=1, source_target_pairs={{0,16},{4,20},{8,24},{12,28},{16,0},{20,4},{24,8},{28,12},{1,17},{... | collective-permute-start | bytes 442376 | tf_op jit(solution)/shard_map/ppermute | solution.py:345
  95.3 3.1 %collective-permute-done.19.refs_0_ = bf16[2,224,256]{2,1,0:T(8,128)(2,1)S(1)} collective-permute-done((bf16[2,224,256]{2,1,0:T(8,128)(2,1)S(1)}, bf16[2,224,256]{2,1,0:T(8,128)(2,1)S(1)}, u32[]{:S(2)}, u32[]{:S(2)}) %collective-permute-start.19) | collective-permute-done | bytes 229408 | tf_op jit(solution)/shard_map/ppermute | solution.py:338
  98.4 0.6 shard_map.58
  99.0 1.5 %collective-permute-start.20 = (bf16[224,256]{1,0:T(8,128)(2,1)S(1)}, bf16[224,256]{1,0:T(8,128)(2,1)S(1)}, u32[]{:S(2)}, u32[]{:S(2)}) collective-permute-start(bf16[224,256]{1,0:T(8,128)(2,1)S(1)} %bitcast.36), channel_id=1, source_target_pairs={{0,16},{4,20},{8,24},{12,28},{16,0},{20,4},{24,8},{28,12},{1,17},{... | collective-permute-start | bytes 344072 | tf_op jit(solution)/shard_map/ppermute | solution.py:345
  100.6 3.2 %collective-permute-done.14 = bf16[288,256]{1,0:T(8,128)(2,1)S(1)} collective-permute-done((bf16[288,256]{1,0:T(8,128)(2,1)S(1)}, bf16[288,256]{1,0:T(8,128)(2,1)S(1)}, u32[]{:S(2)}, u32[]{:S(2)}) %collective-permute-start.14) | collective-permute-done | bytes 147488 | tf_op jit(solution)/shard_map/ppermute | solution.py:345
  103.8 2.1 %collective-permute-start.15 = (bf16[288,256]{1,0:T(8,128)(2,1)S(1)}, bf16[288,256]{1,0:T(8,128)(2,1)S(1)}, u32[]{:S(2)}, u32[]{:S(2)}) collective-permute-start(bf16[288,256]{1,0:T(8,128)(2,1)S(1)} %add_convert_fusion), channel_id=1, source_target_pairs={{0,0},{1,8},{2,2},{3,10},{4,4},{5,12},{6,6},{7,14},{8,1},{9,9},{10... | collective-permute-start | bytes 442376 | tf_op jit(solution)/shard_map/ppermute | solution.py:352
  105.9 1.1 %collective-permute-done.20 = bf16[224,256]{1,0:T(8,128)(2,1)S(1)} collective-permute-done((bf16[224,256]{1,0:T(8,128)(2,1)S(1)}, bf16[224,256]{1,0:T(8,128)(2,1)S(1)}, u32[]{:S(2)}, u32[]{:S(2)}) %collective-permute-start.20) | collective-permute-done | bytes 114720 | tf_op jit(solution)/shard_map/ppermute | solution.py:345
  107.0 4.7 %collective-permute-done.15 = bf16[288,256]{1,0:T(8,128)(2,1)S(1)} collective-permute-done((bf16[288,256]{1,0:T(8,128)(2,1)S(1)}, bf16[288,256]{1,0:T(8,128)(2,1)S(1)}, u32[]{:S(2)}, u32[]{:S(2)}) %collective-permute-start.15) | collective-permute-done | bytes 147488 | tf_op jit(solution)/shard_map/ppermute | solution.py:352
  111.7 0.7 pad_maximum_fusion
  (11 shorter events, 0.1 us)
Async XLA Ops:
  0.0 3.3 %copy-start.5 = (s32[1,4,16]{2,1,0:T(4,128)S(1)}, s32[1,4,16]{2,1,0:T(4,128)}, u32[]{:S(2)}) copy-start(s32[1,4,16]{2,1,0:T(4,128)} %param.7) | copy-start | bytes 772
  0.0 3.3 %copy-start.4 = (bf16[1,512,2048]{2,1,0:T(8,128)(2,1)S(1)}, bf16[1,512,2048]{2,1,0:T(8,128)(2,1)}, u32[]{:S(2)}) copy-start(bf16[1,512,2048]{2,1,0:T(8,128)(2,1)} %param.5) | copy-start | bytes 6291460
  1.2 13.7 %collective-permute-start = (bf16[128,2048]{1,0:T(8,128)(2,1)S(1)}, bf16[128,2048]{1,0:T(8,128)(2,1)S(1)}, u32[]{:S(2)}, u32[]{:S(2)}) collective-permute-start(bf16[128,2048]{1,0:T(8,128)(2,1)S(1)} %shard_map.46), channel_id=1, source_target_pairs={{1,0},{0,1},{3,2},{2,3},{5,4},{4,5},{7,6},{6,7},{9,8},{8,9},{11,10... | collective-permute-start | bytes 1572872 | tf_op jit(solution)/shard_map/ppermute | solution.py:324
  1.3 13.8 %collective-permute-start.1 = (bf16[128,2048]{1,0:T(8,128)(2,1)S(1)}, bf16[128,2048]{1,0:T(8,128)(2,1)}, u32[]{:S(2)}, u32[]{:S(2)}) collective-permute-start(bf16[128,2048]{1,0:T(8,128)(2,1)S(1)} %shard_map.46), channel_id=1, source_target_pairs={{2,0},{3,1},{0,2},{1,3},{6,4},{7,5},{4,6},{5,7},{10,8},{11,9},{8,1... | collective-permute-start | bytes 1572872 | tf_op jit(solution)/shard_map/ppermute | solution.py:328
  4.6 1.3 %copy-start.1 = (bf16[512,2048]{1,0:T(8,128)(2,1)}, bf16[512,2048]{1,0:T(8,128)(2,1)S(1)}, u32[]{:S(2)}) copy-start(bf16[512,2048]{1,0:T(8,128)(2,1)S(1)} %shard_map.47.rows_ref) | copy-start | bytes 6291460
  5.9 27.1 %copy-start = (bf16[512,2048]{1,0:T(8,128)(2,1)S(1)}, bf16[512,2048]{1,0:T(8,128)(2,1)}, u32[]{:S(2)}) copy-start(bf16[512,2048]{1,0:T(8,128)(2,1)} %refs_0_.1) | copy-start | bytes 6291460
  16.2 4.9 %collective-permute-start.3 = (bf16[256,2048]{1,0:T(8,128)(2,1)S(1)}, bf16[256,2048]{1,0:T(8,128)(2,1)S(1)}, u32[]{:S(2)}, u32[]{:S(2)}) collective-permute-start(bf16[256,2048]{1,0:T(8,128)(2,1)S(1)} %constant_dynamic-update-slice_fusion.refs_1_), channel_id=1, source_target_pairs={{4,0},{0,4},{12,8},{8,12},{20,16},{16,20},{28,24},{24,28},{5,1},{1... | collective-permute-start | bytes 3145736 | tf_op jit(solution)/shard_map/ppermute | solution.py:331
  16.3 14.8 %collective-permute-start.2 = (bf16[128,2048]{1,0:T(8,128)(2,1)S(1)}, bf16[128,2048]{1,0:T(8,128)(2,1)S(1)}, u32[]{:S(2)}, u32[]{:S(2)}) collective-permute-start(bf16[128,2048]{1,0:T(8,128)(2,1)S(1)} %collective-permute-done), channel_id=1, source_target_pairs={{2,0},{3,1},{0,2},{1,3},{6,4},{7,5},{4,6},{5,7},{10,8},{11,9},{8,1... | collective-permute-start | bytes 1572872 | tf_op jit(solution)/shard_map/ppermute | solution.py:328
  18.1 26.0 %collective-permute-start.5 = (bf16[256,2048]{1,0:T(8,128)(2,1)S(1)}, bf16[256,2048]{1,0:T(8,128)(2,1)S(1)}, u32[]{:S(2)}, u32[]{:S(2)}) collective-permute-start(bf16[256,2048]{1,0:T(8,128)(2,1)S(1)} %constant_dynamic-update-slice_fusion.refs_1_), channel_id=1, source_target_pairs={{8,0},{12,4},{0,8},{4,12},{24,16},{28,20},{16,24},{20,28},{9,1},{1... | collective-permute-start | bytes 3145736 | tf_op jit(solution)/shard_map/ppermute | solution.py:331
  19.7 47.6 %collective-permute-start.9 = (bf16[512,2048]{1,0:T(8,128)(2,1)}, bf16[512,2048]{1,0:T(8,128)(2,1)S(1)}, u32[]{:S(2)}, u32[]{:S(2)}) collective-permute-start(bf16[512,2048]{1,0:T(8,128)(2,1)} %copy-done.1), channel_id=1, source_target_pairs={{1,0},{0,1},{3,2},{2,3},{5,4},{4,5},{7,6},{6,7},{9,8},{8,9},{11,10... | collective-permute-start | bytes 6291464 | tf_op jit(solution)/shard_map/ppermute | solution.py:324
  21.2 35.3 %copy-start.2 = (bf16[512,2048]{1,0:T(8,128)(2,1)S(1)}, bf16[512,2048]{1,0:T(8,128)(2,1)}, u32[]{:S(2)}) copy-start(bf16[512,2048]{1,0:T(8,128)(2,1)} %copy-done.1) | copy-start | bytes 6291460
  21.2 54.4 %collective-permute-start.10 = (bf16[512,2048]{1,0:T(8,128)(2,1)}, bf16[512,2048]{1,0:T(8,128)(2,1)S(1)}, u32[]{:S(2)}, u32[]{:S(2)}) collective-permute-start(bf16[512,2048]{1,0:T(8,128)(2,1)} %bitcast.28), channel_id=1, source_target_pairs={{2,0},{3,1},{0,2},{1,3},{6,4},{7,5},{4,6},{5,7},{10,8},{11,9},{8,1... | collective-permute-start | bytes 6291464 | tf_op jit(solution)/shard_map/ppermute | solution.py:328
  31.1 1.9 %collective-permute-start.4 = (bf16[128,2048]{1,0:T(8,128)(2,1)S(1)}, bf16[128,2048]{1,0:T(8,128)(2,1)S(1)}, u32[]{:S(2)}, u32[]{:S(2)}) collective-permute-start(bf16[128,2048]{1,0:T(8,128)(2,1)S(1)} %collective-permute-done.2.refs_2_), channel_id=1, source_target_pairs={{4,0},{0,4},{12,8},{8,12},{20,16},{16,20},{28,24},{24,28},{5,1},{1... | collective-permute-start | bytes 1572872 | tf_op jit(solution)/shard_map/ppermute | solution.py:331
  31.1 23.4 %collective-permute-start.6 = (bf16[128,2048]{1,0:T(8,128)(2,1)S(1)}, bf16[128,2048]{1,0:T(8,128)(2,1)S(1)}, u32[]{:S(2)}, u32[]{:S(2)}) collective-permute-start(bf16[128,2048]{1,0:T(8,128)(2,1)S(1)} %collective-permute-done.2.refs_2_), channel_id=1, source_target_pairs={{8,0},{12,4},{0,8},{4,12},{24,16},{28,20},{16,24},{20,28},{9,1},{1... | collective-permute-start | bytes 1572872 | tf_op jit(solution)/shard_map/ppermute | solution.py:331
  33.4 33.9 %copy-start.3 = (bf16[1,512,2048]{2,1,0:T(8,128)(2,1)S(1)}, bf16[1,512,2048]{2,1,0:T(8,128)(2,1)}, u32[]{:S(2)}) copy-start(bf16[1,512,2048]{2,1,0:T(8,128)(2,1)} %param.6) | copy-start | bytes 6291460
  44.1 12.4 %collective-permute-start.7 = (bf16[256,2048]{1,0:T(8,128)(2,1)S(1)}, bf16[256,2048]{1,0:T(8,128)(2,1)S(1)}, u32[]{:S(2)}, u32[]{:S(2)}) collective-permute-start(bf16[256,2048]{1,0:T(8,128)(2,1)S(1)} %collective-permute-done.5.refs_1_), channel_id=1, source_target_pairs={{4,0},{0,4},{12,8},{8,12},{20,16},{16,20},{28,24},{24,28},{5,1},{1... | collective-permute-start | bytes 3145736 | tf_op jit(solution)/shard_map/ppermute | solution.py:331
  54.6 1.9 %collective-permute-start.8 = (bf16[128,2048]{1,0:T(8,128)(2,1)S(1)}, bf16[128,2048]{1,0:T(8,128)(2,1)S(1)}, u32[]{:S(2)}, u32[]{:S(2)}) collective-permute-start(bf16[128,2048]{1,0:T(8,128)(2,1)S(1)} %collective-permute-done.6.refs_2_), channel_id=1, source_target_pairs={{4,0},{0,4},{12,8},{8,12},{20,16},{16,20},{28,24},{24,28},{5,1},{1... | collective-permute-start | bytes 1572872 | tf_op jit(solution)/shard_map/ppermute | solution.py:331
  75.1 6.9 %collective-permute-start.11 = (bf16[1,2,288,256]{3,2,1,0:T(8,128)(2,1)S(1)}, bf16[1,2,288,256]{3,2,1,0:T(8,128)(2,1)S(1)}, u32[]{:S(2)}, u32[]{:S(2)}) collective-permute-start(bf16[1,2,288,256]{3,2,1,0:T(8,128)(2,1)S(1)} %get-tuple-element.55), channel_id=1, source_target_pairs={{4,0},{0,4},{12,8},{8,12},{20,16},{16,20},{28,24},{24,28},{5,1},{1... | collective-permute-start | bytes 884744 | tf_op jit(solution)/shard_map/ppermute | solution.py:331
  77.3 4.7 %collective-permute-start.12 = (bf16[1,2,288,256]{3,2,1,0:T(8,128)(2,1)S(1)}, bf16[1,2,288,256]{3,2,1,0:T(8,128)(2,1)S(1)}, u32[]{:S(2)}, u32[]{:S(2)}) collective-permute-start(bf16[1,2,288,256]{3,2,1,0:T(8,128)(2,1)S(1)} %get-tuple-element.61), channel_id=1, source_target_pairs={{4,0},{0,4},{12,8},{8,12},{20,16},{16,20},{28,24},{24,28},{5,1},{1... | collective-permute-start | bytes 884744 | tf_op jit(solution)/shard_map/ppermute | solution.py:331
  77.3 1.9 %collective-permute-start.16 = (bf16[1,2,224,256]{3,2,1,0:T(8,128)(2,1)S(1)}, bf16[1,2,224,256]{3,2,1,0:T(8,128)(2,1)S(1)}, u32[]{:S(2)}, u32[]{:S(2)}) collective-permute-start(bf16[1,2,224,256]{3,2,1,0:T(8,128)(2,1)S(1)} %get-tuple-element.56), channel_id=1, source_target_pairs={{4,0},{0,4},{12,8},{8,12},{20,16},{16,20},{28,24},{24,28},{5,1},{1... | collective-permute-start | bytes 688136 | tf_op jit(solution)/shard_map/ppermute | solution.py:331
  77.8 1.7 %collective-permute-start.17 = (bf16[1,2,224,256]{3,2,1,0:T(8,128)(2,1)S(1)}, bf16[1,2,224,256]{3,2,1,0:T(8,128)(2,1)S(1)}, u32[]{:S(2)}, u32[]{:S(2)}) collective-permute-start(bf16[1,2,224,256]{3,2,1,0:T(8,128)(2,1)S(1)} %get-tuple-element.68), channel_id=1, source_target_pairs={{4,0},{0,4},{12,8},{8,12},{20,16},{16,20},{28,24},{24,28},{5,1},{1... | collective-permute-start | bytes 688136 | tf_op jit(solution)/shard_map/ppermute | solution.py:331
  80.2 7.7 %collective-permute-start.18 = (bf16[2,224,256]{2,1,0:T(8,128)(2,1)S(1)}, bf16[2,224,256]{2,1,0:T(8,128)(2,1)S(1)}, u32[]{:S(2)}, u32[]{:S(2)}) collective-permute-start(bf16[2,224,256]{2,1,0:T(8,128)(2,1)S(1)} %bitcast.34), channel_id=1, source_target_pairs={{1,0},{0,1},{3,2},{2,3},{5,4},{4,5},{7,6},{6,7},{9,8},{8,9},{11,10... | collective-permute-start | bytes 688136 | tf_op jit(solution)/shard_map/ppermute | solution.py:324
  82.6 9.7 %collective-permute-start.13 = (bf16[2,288,256]{2,1,0:T(8,128)(2,1)S(1)}, bf16[2,288,256]{2,1,0:T(8,128)(2,1)S(1)}, u32[]{:S(2)}, u32[]{:S(2)}) collective-permute-start(bf16[2,288,256]{2,1,0:T(8,128)(2,1)S(1)} %bitcast.33), channel_id=1, source_target_pairs={{0,8},{4,12},{8,0},{12,4},{16,24},{20,28},{24,16},{28,20},{1,9},{5... | collective-permute-start | bytes 884744 | tf_op jit(solution)/shard_map/ppermute | solution.py:338
  88.5 9.9 %collective-permute-start.19 = (bf16[2,224,256]{2,1,0:T(8,128)(2,1)S(1)}, bf16[2,224,256]{2,1,0:T(8,128)(2,1)S(1)}, u32[]{:S(2)}, u32[]{:S(2)}) collective-permute-start(bf16[2,224,256]{2,1,0:T(8,128)(2,1)S(1)} %get-tuple-element.72), channel_id=1, source_target_pairs={{0,8},{4,12},{8,0},{12,4},{16,24},{20,28},{24,16},{28,20},{1,9},{5... | collective-permute-start | bytes 688136 | tf_op jit(solution)/shard_map/ppermute | solution.py:338
  92.8 10.9 %collective-permute-start.14 = (bf16[288,256]{1,0:T(8,128)(2,1)S(1)}, bf16[288,256]{1,0:T(8,128)(2,1)S(1)}, u32[]{:S(2)}, u32[]{:S(2)}) collective-permute-start(bf16[288,256]{1,0:T(8,128)(2,1)S(1)} %bitcast.35), channel_id=1, source_target_pairs={{0,16},{4,20},{8,24},{12,28},{16,0},{20,4},{24,8},{28,12},{1,17},{... | collective-permute-start | bytes 442376 | tf_op jit(solution)/shard_map/ppermute | solution.py:345
  99.0 8.0 %collective-permute-start.20 = (bf16[224,256]{1,0:T(8,128)(2,1)S(1)}, bf16[224,256]{1,0:T(8,128)(2,1)S(1)}, u32[]{:S(2)}, u32[]{:S(2)}) collective-permute-start(bf16[224,256]{1,0:T(8,128)(2,1)S(1)} %bitcast.36), channel_id=1, source_target_pairs={{0,16},{4,20},{8,24},{12,28},{16,0},{20,4},{24,8},{28,12},{1,17},{... | collective-permute-start | bytes 344072 | tf_op jit(solution)/shard_map/ppermute | solution.py:345
  103.8 7.9 %collective-permute-start.15 = (bf16[288,256]{1,0:T(8,128)(2,1)S(1)}, bf16[288,256]{1,0:T(8,128)(2,1)S(1)}, u32[]{:S(2)}, u32[]{:S(2)}) collective-permute-start(bf16[288,256]{1,0:T(8,128)(2,1)S(1)} %add_convert_fusion), channel_id=1, source_target_pairs={{0,0},{1,8},{2,2},{3,10},{4,4},{5,12},{6,6},{7,14},{8,1},{9,9},{10... | collective-permute-start | bytes 442376 | tf_op jit(solution)/shard_map/ppermute | solution.py:352

commit v6 on v5

--- a/solution.py
+++ b/solution.py
@@ -162,31 +162,14 @@
     products(inner_refs, own_ref[1], outs[PIECES:], 0)
 
 
-def give_kernel(n_inner, n_near, half_ref, *refs):
-    inner_refs, near_refs, refs = refs[:n_inner], refs[n_inner : n_inner + n_near], refs[n_inner + n_near :]
-    outs, kept_refs, (held_ref, sems) = refs[:PIECES], refs[PIECES:-2], refs[-2:]
-    copies = []
-    for k, targets in enumerate(([held_ref.at[j] for j in range(n_near)], kept_refs)):
-        half = half_ref[0] if k == 0 else 1 - half_ref[0]
-        for j, (ref, target) in enumerate(zip(near_refs, targets)):
-            copies.append(pltpu.make_async_copy(ref.at[half], target, sems.at[k, j]))
-            copies[-1].start()
-    for j in range(n_near):
-        copies[j].wait()
-        products(inner_refs, held_ref[j], outs, j)
-    for copy in copies[n_near:]:
-        copy.wait()
-
-
 def keep_kernel(n_inner, *refs):
     inner_refs, near_refs, outs = refs[:n_inner], refs[n_inner:-PIECES], refs[-PIECES:]
     for j, ref in enumerate(near_refs):
         products(inner_refs, ref[...], outs, j)
 
 
-def outer_of(inners, own, nears, half, sizes):
+def outer_of(inners, own, gives, keeps, sizes):
     _, rows, depth = own.shape
-    n = len(nears)
 
     def shapes(blocks, kind):
         return [vmem((blocks, len(inners), size, rows), kind) for size in sizes]
@@ -200,26 +183,16 @@
         cost_estimate=COST,
     )(*held([*inners, own]))
     give, keep = [list(made[:PIECES])], [list(made[PIECES:])]
-    made = pl.pallas_call(
-        functools.partial(give_kernel, len(inners), n),
-        in_specs=[SCALARS] + [WHOLE] * len(inners) + [ANYWHERE] * n,
-        out_specs=[WHOLE] * (PIECES + n),
-        out_shape=shapes(n, jnp.bfloat16) + [vmem((rows, depth), own.dtype)] * n,
-        scratch_shapes=[pltpu.VMEM((n, rows, depth), own.dtype), pltpu.SemaphoreType.DMA((2, n))],
-        compiler_params=params(),
-        cost_estimate=COST,
-    )(half, *held(inners), *after(nears, made))
-    give.append(list(made[:PIECES]))
-    flops = 2 * sum(sizes) * len(inners) * n * rows * depth
-    made = pl.pallas_call(
-        functools.partial(keep_kernel, len(inners)),
-        in_specs=[WHOLE] * (len(inners) + n),
-        out_specs=[WHOLE] * PIECES,
-        out_shape=shapes(n, jnp.float32),
-        compiler_params=params(),
-        cost_estimate=pl.CostEstimate(flops=flops, bytes_accessed=1, transcendentals=0),
-    )(*held([*inners, *made[PIECES:]]))
-    keep.append(list(made))
+    for nears, kind, into in ((gives, jnp.bfloat16, give), (keeps, jnp.float32, keep)):
+        made = pl.pallas_call(
+            functools.partial(keep_kernel, len(inners)),
+            in_specs=[WHOLE] * (len(inners) + len(nears)),
+            out_specs=[WHOLE] * PIECES,
+            out_shape=shapes(len(nears), kind),
+            compiler_params=params(),
+            cost_estimate=COST,
+        )(*held([*inners, *after(nears, made)]))
+        into.append(list(made))
     return give, keep
 
 
@@ -376,8 +349,10 @@
     places = jnp.stack([row * height] + held).astype(jnp.int32)
     half = (1 - core).astype(jnp.int32).reshape(1)
     counted = jnp.arange(s, dtype=jnp.int32)
-    near_x, near_y, own_left, places, half, by_zl, by_zh, counted = lax.optimization_barrier(
-        (near_x, near_y, masked_rows(left_ops[0], block_mask[0]), places, half, members(zl, lo), members(zh, hi), counted)
+    halves = right_ops[0].reshape(2, height // 2, width)
+    own_give, own_keep = [lax.dynamic_index_in_dim(halves, k, 0, keepdims=False) for k in (1 - core, core)]
+    near_x, near_y, own_left, own_give, own_keep, places, half, by_zl, by_zh, counted = lax.optimization_barrier(
+        (near_x, near_y, masked_rows(left_ops[0], block_mask[0]), own_give, own_keep, places, half, members(zl, lo), members(zh, hi), counted)
     )
     far = [from_hi(v, jy) for jy in range(1, s) for v in near_x]
     near = jnp.concatenate(near_x + near_y, 0)
@@ -387,26 +362,24 @@
         near_core = from_term(near, 1)
         first += [(at_near, 1, near_core), (at_far, 1, from_term(far, 1))]
     early = stacked([psi] + [v for _, _, v in first])
+    gives = [from_hi(after(own_give, near), j) for j in range(1, s)]
+    keeps = [from_hi(after(own_keep, gives), j) for j in range(1, s)]
     if sharing > 2:
         near_z, far_z = from_term(near, 2), from_term(far, 2)
         last = [(at_near, 2, near_z), (at_far, 2, far_z)]
-        last += [(at_near, 3, from_term(after(near_z, early), 1)), (at_far, 3, from_term(far_z, 1))]
+        last += [(at_near, 3, from_term(after(near_z, (early, gives)), 1)), (at_far, 3, from_term(far_z, 1))]
     parts = [early] + [v for _, _, v in last]
 
     near_left = [from_lo(own_left, j) for j in range(1, s)]
-    own_right = after(right_ops[0], far if sharing == 1 else near_core)
-    rights = [own_right] + [from_hi(own_right, j) for j in range(1, s)]
-    rights = [a.reshape(2, height // 2, width) for a in rights]
-
     inners = list(inner_of(own_left, parts, sizes, places))
     for rows in near_left:
         rows = after(rows, inners[-1])
-        inner, own_halves = inner_of(rows, parts, sizes, places, rights[0], half)
+        inner, own_halves = inner_of(rows, parts, sizes, places, halves, half)
         inners.append(inner)
 
     cut = height * FIRST[0] // FIRST[1] // 32 * 32
     row_sizes = [cut, height - cut]
-    give, keep = outer_of(inners, own_halves, rights[1:], half, row_sizes)
+    give, keep = outer_of(inners, own_halves, gives, keeps, row_sizes)
     got = [[from_term(v, 1) for v in group] for group in give]
     outs = []
     for p in range(PIECES):

time: 113 us -> 111 us (0.982)
  starting transfers between devices: 21.3 us -> 19.1 us
    ppermute x3 -> x4, waiting for transfers between devices: 10.1 us -> 34.4 us  [from_hi(): return lax.ppermute(value, 'row', pairs)]
    ppermute x10, waiting for transfers between devices: 23.5 us -> 8.26 us  [from_term(): return lax.ppermute(value, 'term', [(a ^ bit, a) for a in range(terms)])]
    ppermute x3, waiting for transfers between devices: 18.2 us -> 12.5 us  [from_lo(): return lax.ppermute(value, 'row', pairs)]
    ppermute x2, waiting for transfers between devices: 4.32 us -> 1.19 us  [to_zh(): return lax.ppermute(value, 'term', pairs)]
    ppermute x2, starting transfers between devices: 3.46 us -> 1.05 us  [to_zl(): return lax.ppermute(value, 'term', pairs)]
    ppermute x1, starting transfers between devices: 2.09 us -> 4.04 us  [crossed(): return lax.ppermute(value, ('term', 'row'), pairs)]
    pallas_call x1 -> x0, Pallas kernels: 1.64 us -> none  [outer_of(): pl.pallas_call(functools.partial(give_kernel, len(inners), n), in_specs=[...]
    ppermute x3, starting transfers between devices: 3.29 us -> 1.67 us  [from_lo(): return lax.ppermute(value, 'row', pairs)]
  transfers between devices with their start and end apart: 21 -> 22, of which waited for: 16 -> 14; matrix products, arithmetic and copies ran while one was open for 0% -> 1% of each run, Pallas kernels for 18% -> 18%
where the time goes in v6:
time: 111 us
  waiting for transfers between devices  66.6 us (60%)
  Pallas kernels  21.7 us (20%)
  starting transfers between devices  19.1 us (17%)
  local copies, waits for them, and re-layouts  2.78 us (3%)
    ppermute x4, waiting for transfers between devices, from_hi(): return lax.ppermute(value, 'row', pairs)  34.4 us
    ppermute x3, waiting for transfers between devices, from_lo(): return lax.ppermute(value, 'row', pairs)  12.5 us
    pallas_call x2, Pallas kernels, inner_of(): pl.pallas_call(functools.partial(inner_kernel, sizes, len(parts)), in_spe...  10.7 us
    ppermute x10, waiting for transfers between devices, from_term(): return lax.ppermute(value, 'term', [(a ^ bit, a) for a in range(terms)])  8.26 us
    ppermute x2, waiting for transfers between devices, to_zl(): return lax.ppermute(value, 'term', pairs)  6.24 us
    ppermute x10, starting transfers between devices, from_term(): return lax.ppermute(value, 'term', [(a ^ bit, a) for a in range(terms)])  4.31 us
    ppermute x4, starting transfers between devices, from_hi(): return lax.ppermute(value, 'row', pairs)  4.28 us
    ppermute x1, starting transfers between devices, crossed(): return lax.ppermute(value, ('term', 'row'), pairs)  4.04 us
  transfers between devices with their start and end apart: 22, of which 14 were waited for; matrix products, arithmetic and copies ran while one was open for 1% of the time, Pallas kernels for 18%

profile of v6, /device:TPU:2, one launch (start us, length us, event | category | flops | bytes accessed | tf_op | source)
XLA Modules:
  0.0 111.1 jit_solution(752432143130917897)
XLA Ops:
  0.0 1.2 %shard_map.46 = bf16[128,2048]{1,0:T(8,128)(2,1)S(1)} custom-call(s32[1]{0:T(128)} %bitcast.start_ref, bf16[512,2048]{1,0:T(8,128)(2,1)} %refs_0_.1), custom_call_target="tpu_custom_call" | custom-call | flops 1 | bytes 1 | tf_op jit(solution)/shard_map/pallas_call | solution.py:65
  1.2 1.6 %collective-permute-start.1 = (bf16[128,2048]{1,0:T(8,128)(2,1)S(1)}, bf16[128,2048]{1,0:T(8,128)(2,1)}, u32[]{:S(2)}, u32[]{:S(2)}) collective-permute-start(bf16[128,2048]{1,0:T(8,128)(2,1)S(1)} %shard_map.46), channel_id=1, source_target_pairs={{2,0},{3,1},{0,2},{1,3},{6,4},{7,5},{4,6},{5,7},{10,8},{11,9},{8,1... | collective-permute-start | bytes 1572872 | tf_op jit(solution)/shard_map/ppermute | solution.py:301
  2.8 0.5 collective-permute-start
  3.3 1.3 %shard_map.47.rows_ref = bf16[512,2048]{1,0:T(8,128)(2,1)S(1)} custom-call(s32[4,16]{1,0:T(4,128)S(1)} %bitcast.33, bf16[512,2048]{1,0:T(8,128)(2,1)S(1)} %bitcast.32), custom_call_target="tpu_custom_call" | custom-call | flops 1 | bytes 1 | tf_op jit(solution)/shard_map/pallas_call | solution.py:45
  4.6 1.4 %copy-done.2 = bf16[512,2048]{1,0:T(8,128)(2,1)} copy-done((bf16[512,2048]{1,0:T(8,128)(2,1)}, bf16[512,2048]{1,0:T(8,128)(2,1)S(1)}, u32[]{:S(2)}) %copy-start.2) | copy-done | bytes 2097176
  6.0 0.1 stack.73.place_ref
  6.1 0.1 pad_add_fusion
  6.1 0.2 dynamic-slice_bitcast_fusion
  6.3 0.0 copy-start.1
  6.3 8.7 %collective-permute-done.1 = bf16[128,2048]{1,0:T(8,128)(2,1)} collective-permute-done((bf16[128,2048]{1,0:T(8,128)(2,1)S(1)}, bf16[128,2048]{1,0:T(8,128)(2,1)}, u32[]{:S(2)}, u32[]{:S(2)}) %collective-permute-start.1) | collective-permute-done | bytes 524320 | tf_op jit(solution)/shard_map/ppermute | solution.py:301
  15.0 1.1 %collective-permute-done = bf16[128,2048]{1,0:T(8,128)(2,1)S(1)} collective-permute-done((bf16[128,2048]{1,0:T(8,128)(2,1)S(1)}, bf16[128,2048]{1,0:T(8,128)(2,1)S(1)}, u32[]{:S(2)}, u32[]{:S(2)}) %collective-permute-start) | collective-permute-done | bytes 524320 | tf_op jit(solution)/shard_map/ppermute | solution.py:297
  16.2 0.5 collective-permute-start.2
  16.7 1.1 constant_dynamic-update-slice_fusion.refs_1_
  17.8 0.1 collective-permute-start.3
  17.9 1.6 %collective-permute-start.7 = (bf16[256,2048]{1,0:T(8,128)(2,1)S(1)}, bf16[256,2048]{1,0:T(8,128)(2,1)S(1)}, u32[]{:S(2)}, u32[]{:S(2)}) collective-permute-start(bf16[256,2048]{1,0:T(8,128)(2,1)S(1)} %get-tuple-element.52), channel_id=1, source_target_pairs={{2,0},{3,1},{0,2},{1,3},{6,4},{7,5},{4,6},{5,7},{10,8},{11,9},{8,1... | collective-permute-start | bytes 3145736 | tf_op jit(solution)/shard_map/ppermute | solution.py:301
  19.5 1.6 %collective-permute-start.5 = (bf16[256,2048]{1,0:T(8,128)(2,1)S(1)}, bf16[256,2048]{1,0:T(8,128)(2,1)S(1)}, u32[]{:S(2)}, u32[]{:S(2)}) collective-permute-start(bf16[256,2048]{1,0:T(8,128)(2,1)S(1)} %constant_dynamic-update-slice_fusion.refs_1_), channel_id=1, source_target_pairs={{8,0},{12,4},{0,8},{4,12},{24,16},{28,20},{16,24},{20,28},{9,1},{1... | collective-permute-start | bytes 3145736 | tf_op jit(solution)/shard_map/ppermute | solution.py:304
  21.1 0.5 collective-permute-start.10
  21.6 9.4 %collective-permute-done.2.refs_2_ = bf16[128,2048]{1,0:T(8,128)(2,1)S(1)} collective-permute-done((bf16[128,2048]{1,0:T(8,128)(2,1)S(1)}, bf16[128,2048]{1,0:T(8,128)(2,1)S(1)}, u32[]{:S(2)}, u32[]{:S(2)}) %collective-permute-start.2) | collective-permute-done | bytes 524320 | tf_op jit(solution)/shard_map/ppermute | solution.py:301
  31.0 0.0 collective-permute-start.4
  31.0 1.9 %collective-permute-done.4.refs_4_ = bf16[128,2048]{1,0:T(8,128)(2,1)S(1)} collective-permute-done((bf16[128,2048]{1,0:T(8,128)(2,1)S(1)}, bf16[128,2048]{1,0:T(8,128)(2,1)S(1)}, u32[]{:S(2)}, u32[]{:S(2)}) %collective-permute-start.4) | collective-permute-done | bytes 524320 | tf_op jit(solution)/shard_map/ppermute | solution.py:304
  33.0 1.6 %collective-permute-start.6 = (bf16[128,2048]{1,0:T(8,128)(2,1)S(1)}, bf16[128,2048]{1,0:T(8,128)(2,1)S(1)}, u32[]{:S(2)}, u32[]{:S(2)}) collective-permute-start(bf16[128,2048]{1,0:T(8,128)(2,1)S(1)} %collective-permute-done.2.refs_2_), channel_id=1, source_target_pairs={{8,0},{12,4},{0,8},{4,12},{24,16},{28,20},{16,24},{20,28},{9,1},{1... | collective-permute-start | bytes 1572872 | tf_op jit(solution)/shard_map/ppermute | solution.py:304
  34.5 0.0 collective-permute-done.3.refs_3_
  34.5 0.4 shard_map.48.refs_0_
  35.0 16.3 %collective-permute-done.7.refs_2_ = bf16[256,2048]{1,0:T(8,128)(2,1)S(1)} collective-permute-done((bf16[256,2048]{1,0:T(8,128)(2,1)S(1)}, bf16[256,2048]{1,0:T(8,128)(2,1)S(1)}, u32[]{:S(2)}, u32[]{:S(2)}) %collective-permute-start.7) | collective-permute-done | bytes 1048608 | tf_op jit(solution)/shard_map/ppermute | solution.py:301
  51.2 0.0 collective-permute-done.5.refs_1_
  51.2 0.0 collective-permute-start.8
  51.2 0.6 collective-permute-start.11
  51.8 4.1 %collective-permute-done.6.refs_2_ = bf16[128,2048]{1,0:T(8,128)(2,1)S(1)} collective-permute-done((bf16[128,2048]{1,0:T(8,128)(2,1)S(1)}, bf16[128,2048]{1,0:T(8,128)(2,1)S(1)}, u32[]{:S(2)}, u32[]{:S(2)}) %collective-permute-start.6) | collective-permute-done | bytes 524320 | tf_op jit(solution)/shard_map/ppermute | solution.py:304
  55.9 0.0 collective-permute-start.9
  56.0 1.9 %collective-permute-done.9.refs_4_ = bf16[128,2048]{1,0:T(8,128)(2,1)S(1)} collective-permute-done((bf16[128,2048]{1,0:T(8,128)(2,1)S(1)}, bf16[128,2048]{1,0:T(8,128)(2,1)S(1)}, u32[]{:S(2)}, u32[]{:S(2)}) %collective-permute-start.9) | collective-permute-done | bytes 524320 | tf_op jit(solution)/shard_map/ppermute | solution.py:304
  57.9 0.0 collective-permute-done.8.refs_3_
  57.9 5.2 %shard_map.49.refs_0_ = bf16[512,2048]{1,0:T(8,128)(2,1)S(1)} custom-call(s32[13]{0:T(128)S(1)} %stack.73.place_ref, bf16[512,2048]{1,0:T(8,128)(2,1)S(1)} %copy-done.3, bf16[1280,2048]{1,0:T(8,128)(2,1)S(1)} %shard_map.48.refs_0_, bf16[256,2048]{1,0:T(8,128)(2,1)S(1)} %collective-permute-done.5.refs_1_, ...), custom_call_target="tpu_custom_call" | custom-call | flops 1 | bytes 1 | tf_op jit(solution)/shard_map/pallas_call | solution.py:136
  63.0 5.4 %collective-permute-done.10.rows_ref = bf16[512,2048]{1,0:T(8,128)(2,1)S(1)} collective-permute-done((bf16[512,2048]{1,0:T(8,128)(2,1)S(1)}, bf16[512,2048]{1,0:T(8,128)(2,1)S(1)}, u32[]{:S(2)}, u32[]{:S(2)}) %collective-permute-start.10) | collective-permute-done | bytes 2097184 | tf_op jit(solution)/shard_map/ppermute | solution.py:297
  68.5 5.5 %shard_map.50 = (bf16[512,2048]{1,0:T(8,128)(2,1)S(1)}, bf16[2,256,2048]{2,1,0:T(8,128)(2,1)S(1)}) custom-call(s32[13]{0:T(128)S(1)} %stack.73.place_ref, bf16[512,2048]{1,0:T(8,128)(2,1)S(1)} %collective-permute-done.10.rows_ref, bf16[1280,2048]{1,0:T(8,128)(2,1)S(1)} %shard_map.48.refs_0_, bf16[256,2048]{1,0:T(8,128)(2,1)S(1)} %collective-permute-done.5.refs_1_, ...), custom_call_target="tpu_custom_call" | custom-call | flops 1 | bytes 1 | tf_op jit(solution)/shard_map/pallas_call | solution.py:136
  74.0 2.4 %shard_map.51 = (bf16[1,2,288,256]{3,2,1,0:T(8,128)(2,1)S(1)}, bf16[1,2,224,256]{3,2,1,0:T(8,128)(2,1)S(1)}, f32[1,2,288,256]{3,2,1,0:T(8,128)S(1)}, f32[1,2,224,256]{3,2,1,0:T(8,128)S(1)}) custom-call(bf16[512,2048]{1,0:T(8,128)(2,1)S(1)} %shard_map.49.refs_0_, bf16[512,2048]{1,0:T(8,128)(2,1)S(1)} %get-tuple-element.56.refs_1_, ...), custom_call_target="tpu_custom_call" | custom-call | flops 1 | bytes 1 | tf_op jit(solution)/shard_map/pallas_call | solution.py:177
  76.4 1.3 %shard_map.52 = (bf16[1,2,288,256]{3,2,1,0:T(8,128)(2,1)S(1)}, bf16[1,2,224,256]{3,2,1,0:T(8,128)(2,1)S(1)}) custom-call(bf16[512,2048]{1,0:T(8,128)(2,1)S(1)} %shard_map.49.refs_0_, bf16[512,2048]{1,0:T(8,128)(2,1)S(1)} %get-tuple-element.56.refs_1_, bf16[256,2048]{1,0:T(8,128)(2,1)S(1)} %collective-permute-done.7.refs_2_), custom_call_target="tpu_custom_call" | custom-call | flops 1 | bytes 1 | tf_op jit(solution)/shard_map/pallas_call | solution.py:187
  77.7 0.1 collective-permute-start.13
  77.8 0.5 collective-permute-start.12
  78.3 0.1 collective-permute-start.18
  78.4 0.4 collective-permute-start.17
  78.8 0.0 collective-permute-done.11.refs_2_
  78.8 1.3 %shard_map.53 = (f32[1,2,288,256]{3,2,1,0:T(8,128)S(1)}, f32[1,2,224,256]{3,2,1,0:T(8,128)S(1)}) custom-call(bf16[512,2048]{1,0:T(8,128)(2,1)S(1)} %shard_map.49.refs_0_, bf16[512,2048]{1,0:T(8,128)(2,1)S(1)} %get-tuple-element.56.refs_1_, bf16[256,2048]{1,0:T(8,128)(2,1)S(1)} %collective-permute-done.11.refs_2_), custom_call_target="tpu_custom_call" | custom-call | flops 1 | bytes 1 | tf_op jit(solution)/shard_map/pallas_call | solution.py:187
  80.1 0.0 collective-permute-done.18.refs_3_
  80.1 0.3 collective-permute-done.17.refs_2_
  80.4 0.7 shard_map.56
  81.1 0.6 collective-permute-start.19
  81.7 0.0 collective-permute-done.13.refs_3_
  81.7 0.0 collective-permute-done.12.refs_2_
  81.7 0.7 shard_map.54
  82.4 0.5 collective-permute-start.14
  82.9 5.9 %collective-permute-done.19.refs_1_ = bf16[2,224,256]{2,1,0:T(8,128)(2,1)S(1)} collective-permute-done((bf16[2,224,256]{2,1,0:T(8,128)(2,1)S(1)}, bf16[2,224,256]{2,1,0:T(8,128)(2,1)S(1)}, u32[]{:S(2)}, u32[]{:S(2)}) %collective-permute-start.19) | collective-permute-done | bytes 229408 | tf_op jit(solution)/shard_map/ppermute | solution.py:297
  88.8 0.6 shard_map.57
  89.4 0.5 collective-permute-start.20
  90.0 1.2 %collective-permute-done.14.refs_0_ = bf16[2,288,256]{2,1,0:T(8,128)(2,1)S(1)} collective-permute-done((bf16[2,288,256]{2,1,0:T(8,128)(2,1)S(1)}, bf16[2,288,256]{2,1,0:T(8,128)(2,1)S(1)}, u32[]{:S(2)}, u32[]{:S(2)}) %collective-permute-start.14) | collective-permute-done | bytes 294944 | tf_op jit(solution)/shard_map/ppermute | solution.py:311
  91.2 0.6 shard_map.55
  91.8 2.7 %collective-permute-start.15 = (bf16[288,256]{1,0:T(8,128)(2,1)S(1)}, bf16[288,256]{1,0:T(8,128)(2,1)S(1)}, u32[]{:S(2)}, u32[]{:S(2)}) collective-permute-start(bf16[288,256]{1,0:T(8,128)(2,1)S(1)} %bitcast.36), channel_id=1, source_target_pairs={{0,16},{4,20},{8,24},{12,28},{16,0},{20,4},{24,8},{28,12},{1,17},{... | collective-permute-start | bytes 442376 | tf_op jit(solution)/shard_map/ppermute | solution.py:318
  94.5 5.0 %collective-permute-done.20.refs_0_ = bf16[2,224,256]{2,1,0:T(8,128)(2,1)S(1)} collective-permute-done((bf16[2,224,256]{2,1,0:T(8,128)(2,1)S(1)}, bf16[2,224,256]{2,1,0:T(8,128)(2,1)S(1)}, u32[]{:S(2)}, u32[]{:S(2)}) %collective-permute-start.20) | collective-permute-done | bytes 229408 | tf_op jit(solution)/shard_map/ppermute | solution.py:311
  99.5 0.6 shard_map.58
  100.1 1.1 collective-permute-start.21
  101.1 0.0 collective-permute-done.15
  101.2 4.0 %collective-permute-start.16 = (bf16[288,256]{1,0:T(8,128)(2,1)S(1)}, bf16[288,256]{1,0:T(8,128)(2,1)S(1)}, u32[]{:S(2)}, u32[]{:S(2)}) collective-permute-start(bf16[288,256]{1,0:T(8,128)(2,1)S(1)} %add_convert_fusion), channel_id=1, source_target_pairs={{0,0},{1,8},{2,2},{3,10},{4,4},{5,12},{6,6},{7,14},{8,1},{9,9},{10... | collective-permute-start | bytes 442376 | tf_op jit(solution)/shard_map/ppermute | solution.py:325
  105.2 1.2 %collective-permute-done.21 = bf16[224,256]{1,0:T(8,128)(2,1)S(1)} collective-permute-done((bf16[224,256]{1,0:T(8,128)(2,1)S(1)}, bf16[224,256]{1,0:T(8,128)(2,1)S(1)}, u32[]{:S(2)}, u32[]{:S(2)}) %collective-permute-start.21) | collective-permute-done | bytes 114720 | tf_op jit(solution)/shard_map/ppermute | solution.py:318
  106.4 4.0 %collective-permute-done.16 = bf16[288,256]{1,0:T(8,128)(2,1)S(1)} collective-permute-done((bf16[288,256]{1,0:T(8,128)(2,1)S(1)}, bf16[288,256]{1,0:T(8,128)(2,1)S(1)}, u32[]{:S(2)}, u32[]{:S(2)}) %collective-permute-start.16) | collective-permute-done | bytes 147488 | tf_op jit(solution)/shard_map/ppermute | solution.py:325
  110.4 0.7 pad_maximum_fusion
  (14 shorter events, 0.1 us)
Async XLA Ops:
  0.0 3.3 %copy-start.5 = (s32[1,4,16]{2,1,0:T(4,128)S(1)}, s32[1,4,16]{2,1,0:T(4,128)}, u32[]{:S(2)}) copy-start(s32[1,4,16]{2,1,0:T(4,128)} %param.7) | copy-start | bytes 772
  0.0 3.3 %copy-start.4 = (bf16[1,512,2048]{2,1,0:T(8,128)(2,1)S(1)}, bf16[1,512,2048]{2,1,0:T(8,128)(2,1)}, u32[]{:S(2)}) copy-start(bf16[1,512,2048]{2,1,0:T(8,128)(2,1)} %param.5) | copy-start | bytes 6291460
  1.2 13.8 %collective-permute-start.1 = (bf16[128,2048]{1,0:T(8,128)(2,1)S(1)}, bf16[128,2048]{1,0:T(8,128)(2,1)}, u32[]{:S(2)}, u32[]{:S(2)}) collective-permute-start(bf16[128,2048]{1,0:T(8,128)(2,1)S(1)} %shard_map.46), channel_id=1, source_target_pairs={{2,0},{3,1},{0,2},{1,3},{6,4},{7,5},{4,6},{5,7},{10,8},{11,9},{8,1... | collective-permute-start | bytes 1572872 | tf_op jit(solution)/shard_map/ppermute | solution.py:301
  2.8 13.4 %collective-permute-start = (bf16[128,2048]{1,0:T(8,128)(2,1)S(1)}, bf16[128,2048]{1,0:T(8,128)(2,1)S(1)}, u32[]{:S(2)}, u32[]{:S(2)}) collective-permute-start(bf16[128,2048]{1,0:T(8,128)(2,1)S(1)} %shard_map.46), channel_id=1, source_target_pairs={{1,0},{0,1},{3,2},{2,3},{5,4},{4,5},{7,6},{6,7},{9,8},{8,9},{11,10... | collective-permute-start | bytes 1572872 | tf_op jit(solution)/shard_map/ppermute | solution.py:297
  3.3 2.8 %copy-start = (bf16[1,512,2048]{2,1,0:T(8,128)(2,1)S(1)}, bf16[1,512,2048]{2,1,0:T(8,128)(2,1)}, u32[]{:S(2)}) copy-start(bf16[1,512,2048]{2,1,0:T(8,128)(2,1)} %param.6) | copy-start | bytes 6291460
  4.6 1.4 %copy-start.2 = (bf16[512,2048]{1,0:T(8,128)(2,1)}, bf16[512,2048]{1,0:T(8,128)(2,1)S(1)}, u32[]{:S(2)}) copy-start(bf16[512,2048]{1,0:T(8,128)(2,1)S(1)} %shard_map.47.rows_ref) | copy-start | bytes 6291460
  6.1 14.9 %copy-start.3 = (bf16[512,2048]{1,0:T(8,128)(2,1)S(1)}, bf16[512,2048]{1,0:T(8,128)(2,1)}, u32[]{:S(2)}) copy-start(bf16[512,2048]{1,0:T(8,128)(2,1)} %copy-done.2) | copy-start | bytes 6291460
  6.3 28.2 %copy-start.1 = (bf16[512,2048]{1,0:T(8,128)(2,1)S(1)}, bf16[512,2048]{1,0:T(8,128)(2,1)}, u32[]{:S(2)}) copy-start(bf16[512,2048]{1,0:T(8,128)(2,1)} %refs_0_.1) | copy-start | bytes 6291460
  16.2 14.9 %collective-permute-start.2 = (bf16[128,2048]{1,0:T(8,128)(2,1)S(1)}, bf16[128,2048]{1,0:T(8,128)(2,1)S(1)}, u32[]{:S(2)}, u32[]{:S(2)}) collective-permute-start(bf16[128,2048]{1,0:T(8,128)(2,1)S(1)} %collective-permute-done), channel_id=1, source_target_pairs={{2,0},{3,1},{0,2},{1,3},{6,4},{7,5},{4,6},{5,7},{10,8},{11,9},{8,1... | collective-permute-start | bytes 1572872 | tf_op jit(solution)/shard_map/ppermute | solution.py:301
  17.8 16.7 %collective-permute-start.3 = (bf16[256,2048]{1,0:T(8,128)(2,1)S(1)}, bf16[256,2048]{1,0:T(8,128)(2,1)S(1)}, u32[]{:S(2)}, u32[]{:S(2)}) collective-permute-start(bf16[256,2048]{1,0:T(8,128)(2,1)S(1)} %constant_dynamic-update-slice_fusion.refs_1_), channel_id=1, source_target_pairs={{4,0},{0,4},{12,8},{8,12},{20,16},{16,20},{28,24},{24,28},{5,1},{1... | collective-permute-start | bytes 3145736 | tf_op jit(solution)/shard_map/ppermute | solution.py:304
  17.9 33.3 %collective-permute-start.7 = (bf16[256,2048]{1,0:T(8,128)(2,1)S(1)}, bf16[256,2048]{1,0:T(8,128)(2,1)S(1)}, u32[]{:S(2)}, u32[]{:S(2)}) collective-permute-start(bf16[256,2048]{1,0:T(8,128)(2,1)S(1)} %get-tuple-element.52), channel_id=1, source_target_pairs={{2,0},{3,1},{0,2},{1,3},{6,4},{7,5},{4,6},{5,7},{10,8},{11,9},{8,1... | collective-permute-start | bytes 3145736 | tf_op jit(solution)/shard_map/ppermute | solution.py:301
  19.5 31.8 %collective-permute-start.5 = (bf16[256,2048]{1,0:T(8,128)(2,1)S(1)}, bf16[256,2048]{1,0:T(8,128)(2,1)S(1)}, u32[]{:S(2)}, u32[]{:S(2)}) collective-permute-start(bf16[256,2048]{1,0:T(8,128)(2,1)S(1)} %constant_dynamic-update-slice_fusion.refs_1_), channel_id=1, source_target_pairs={{8,0},{12,4},{0,8},{4,12},{24,16},{28,20},{16,24},{20,28},{9,1},{1... | collective-permute-start | bytes 3145736 | tf_op jit(solution)/shard_map/ppermute | solution.py:304
  21.1 47.4 %collective-permute-start.10 = (bf16[512,2048]{1,0:T(8,128)(2,1)S(1)}, bf16[512,2048]{1,0:T(8,128)(2,1)S(1)}, u32[]{:S(2)}, u32[]{:S(2)}) collective-permute-start(bf16[512,2048]{1,0:T(8,128)(2,1)S(1)} %copy-done.3), channel_id=1, source_target_pairs={{1,0},{0,1},{3,2},{2,3},{5,4},{4,5},{7,6},{6,7},{9,8},{8,9},{11,10... | collective-permute-start | bytes 6291464 | tf_op jit(solution)/shard_map/ppermute | solution.py:297
  31.0 1.9 %collective-permute-start.4 = (bf16[128,2048]{1,0:T(8,128)(2,1)S(1)}, bf16[128,2048]{1,0:T(8,128)(2,1)S(1)}, u32[]{:S(2)}, u32[]{:S(2)}) collective-permute-start(bf16[128,2048]{1,0:T(8,128)(2,1)S(1)} %collective-permute-done.2.refs_2_), channel_id=1, source_target_pairs={{4,0},{0,4},{12,8},{8,12},{20,16},{16,20},{28,24},{24,28},{5,1},{1... | collective-permute-start | bytes 1572872 | tf_op jit(solution)/shard_map/ppermute | solution.py:304
  33.0 23.0 %collective-permute-start.6 = (bf16[128,2048]{1,0:T(8,128)(2,1)S(1)}, bf16[128,2048]{1,0:T(8,128)(2,1)S(1)}, u32[]{:S(2)}, u32[]{:S(2)}) collective-permute-start(bf16[128,2048]{1,0:T(8,128)(2,1)S(1)} %collective-permute-done.2.refs_2_), channel_id=1, source_target_pairs={{8,0},{12,4},{0,8},{4,12},{24,16},{28,20},{16,24},{20,28},{9,1},{1... | collective-permute-start | bytes 1572872 | tf_op jit(solution)/shard_map/ppermute | solution.py:304
  51.2 6.6 %collective-permute-start.8 = (bf16[256,2048]{1,0:T(8,128)(2,1)S(1)}, bf16[256,2048]{1,0:T(8,128)(2,1)S(1)}, u32[]{:S(2)}, u32[]{:S(2)}) collective-permute-start(bf16[256,2048]{1,0:T(8,128)(2,1)S(1)} %collective-permute-done.5.refs_1_), channel_id=1, source_target_pairs={{4,0},{0,4},{12,8},{8,12},{20,16},{16,20},{28,24},{24,28},{5,1},{1... | collective-permute-start | bytes 3145736 | tf_op jit(solution)/shard_map/ppermute | solution.py:304
  51.2 27.5 %collective-permute-start.11 = (bf16[256,2048]{1,0:T(8,128)(2,1)S(1)}, bf16[256,2048]{1,0:T(8,128)(2,1)S(1)}, u32[]{:S(2)}, u32[]{:S(2)}) collective-permute-start(bf16[256,2048]{1,0:T(8,128)(2,1)S(1)} %get-tuple-element.60), channel_id=1, source_target_pairs={{2,0},{3,1},{0,2},{1,3},{6,4},{7,5},{4,6},{5,7},{10,8},{11,9},{8,1... | collective-permute-start | bytes 3145736 | tf_op jit(solution)/shard_map/ppermute | solution.py:301
  55.9 1.9 %collective-permute-start.9 = (bf16[128,2048]{1,0:T(8,128)(2,1)S(1)}, bf16[128,2048]{1,0:T(8,128)(2,1)S(1)}, u32[]{:S(2)}, u32[]{:S(2)}) collective-permute-start(bf16[128,2048]{1,0:T(8,128)(2,1)S(1)} %collective-permute-done.6.refs_2_), channel_id=1, source_target_pairs={{4,0},{0,4},{12,8},{8,12},{20,16},{16,20},{28,24},{24,28},{5,1},{1... | collective-permute-start | bytes 1572872 | tf_op jit(solution)/shard_map/ppermute | solution.py:304
  77.7 4.0 %collective-permute-start.13 = (bf16[1,2,288,256]{3,2,1,0:T(8,128)(2,1)S(1)}, bf16[1,2,288,256]{3,2,1,0:T(8,128)(2,1)S(1)}, u32[]{:S(2)}, u32[]{:S(2)}) collective-permute-start(bf16[1,2,288,256]{3,2,1,0:T(8,128)(2,1)S(1)} %get-tuple-element.65), channel_id=1, source_target_pairs={{4,0},{0,4},{12,8},{8,12},{20,16},{16,20},{28,24},{24,28},{5,1},{1... | collective-permute-start | bytes 884744 | tf_op jit(solution)/shard_map/ppermute | solution.py:304
  77.8 3.9 %collective-permute-start.12 = (bf16[1,2,288,256]{3,2,1,0:T(8,128)(2,1)S(1)}, bf16[1,2,288,256]{3,2,1,0:T(8,128)(2,1)S(1)}, u32[]{:S(2)}, u32[]{:S(2)}) collective-permute-start(bf16[1,2,288,256]{3,2,1,0:T(8,128)(2,1)S(1)} %get-tuple-element.61), channel_id=1, source_target_pairs={{4,0},{0,4},{12,8},{8,12},{20,16},{16,20},{28,24},{24,28},{5,1},{1... | collective-permute-start | bytes 884744 | tf_op jit(solution)/shard_map/ppermute | solution.py:304
  78.3 1.8 %collective-permute-start.18 = (bf16[1,2,224,256]{3,2,1,0:T(8,128)(2,1)S(1)}, bf16[1,2,224,256]{3,2,1,0:T(8,128)(2,1)S(1)}, u32[]{:S(2)}, u32[]{:S(2)}) collective-permute-start(bf16[1,2,224,256]{3,2,1,0:T(8,128)(2,1)S(1)} %get-tuple-element.66), channel_id=1, source_target_pairs={{4,0},{0,4},{12,8},{8,12},{20,16},{16,20},{28,24},{24,28},{5,1},{1... | collective-permute-start | bytes 688136 | tf_op jit(solution)/shard_map/ppermute | solution.py:304
  78.4 2.1 %collective-permute-start.17 = (bf16[1,2,224,256]{3,2,1,0:T(8,128)(2,1)S(1)}, bf16[1,2,224,256]{3,2,1,0:T(8,128)(2,1)S(1)}, u32[]{:S(2)}, u32[]{:S(2)}) collective-permute-start(bf16[1,2,224,256]{3,2,1,0:T(8,128)(2,1)S(1)} %get-tuple-element.62), channel_id=1, source_target_pairs={{4,0},{0,4},{12,8},{8,12},{20,16},{16,20},{28,24},{24,28},{5,1},{1... | collective-permute-start | bytes 688136 | tf_op jit(solution)/shard_map/ppermute | solution.py:304
  81.1 7.7 %collective-permute-start.19 = (bf16[2,224,256]{2,1,0:T(8,128)(2,1)S(1)}, bf16[2,224,256]{2,1,0:T(8,128)(2,1)S(1)}, u32[]{:S(2)}, u32[]{:S(2)}) collective-permute-start(bf16[2,224,256]{2,1,0:T(8,128)(2,1)S(1)} %bitcast.35), channel_id=1, source_target_pairs={{1,0},{0,1},{3,2},{2,3},{5,4},{4,5},{7,6},{6,7},{9,8},{8,9},{11,10... | collective-permute-start | bytes 688136 | tf_op jit(solution)/shard_map/ppermute | solution.py:297
  82.4 8.8 %collective-permute-start.14 = (bf16[2,288,256]{2,1,0:T(8,128)(2,1)S(1)}, bf16[2,288,256]{2,1,0:T(8,128)(2,1)S(1)}, u32[]{:S(2)}, u32[]{:S(2)}) collective-permute-start(bf16[2,288,256]{2,1,0:T(8,128)(2,1)S(1)} %bitcast.34), channel_id=1, source_target_pairs={{0,8},{4,12},{8,0},{12,4},{16,24},{20,28},{24,16},{28,20},{1,9},{5... | collective-permute-start | bytes 884744 | tf_op jit(solution)/shard_map/ppermute | solution.py:311
  89.4 10.0 %collective-permute-start.20 = (bf16[2,224,256]{2,1,0:T(8,128)(2,1)S(1)}, bf16[2,224,256]{2,1,0:T(8,128)(2,1)S(1)}, u32[]{:S(2)}, u32[]{:S(2)}) collective-permute-start(bf16[2,224,256]{2,1,0:T(8,128)(2,1)S(1)} %get-tuple-element.78), channel_id=1, source_target_pairs={{0,8},{4,12},{8,0},{12,4},{16,24},{20,28},{24,16},{28,20},{1,9},{5... | collective-permute-start | bytes 688136 | tf_op jit(solution)/shard_map/ppermute | solution.py:311
  91.8 9.3 %collective-permute-start.15 = (bf16[288,256]{1,0:T(8,128)(2,1)S(1)}, bf16[288,256]{1,0:T(8,128)(2,1)S(1)}, u32[]{:S(2)}, u32[]{:S(2)}) collective-permute-start(bf16[288,256]{1,0:T(8,128)(2,1)S(1)} %bitcast.36), channel_id=1, source_target_pairs={{0,16},{4,20},{8,24},{12,28},{16,0},{20,4},{24,8},{28,12},{1,17},{... | collective-permute-start | bytes 442376 | tf_op jit(solution)/shard_map/ppermute | solution.py:318
  100.1 6.3 %collective-permute-start.21 = (bf16[224,256]{1,0:T(8,128)(2,1)S(1)}, bf16[224,256]{1,0:T(8,128)(2,1)S(1)}, u32[]{:S(2)}, u32[]{:S(2)}) collective-permute-start(bf16[224,256]{1,0:T(8,128)(2,1)S(1)} %bitcast.37), channel_id=1, source_target_pairs={{0,16},{4,20},{8,24},{12,28},{16,0},{20,4},{24,8},{28,12},{1,17},{... | collective-permute-start | bytes 344072 | tf_op jit(solution)/shard_map/ppermute | solution.py:318
  101.2 9.2 %collective-permute-start.16 = (bf16[288,256]{1,0:T(8,128)(2,1)S(1)}, bf16[288,256]{1,0:T(8,128)(2,1)S(1)}, u32[]{:S(2)}, u32[]{:S(2)}) collective-permute-start(bf16[288,256]{1,0:T(8,128)(2,1)S(1)} %add_convert_fusion), channel_id=1, source_target_pairs={{0,0},{1,8},{2,2},{3,10},{4,4},{5,12},{6,6},{7,14},{8,1},{9,9},{10... | collective-permute-start | bytes 442376 | tf_op jit(solution)/shard_map/ppermute | solution.py:325

commit v7 on v6

--- a/solution.py
+++ b/solution.py
@@ -156,10 +156,27 @@
             at += size
 
 
-def own_kernel(n_inner, *refs):
-    inner_refs, own_ref, outs = refs[:n_inner], refs[n_inner], refs[n_inner + 1 :]
-    products(inner_refs, own_ref[0], outs[:PIECES], 0)
-    products(inner_refs, own_ref[1], outs[PIECES:], 0)
+def rows_kernel(n_give, inner_ref, own_ref, *refs):
+    give_refs, outs = refs[:n_give], refs[n_give:]
+    products([inner_ref], own_ref[0], outs[:PIECES], 0)
+    products([inner_ref], own_ref[1], outs[PIECES:], 0)
+    for j, ref in enumerate(give_refs):
+        products([inner_ref], ref[...], outs[:PIECES], 1 + j)
+
+
+def rows_of(inner, own, gives, sizes):
+    cols = own.shape[1]
+    give = [vmem((1 + len(gives), 1, size, cols), jnp.bfloat16) for size in sizes]
+    keep = [vmem((1, 1, size, cols), jnp.float32) for size in sizes]
+    made = pl.pallas_call(
+        functools.partial(rows_kernel, len(gives)),
+        in_specs=[WHOLE] * (2 + len(gives)),
+        out_specs=[WHOLE] * (2 * PIECES),
+        out_shape=give + keep,
+        compiler_params=params(),
+        cost_estimate=COST,
+    )(*held([inner, own, *gives]))
+    return list(made[:PIECES]), list(made[PIECES:])
 
 
 def keep_kernel(n_inner, *refs):
@@ -168,63 +185,50 @@
         products(inner_refs, ref[...], outs, j)
 
 
-def outer_of(inners, own, gives, keeps, sizes):
-    _, rows, depth = own.shape
-
-    def shapes(blocks, kind):
-        return [vmem((blocks, len(inners), size, rows), kind) for size in sizes]
-
+def keep_of(inners, nears, sizes):
+    cols = nears[0].shape[0]
     made = pl.pallas_call(
-        functools.partial(own_kernel, len(inners)),
-        in_specs=[WHOLE] * (len(inners) + 1),
-        out_specs=[WHOLE] * (2 * PIECES),
-        out_shape=shapes(1, jnp.bfloat16) + shapes(1, jnp.float32),
-        compiler_params=params(),
-        cost_estimate=COST,
-    )(*held([*inners, own]))
-    give, keep = [list(made[:PIECES])], [list(made[PIECES:])]
-    for nears, kind, into in ((gives, jnp.bfloat16, give), (keeps, jnp.float32, keep)):
-        made = pl.pallas_call(
-            functools.partial(keep_kernel, len(inners)),
-            in_specs=[WHOLE] * (len(inners) + len(nears)),
-            out_specs=[WHOLE] * PIECES,
-            out_shape=shapes(len(nears), kind),
-            compiler_params=params(),
-            cost_estimate=COST,
-        )(*held([*inners, *after(nears, made)]))
-        into.append(list(made))
-    return give, keep
-
-
-def cores_kernel(index_ref, *refs):
-    (own_ref, near_ref), (got_own_ref, got_near_ref), (kept_ref, sent_ref) = refs[:2], refs[2:4], refs[4:]
-    for k in range(index_ref.shape[0]):
-        block = index_ref[k]
-        for j in range(kept_ref.shape[0]):
-            if j == 0:
-                total = own_ref[0, block] + got_own_ref[0, block]
-            else:
-                total = near_ref[j - 1, block] + got_near_ref[j - 1, block]
-            if k == 0:
-                kept_ref[j] = total
-            else:
-                sent_ref[k - 1, j] = total.astype(sent_ref.dtype)
-
-
-def cores_summed(keep, got, index):
-    near, _, height, wide = keep[1].shape
+        functools.partial(keep_kernel, len(inners)),
+        in_specs=[WHOLE] * (len(inners) + len(nears)),
+        out_specs=[WHOLE] * PIECES,
+        out_shape=[vmem((len(nears), len(inners), size, cols), jnp.float32) for size in sizes],
+        compiler_params=params(),
+        cost_estimate=COST,
+    )(*held([*inners, *nears]))
+    return list(made)
+
+
+def cores_kernel(index_ref, near_ref, *refs):
+    n = (len(refs) - 2) // 2
+    own_refs, got_refs, (kept_ref, sent_ref) = refs[:n], refs[n : 2 * n], refs[2 * n :]
+    for k in range(n):
+        for e in range(n):
+
+            @pl.when(index_ref[k] == e)
+            def _(k=k, e=e):
+                for j in range(kept_ref.shape[0]):
+                    mine = own_refs[e][0, 0] if j == 0 else near_ref[j - 1, e]
+                    total = mine + got_refs[e][j, 0]
+                    if k == 0:
+                        kept_ref[j] = total
+                    else:
+                        sent_ref[k - 1, j] = total.astype(sent_ref.dtype)
+
+
+def cores_summed(near, own, got, index):
+    blocks, _, height, wide = near.shape
     others = index.shape[0] - 1
     return pl.pallas_call(
         cores_kernel,
-        in_specs=[SCALARS] + [WHOLE] * 4,
+        in_specs=[SCALARS] + [WHOLE] * (1 + len(own) + len(got)),
         out_specs=[WHOLE, WHOLE],
         out_shape=[
-            vmem((1 + near, height, wide), jnp.float32),
-            vmem((others, 1 + near, height, wide), jnp.bfloat16),
+            vmem((1 + blocks, height, wide), jnp.float32),
+            vmem((others, 1 + blocks, height, wide), jnp.bfloat16),
         ],
         compiler_params=params(),
         cost_estimate=COST,
-    )(index, *held([*keep, *got]))
+    )(index, *held([near, *own, *got]))
 
 
 def chosen_kernel(index_ref, *refs):
@@ -371,21 +375,22 @@
     parts = [early] + [v for _, _, v in last]
 
     near_left = [from_lo(own_left, j) for j in range(1, s)]
-    inners = list(inner_of(own_left, parts, sizes, places))
-    for rows in near_left:
-        rows = after(rows, inners[-1])
-        inner, own_halves = inner_of(rows, parts, sizes, places, halves, half)
-        inners.append(inner)
-
     cut = height * FIRST[0] // FIRST[1] // 32 * 32
     row_sizes = [cut, height - cut]
-    give, keep = outer_of(inners, own_halves, gives, keeps, row_sizes)
-    got = [[from_term(v, 1) for v in group] for group in give]
+    inner, own_halves = inner_of(own_left, parts, sizes, places, halves, half)
+    inners, own, got = [inner], [], []
+    for rows in [*near_left, None]:
+        give, keep = rows_of(inners[-1], own_halves, gives, row_sizes)
+        own.append(keep)
+        got.append([from_term(v, 1) for v in give])
+        if rows is not None:
+            inners += inner_of(after(rows, keep), parts, sizes, places)
+    near_keep = keep_of(inners, after(keeps, own), row_sizes)
     outs = []
     for p in range(PIECES):
         home_first = p % 2 == 1
         index = counted if home_first else by_zl
-        kept, sent = cores_summed([v[p] for v in keep], [v[p] for v in got], index)
+        kept, sent = cores_summed(near_keep[p], [v[p] for v in own], [v[p] for v in got], index)
         if home_first:
             held_blocks = [kept] + [from_lo(sent[s - j - 1], j) for j in range(1, s)]
             kept, *sent = chosen_of(held_blocks, by_zl)

time: 111 us -> 110 us (level); the launches traced: 111 us -> 109 us
  waiting for transfers between devices: 66.6 us -> 62.4 us
  starting transfers between devices: 19.1 us -> 21.2 us
    ppermute x3, waiting for transfers between devices: 12.5 us -> 9.45 us  [from_lo(): return lax.ppermute(value, 'row', pairs)]
    ppermute x2, starting transfers between devices: 1.05 us -> 2.71 us  [to_zl(): return lax.ppermute(value, 'term', pairs)]
  transfers between devices with their start and end apart: 22 -> 22, of which waited for: 14 -> 15; matrix products, arithmetic and copies ran while one was open for 1% -> 1% of each run, Pallas kernels for 18% -> 19%
where the time goes in v7:
time: 110 us; the launch traced here: 109 us
  waiting for transfers between devices  62.4 us (57%)
  Pallas kernels  21.4 us (19%)
  starting transfers between devices  21.2 us (19%)
  local copies, waits for them, and re-layouts  2.72 us (2%)
    ppermute x4, waiting for transfers between devices, from_hi(): return lax.ppermute(value, 'row', pairs)  34.7 us
    pallas_call x2, Pallas kernels, inner_of(): pl.pallas_call(functools.partial(inner_kernel, sizes, len(parts)), in_spe...  10.5 us
    ppermute x3, waiting for transfers between devices, from_lo(): return lax.ppermute(value, 'row', pairs)  9.45 us
    ppermute x10, waiting for transfers between devices, from_term(): return lax.ppermute(value, 'term', [(a ^ bit, a) for a in range(terms)])  8.01 us
    ppermute x2, waiting for transfers between devices, to_zl(): return lax.ppermute(value, 'term', pairs)  5.63 us
    ppermute x1, starting transfers between devices, crossed(): return lax.ppermute(value, ('term', 'row'), pairs)  4.55 us
    ppermute x10, starting transfers between devices, from_term(): return lax.ppermute(value, 'term', [(a ^ bit, a) for a in range(terms)])  4.31 us
    ppermute x4, starting transfers between devices, from_hi(): return lax.ppermute(value, 'row', pairs)  4.28 us
  transfers between devices with their start and end apart: 22, of which 15 were waited for; matrix products, arithmetic and copies ran while one was open for 1% of the time, Pallas kernels for 19%

profile of v7, /device:TPU:2, one launch (start us, length us, event | category | flops | bytes accessed | tf_op | source)
XLA Modules:
  0.0 108.8 jit_solution(7215162365801749877)
XLA Ops:
  0.0 1.2 %shard_map.46 = bf16[128,2048]{1,0:T(8,128)(2,1)S(1)} custom-call(s32[1]{0:T(128)} %bitcast.start_ref, bf16[512,2048]{1,0:T(8,128)(2,1)} %refs_0_.1), custom_call_target="tpu_custom_call" | custom-call | flops 1 | bytes 1 | tf_op jit(solution)/shard_map/pallas_call | solution.py:65
  1.2 1.6 %collective-permute-start.1 = (bf16[128,2048]{1,0:T(8,128)(2,1)S(1)}, bf16[128,2048]{1,0:T(8,128)(2,1)}, u32[]{:S(2)}, u32[]{:S(2)}) collective-permute-start(bf16[128,2048]{1,0:T(8,128)(2,1)S(1)} %shard_map.46), channel_id=1, source_target_pairs={{2,0},{3,1},{0,2},{1,3},{6,4},{7,5},{4,6},{5,7},{10,8},{11,9},{8,1... | collective-permute-start | bytes 1572872 | tf_op jit(solution)/shard_map/ppermute | solution.py:305
  2.8 0.5 collective-permute-start
  3.3 1.3 %shard_map.47.rows_ref = bf16[512,2048]{1,0:T(8,128)(2,1)S(1)} custom-call(s32[4,16]{1,0:T(4,128)S(1)} %bitcast.33, bf16[512,2048]{1,0:T(8,128)(2,1)S(1)} %bitcast.32), custom_call_target="tpu_custom_call" | custom-call | flops 1 | bytes 1 | tf_op jit(solution)/shard_map/pallas_call | solution.py:45
  4.6 1.4 %copy-done.2 = bf16[512,2048]{1,0:T(8,128)(2,1)} copy-done((bf16[512,2048]{1,0:T(8,128)(2,1)}, bf16[512,2048]{1,0:T(8,128)(2,1)S(1)}, u32[]{:S(2)}) %copy-start.2) | copy-done | bytes 2097176
  6.0 0.1 stack.73.place_ref
  6.1 0.1 pad_add_fusion
  6.1 0.1 dynamic-slice_bitcast_fusion
  6.3 0.0 copy-start.1
  6.3 8.8 %collective-permute-done.1 = bf16[128,2048]{1,0:T(8,128)(2,1)} collective-permute-done((bf16[128,2048]{1,0:T(8,128)(2,1)S(1)}, bf16[128,2048]{1,0:T(8,128)(2,1)}, u32[]{:S(2)}, u32[]{:S(2)}) %collective-permute-start.1) | collective-permute-done | bytes 524320 | tf_op jit(solution)/shard_map/ppermute | solution.py:305
  15.0 1.1 %collective-permute-done = bf16[128,2048]{1,0:T(8,128)(2,1)S(1)} collective-permute-done((bf16[128,2048]{1,0:T(8,128)(2,1)S(1)}, bf16[128,2048]{1,0:T(8,128)(2,1)S(1)}, u32[]{:S(2)}, u32[]{:S(2)}) %collective-permute-start) | collective-permute-done | bytes 524320 | tf_op jit(solution)/shard_map/ppermute | solution.py:301
  16.2 0.5 collective-permute-start.2
  16.7 1.1 constant_dynamic-update-slice_fusion.refs_1_
  17.8 0.1 collective-permute-start.3
  17.9 1.6 %collective-permute-start.7 = (bf16[256,2048]{1,0:T(8,128)(2,1)S(1)}, bf16[256,2048]{1,0:T(8,128)(2,1)S(1)}, u32[]{:S(2)}, u32[]{:S(2)}) collective-permute-start(bf16[256,2048]{1,0:T(8,128)(2,1)S(1)} %get-tuple-element.53), channel_id=1, source_target_pairs={{2,0},{3,1},{0,2},{1,3},{6,4},{7,5},{4,6},{5,7},{10,8},{11,9},{8,1... | collective-permute-start | bytes 3145736 | tf_op jit(solution)/shard_map/ppermute | solution.py:305
  19.5 1.6 %collective-permute-start.5 = (bf16[256,2048]{1,0:T(8,128)(2,1)S(1)}, bf16[256,2048]{1,0:T(8,128)(2,1)S(1)}, u32[]{:S(2)}, u32[]{:S(2)}) collective-permute-start(bf16[256,2048]{1,0:T(8,128)(2,1)S(1)} %constant_dynamic-update-slice_fusion.refs_1_), channel_id=1, source_target_pairs={{8,0},{12,4},{0,8},{4,12},{24,16},{28,20},{16,24},{20,28},{9,1},{1... | collective-permute-start | bytes 3145736 | tf_op jit(solution)/shard_map/ppermute | solution.py:308
  21.1 0.5 collective-permute-start.10
  21.6 9.5 %collective-permute-done.2.refs_2_ = bf16[128,2048]{1,0:T(8,128)(2,1)S(1)} collective-permute-done((bf16[128,2048]{1,0:T(8,128)(2,1)S(1)}, bf16[128,2048]{1,0:T(8,128)(2,1)S(1)}, u32[]{:S(2)}, u32[]{:S(2)}) %collective-permute-start.2) | collective-permute-done | bytes 524320 | tf_op jit(solution)/shard_map/ppermute | solution.py:305
  31.0 0.0 collective-permute-start.4
  31.0 1.9 %collective-permute-done.4.refs_4_ = bf16[128,2048]{1,0:T(8,128)(2,1)S(1)} collective-permute-done((bf16[128,2048]{1,0:T(8,128)(2,1)S(1)}, bf16[128,2048]{1,0:T(8,128)(2,1)S(1)}, u32[]{:S(2)}, u32[]{:S(2)}) %collective-permute-start.4) | collective-permute-done | bytes 524320 | tf_op jit(solution)/shard_map/ppermute | solution.py:308
  33.0 1.6 %collective-permute-start.6 = (bf16[128,2048]{1,0:T(8,128)(2,1)S(1)}, bf16[128,2048]{1,0:T(8,128)(2,1)S(1)}, u32[]{:S(2)}, u32[]{:S(2)}) collective-permute-start(bf16[128,2048]{1,0:T(8,128)(2,1)S(1)} %collective-permute-done.2.refs_2_), channel_id=1, source_target_pairs={{8,0},{12,4},{0,8},{4,12},{24,16},{28,20},{16,24},{20,28},{9,1},{1... | collective-permute-start | bytes 1572872 | tf_op jit(solution)/shard_map/ppermute | solution.py:308
  34.5 0.0 collective-permute-done.3.refs_3_
  34.5 0.4 shard_map.48.refs_0_
  35.0 16.3 %collective-permute-done.7.refs_0_ = bf16[256,2048]{1,0:T(8,128)(2,1)S(1)} collective-permute-done((bf16[256,2048]{1,0:T(8,128)(2,1)S(1)}, bf16[256,2048]{1,0:T(8,128)(2,1)S(1)}, u32[]{:S(2)}, u32[]{:S(2)}) %collective-permute-start.7) | collective-permute-done | bytes 1048608 | tf_op jit(solution)/shard_map/ppermute | solution.py:305
  51.2 0.0 collective-permute-done.5.refs_1_
  51.2 0.0 collective-permute-start.8
  51.2 0.6 collective-permute-start.11
  51.8 4.1 %collective-permute-done.6.refs_2_ = bf16[128,2048]{1,0:T(8,128)(2,1)S(1)} collective-permute-done((bf16[128,2048]{1,0:T(8,128)(2,1)S(1)}, bf16[128,2048]{1,0:T(8,128)(2,1)S(1)}, u32[]{:S(2)}, u32[]{:S(2)}) %collective-permute-start.6) | collective-permute-done | bytes 524320 | tf_op jit(solution)/shard_map/ppermute | solution.py:308
  55.9 0.0 collective-permute-start.9
  55.9 1.9 %collective-permute-done.9.refs_4_ = bf16[128,2048]{1,0:T(8,128)(2,1)S(1)} collective-permute-done((bf16[128,2048]{1,0:T(8,128)(2,1)S(1)}, bf16[128,2048]{1,0:T(8,128)(2,1)S(1)}, u32[]{:S(2)}, u32[]{:S(2)}) %collective-permute-start.9) | collective-permute-done | bytes 524320 | tf_op jit(solution)/shard_map/ppermute | solution.py:308
  57.9 0.0 collective-permute-done.8.refs_3_
  57.9 5.3 %shard_map.49 = (bf16[512,2048]{1,0:T(8,128)(2,1)S(1)}, bf16[2,256,2048]{2,1,0:T(8,128)(2,1)S(1)}) custom-call(s32[13]{0:T(128)S(1)} %stack.73.place_ref, bf16[512,2048]{1,0:T(8,128)(2,1)S(1)} %copy-done.3, bf16[1280,2048]{1,0:T(8,128)(2,1)S(1)} %shard_map.48.refs_0_, bf16[256,2048]{1,0:T(8,128)(2,1)S(1)} %collective-permute-done.5.refs_1_, ...), custom_call_target="tpu_custom_call" | custom-call | flops 1 | bytes 1 | tf_op jit(solution)/shard_map/pallas_call | solution.py:136
  63.2 1.8 %shard_map.50 = (bf16[2,1,288,256]{3,2,1,0:T(8,128)(2,1)S(1)}, bf16[2,1,224,256]{3,2,1,0:T(8,128)(2,1)S(1)}, f32[1,1,288,256]{3,2,1,0:T(8,128)S(1)}, f32[1,1,224,256]{3,2,1,0:T(8,128)S(1)}) custom-call(bf16[512,2048]{1,0:T(8,128)(2,1)S(1)} %get-tuple-element.56.inner_ref.refs_0_, bf16[2,256,2048]{2,1,0:T(8,128)(2,1)S(1)} %get-tuple-element.57.own_ref, ...), custom_call_target="tpu_custom_call" | custom-call | flops 1 | bytes 1 | tf_op jit(solution)/shard_map/pallas_call | solution.py:171
  65.0 3.5 %collective-permute-done.10.rows_ref = bf16[512,2048]{1,0:T(8,128)(2,1)S(1)} collective-permute-done((bf16[512,2048]{1,0:T(8,128)(2,1)S(1)}, bf16[512,2048]{1,0:T(8,128)(2,1)S(1)}, u32[]{:S(2)}, u32[]{:S(2)}) %collective-permute-start.10) | collective-permute-done | bytes 2097184 | tf_op jit(solution)/shard_map/ppermute | solution.py:301
  68.5 5.2 %shard_map.51.inner_ref.refs_1_ = bf16[512,2048]{1,0:T(8,128)(2,1)S(1)} custom-call(s32[13]{0:T(128)S(1)} %stack.73.place_ref, bf16[512,2048]{1,0:T(8,128)(2,1)S(1)} %collective-permute-done.10.rows_ref, bf16[1280,2048]{1,0:T(8,128)(2,1)S(1)} %shard_map.48.refs_0_, bf16[256,2048]{1,0:T(8,128)(2,1)S(1)} %collective-permute-done.5.refs_1_, ...), custom_call_target="tpu_custom_call" | custom-call | flops 1 | bytes 1 | tf_op jit(solution)/shard_map/pallas_call | solution.py:136
  73.6 1.8 %shard_map.52 = (bf16[2,1,288,256]{3,2,1,0:T(8,128)(2,1)S(1)}, bf16[2,1,224,256]{3,2,1,0:T(8,128)(2,1)S(1)}, f32[1,1,288,256]{3,2,1,0:T(8,128)S(1)}, f32[1,1,224,256]{3,2,1,0:T(8,128)S(1)}) custom-call(bf16[512,2048]{1,0:T(8,128)(2,1)S(1)} %shard_map.51.inner_ref.refs_1_, bf16[2,256,2048]{2,1,0:T(8,128)(2,1)S(1)} %get-tuple-element.57.own_ref, ...), custom_call_target="tpu_custom_call" | custom-call | flops 1 | bytes 1 | tf_op jit(solution)/shard_map/pallas_call | solution.py:171
  75.5 0.1 collective-permute-start.13
  75.6 0.5 collective-permute-start.12
  76.1 0.1 collective-permute-start.18
  76.1 0.4 collective-permute-start.17
  76.6 0.2 collective-permute-done.11.refs_2_
  76.8 1.3 %shard_map.53 = (f32[1,2,288,256]{3,2,1,0:T(8,128)S(1)}, f32[1,2,224,256]{3,2,1,0:T(8,128)S(1)}) custom-call(bf16[512,2048]{1,0:T(8,128)(2,1)S(1)} %get-tuple-element.56.inner_ref.refs_0_, bf16[512,2048]{1,0:T(8,128)(2,1)S(1)} %shard_map.51.inner_ref.refs_1_, bf16[256,2048]{1,0:T(8,128)(2,1)S(1)} %collective-permute-done.11.refs_2_), custom_call_target="tpu_custom_call" | custom-call | flops 1 | bytes 1 | tf_op jit(solution)/shard_map/pallas_call | solution.py:190
  78.1 0.0 collective-permute-done.18.refs_3_
  78.1 0.1 collective-permute-done.17.refs_2_
  78.2 0.6 shard_map.56
  78.9 0.6 collective-permute-start.19
  79.5 0.0 collective-permute-done.13.refs_3_
  79.5 0.0 collective-permute-done.12.refs_2_
  79.5 0.7 shard_map.54
  80.1 1.6 %collective-permute-start.14 = (bf16[2,288,256]{2,1,0:T(8,128)(2,1)S(1)}, bf16[2,288,256]{2,1,0:T(8,128)(2,1)S(1)}, u32[]{:S(2)}, u32[]{:S(2)}) collective-permute-start(bf16[2,288,256]{2,1,0:T(8,128)(2,1)S(1)} %bitcast.34), channel_id=1, source_target_pairs={{0,8},{4,12},{8,0},{12,4},{16,24},{20,28},{24,16},{28,20},{1,9},{5... | collective-permute-start | bytes 884744 | tf_op jit(solution)/shard_map/ppermute | solution.py:315
  81.7 4.9 %collective-permute-done.19.refs_1_ = bf16[2,224,256]{2,1,0:T(8,128)(2,1)S(1)} collective-permute-done((bf16[2,224,256]{2,1,0:T(8,128)(2,1)S(1)}, bf16[2,224,256]{2,1,0:T(8,128)(2,1)S(1)}, u32[]{:S(2)}, u32[]{:S(2)}) %collective-permute-start.19) | collective-permute-done | bytes 229408 | tf_op jit(solution)/shard_map/ppermute | solution.py:301
  86.6 0.6 shard_map.57
  87.2 1.2 %collective-permute-start.20 = (bf16[2,224,256]{2,1,0:T(8,128)(2,1)S(1)}, bf16[2,224,256]{2,1,0:T(8,128)(2,1)S(1)}, u32[]{:S(2)}, u32[]{:S(2)}) collective-permute-start(bf16[2,224,256]{2,1,0:T(8,128)(2,1)S(1)} %get-tuple-element.80), channel_id=1, source_target_pairs={{0,8},{4,12},{8,0},{12,4},{16,24},{20,28},{24,16},{28,20},{1,9},{5... | collective-permute-start | bytes 688136 | tf_op jit(solution)/shard_map/ppermute | solution.py:315
  88.4 0.6 collective-permute-done.14.refs_0_
  89.0 0.6 shard_map.55
  89.6 2.7 %collective-permute-start.15 = (bf16[288,256]{1,0:T(8,128)(2,1)S(1)}, bf16[288,256]{1,0:T(8,128)(2,1)S(1)}, u32[]{:S(2)}, u32[]{:S(2)}) collective-permute-start(bf16[288,256]{1,0:T(8,128)(2,1)S(1)} %bitcast.36), channel_id=1, source_target_pairs={{0,16},{4,20},{8,24},{12,28},{16,0},{20,4},{24,8},{28,12},{1,17},{... | collective-permute-start | bytes 442376 | tf_op jit(solution)/shard_map/ppermute | solution.py:322
  92.2 5.0 %collective-permute-done.20.refs_0_ = bf16[2,224,256]{2,1,0:T(8,128)(2,1)S(1)} collective-permute-done((bf16[2,224,256]{2,1,0:T(8,128)(2,1)S(1)}, bf16[2,224,256]{2,1,0:T(8,128)(2,1)S(1)}, u32[]{:S(2)}, u32[]{:S(2)}) %collective-permute-start.20) | collective-permute-done | bytes 229408 | tf_op jit(solution)/shard_map/ppermute | solution.py:315
  97.2 0.6 shard_map.58
  97.8 1.1 collective-permute-start.21
  98.9 0.0 collective-permute-done.15
  98.9 4.5 %collective-permute-start.16 = (bf16[288,256]{1,0:T(8,128)(2,1)S(1)}, bf16[288,256]{1,0:T(8,128)(2,1)S(1)}, u32[]{:S(2)}, u32[]{:S(2)}) collective-permute-start(bf16[288,256]{1,0:T(8,128)(2,1)S(1)} %add_convert_fusion), channel_id=1, source_target_pairs={{0,0},{1,8},{2,2},{3,10},{4,4},{5,12},{6,6},{7,14},{8,1},{9,9},{10... | collective-permute-start | bytes 442376 | tf_op jit(solution)/shard_map/ppermute | solution.py:329
  103.5 0.7 collective-permute-done.21
  104.2 3.9 %collective-permute-done.16 = bf16[288,256]{1,0:T(8,128)(2,1)S(1)} collective-permute-done((bf16[288,256]{1,0:T(8,128)(2,1)S(1)}, bf16[288,256]{1,0:T(8,128)(2,1)S(1)}, u32[]{:S(2)}, u32[]{:S(2)}) %collective-permute-start.16) | collective-permute-done | bytes 147488 | tf_op jit(solution)/shard_map/ppermute | solution.py:329
  108.1 0.7 pad_maximum_fusion
  (14 shorter events, 0.1 us)
Async XLA Ops:
  0.0 3.3 %copy-start.5 = (s32[1,4,16]{2,1,0:T(4,128)S(1)}, s32[1,4,16]{2,1,0:T(4,128)}, u32[]{:S(2)}) copy-start(s32[1,4,16]{2,1,0:T(4,128)} %param.7) | copy-start | bytes 772
  0.0 3.3 %copy-start.4 = (bf16[1,512,2048]{2,1,0:T(8,128)(2,1)S(1)}, bf16[1,512,2048]{2,1,0:T(8,128)(2,1)}, u32[]{:S(2)}) copy-start(bf16[1,512,2048]{2,1,0:T(8,128)(2,1)} %param.5) | copy-start | bytes 6291460
  1.2 13.8 %collective-permute-start.1 = (bf16[128,2048]{1,0:T(8,128)(2,1)S(1)}, bf16[128,2048]{1,0:T(8,128)(2,1)}, u32[]{:S(2)}, u32[]{:S(2)}) collective-permute-start(bf16[128,2048]{1,0:T(8,128)(2,1)S(1)} %shard_map.46), channel_id=1, source_target_pairs={{2,0},{3,1},{0,2},{1,3},{6,4},{7,5},{4,6},{5,7},{10,8},{11,9},{8,1... | collective-permute-start | bytes 1572872 | tf_op jit(solution)/shard_map/ppermute | solution.py:305
  2.8 13.4 %collective-permute-start = (bf16[128,2048]{1,0:T(8,128)(2,1)S(1)}, bf16[128,2048]{1,0:T(8,128)(2,1)S(1)}, u32[]{:S(2)}, u32[]{:S(2)}) collective-permute-start(bf16[128,2048]{1,0:T(8,128)(2,1)S(1)} %shard_map.46), channel_id=1, source_target_pairs={{1,0},{0,1},{3,2},{2,3},{5,4},{4,5},{7,6},{6,7},{9,8},{8,9},{11,10... | collective-permute-start | bytes 1572872 | tf_op jit(solution)/shard_map/ppermute | solution.py:301
  3.3 2.8 %copy-start = (bf16[1,512,2048]{2,1,0:T(8,128)(2,1)S(1)}, bf16[1,512,2048]{2,1,0:T(8,128)(2,1)}, u32[]{:S(2)}) copy-start(bf16[1,512,2048]{2,1,0:T(8,128)(2,1)} %param.6) | copy-start | bytes 6291460
  4.6 1.4 %copy-start.2 = (bf16[512,2048]{1,0:T(8,128)(2,1)}, bf16[512,2048]{1,0:T(8,128)(2,1)S(1)}, u32[]{:S(2)}) copy-start(bf16[512,2048]{1,0:T(8,128)(2,1)S(1)} %shard_map.47.rows_ref) | copy-start | bytes 6291460
  6.1 14.9 %copy-start.3 = (bf16[512,2048]{1,0:T(8,128)(2,1)S(1)}, bf16[512,2048]{1,0:T(8,128)(2,1)}, u32[]{:S(2)}) copy-start(bf16[512,2048]{1,0:T(8,128)(2,1)} %copy-done.2) | copy-start | bytes 6291460
  6.3 28.3 %copy-start.1 = (bf16[512,2048]{1,0:T(8,128)(2,1)S(1)}, bf16[512,2048]{1,0:T(8,128)(2,1)}, u32[]{:S(2)}) copy-start(bf16[512,2048]{1,0:T(8,128)(2,1)} %refs_0_.1) | copy-start | bytes 6291460
  16.2 14.9 %collective-permute-start.2 = (bf16[128,2048]{1,0:T(8,128)(2,1)S(1)}, bf16[128,2048]{1,0:T(8,128)(2,1)S(1)}, u32[]{:S(2)}, u32[]{:S(2)}) collective-permute-start(bf16[128,2048]{1,0:T(8,128)(2,1)S(1)} %collective-permute-done), channel_id=1, source_target_pairs={{2,0},{3,1},{0,2},{1,3},{6,4},{7,5},{4,6},{5,7},{10,8},{11,9},{8,1... | collective-permute-start | bytes 1572872 | tf_op jit(solution)/shard_map/ppermute | solution.py:305
  17.8 16.7 %collective-permute-start.3 = (bf16[256,2048]{1,0:T(8,128)(2,1)S(1)}, bf16[256,2048]{1,0:T(8,128)(2,1)S(1)}, u32[]{:S(2)}, u32[]{:S(2)}) collective-permute-start(bf16[256,2048]{1,0:T(8,128)(2,1)S(1)} %constant_dynamic-update-slice_fusion.refs_1_), channel_id=1, source_target_pairs={{4,0},{0,4},{12,8},{8,12},{20,16},{16,20},{28,24},{24,28},{5,1},{1... | collective-permute-start | bytes 3145736 | tf_op jit(solution)/shard_map/ppermute | solution.py:308
  17.9 33.3 %collective-permute-start.7 = (bf16[256,2048]{1,0:T(8,128)(2,1)S(1)}, bf16[256,2048]{1,0:T(8,128)(2,1)S(1)}, u32[]{:S(2)}, u32[]{:S(2)}) collective-permute-start(bf16[256,2048]{1,0:T(8,128)(2,1)S(1)} %get-tuple-element.53), channel_id=1, source_target_pairs={{2,0},{3,1},{0,2},{1,3},{6,4},{7,5},{4,6},{5,7},{10,8},{11,9},{8,1... | collective-permute-start | bytes 3145736 | tf_op jit(solution)/shard_map/ppermute | solution.py:305
  19.5 31.8 %collective-permute-start.5 = (bf16[256,2048]{1,0:T(8,128)(2,1)S(1)}, bf16[256,2048]{1,0:T(8,128)(2,1)S(1)}, u32[]{:S(2)}, u32[]{:S(2)}) collective-permute-start(bf16[256,2048]{1,0:T(8,128)(2,1)S(1)} %constant_dynamic-update-slice_fusion.refs_1_), channel_id=1, source_target_pairs={{8,0},{12,4},{0,8},{4,12},{24,16},{28,20},{16,24},{20,28},{9,1},{1... | collective-permute-start | bytes 3145736 | tf_op jit(solution)/shard_map/ppermute | solution.py:308
  21.1 47.4 %collective-permute-start.10 = (bf16[512,2048]{1,0:T(8,128)(2,1)S(1)}, bf16[512,2048]{1,0:T(8,128)(2,1)S(1)}, u32[]{:S(2)}, u32[]{:S(2)}) collective-permute-start(bf16[512,2048]{1,0:T(8,128)(2,1)S(1)} %copy-done.3), channel_id=1, source_target_pairs={{1,0},{0,1},{3,2},{2,3},{5,4},{4,5},{7,6},{6,7},{9,8},{8,9},{11,10... | collective-permute-start | bytes 6291464 | tf_op jit(solution)/shard_map/ppermute | solution.py:301
  31.0 1.9 %collective-permute-start.4 = (bf16[128,2048]{1,0:T(8,128)(2,1)S(1)}, bf16[128,2048]{1,0:T(8,128)(2,1)S(1)}, u32[]{:S(2)}, u32[]{:S(2)}) collective-permute-start(bf16[128,2048]{1,0:T(8,128)(2,1)S(1)} %collective-permute-done.2.refs_2_), channel_id=1, source_target_pairs={{4,0},{0,4},{12,8},{8,12},{20,16},{16,20},{28,24},{24,28},{5,1},{1... | collective-permute-start | bytes 1572872 | tf_op jit(solution)/shard_map/ppermute | solution.py:308
  33.0 23.0 %collective-permute-start.6 = (bf16[128,2048]{1,0:T(8,128)(2,1)S(1)}, bf16[128,2048]{1,0:T(8,128)(2,1)S(1)}, u32[]{:S(2)}, u32[]{:S(2)}) collective-permute-start(bf16[128,2048]{1,0:T(8,128)(2,1)S(1)} %collective-permute-done.2.refs_2_), channel_id=1, source_target_pairs={{8,0},{12,4},{0,8},{4,12},{24,16},{28,20},{16,24},{20,28},{9,1},{1... | collective-permute-start | bytes 1572872 | tf_op jit(solution)/shard_map/ppermute | solution.py:308
  51.2 6.6 %collective-permute-start.8 = (bf16[256,2048]{1,0:T(8,128)(2,1)S(1)}, bf16[256,2048]{1,0:T(8,128)(2,1)S(1)}, u32[]{:S(2)}, u32[]{:S(2)}) collective-permute-start(bf16[256,2048]{1,0:T(8,128)(2,1)S(1)} %collective-permute-done.5.refs_1_), channel_id=1, source_target_pairs={{4,0},{0,4},{12,8},{8,12},{20,16},{16,20},{28,24},{24,28},{5,1},{1... | collective-permute-start | bytes 3145736 | tf_op jit(solution)/shard_map/ppermute | solution.py:308
  51.2 25.6 %collective-permute-start.11 = (bf16[256,2048]{1,0:T(8,128)(2,1)S(1)}, bf16[256,2048]{1,0:T(8,128)(2,1)S(1)}, u32[]{:S(2)}, u32[]{:S(2)}) collective-permute-start(bf16[256,2048]{1,0:T(8,128)(2,1)S(1)} %get-tuple-element.62), channel_id=1, source_target_pairs={{2,0},{3,1},{0,2},{1,3},{6,4},{7,5},{4,6},{5,7},{10,8},{11,9},{8,1... | collective-permute-start | bytes 3145736 | tf_op jit(solution)/shard_map/ppermute | solution.py:305
  55.9 1.9 %collective-permute-start.9 = (bf16[128,2048]{1,0:T(8,128)(2,1)S(1)}, bf16[128,2048]{1,0:T(8,128)(2,1)S(1)}, u32[]{:S(2)}, u32[]{:S(2)}) collective-permute-start(bf16[128,2048]{1,0:T(8,128)(2,1)S(1)} %collective-permute-done.6.refs_2_), channel_id=1, source_target_pairs={{4,0},{0,4},{12,8},{8,12},{20,16},{16,20},{28,24},{24,28},{5,1},{1... | collective-permute-start | bytes 1572872 | tf_op jit(solution)/shard_map/ppermute | solution.py:308
  75.5 4.0 %collective-permute-start.13 = (bf16[2,1,288,256]{3,2,1,0:T(8,128)(2,1)S(1)}, bf16[2,1,288,256]{3,2,1,0:T(8,128)(2,1)S(1)}, u32[]{:S(2)}, u32[]{:S(2)}) collective-permute-start(bf16[2,1,288,256]{3,2,1,0:T(8,128)(2,1)S(1)} %get-tuple-element.68), channel_id=1, source_target_pairs={{4,0},{0,4},{12,8},{8,12},{20,16},{16,20},{28,24},{24,28},{5,1},{1... | collective-permute-start | bytes 884744 | tf_op jit(solution)/shard_map/ppermute | solution.py:308
  75.6 3.9 %collective-permute-start.12 = (bf16[2,1,288,256]{3,2,1,0:T(8,128)(2,1)S(1)}, bf16[2,1,288,256]{3,2,1,0:T(8,128)(2,1)S(1)}, u32[]{:S(2)}, u32[]{:S(2)}) collective-permute-start(bf16[2,1,288,256]{3,2,1,0:T(8,128)(2,1)S(1)} %get-tuple-element.67), channel_id=1, source_target_pairs={{4,0},{0,4},{12,8},{8,12},{20,16},{16,20},{28,24},{24,28},{5,1},{1... | collective-permute-start | bytes 884744 | tf_op jit(solution)/shard_map/ppermute | solution.py:308
  76.1 2.1 %collective-permute-start.18 = (bf16[2,1,224,256]{3,2,1,0:T(8,128)(2,1)S(1)}, bf16[2,1,224,256]{3,2,1,0:T(8,128)(2,1)S(1)}, u32[]{:S(2)}, u32[]{:S(2)}) collective-permute-start(bf16[2,1,224,256]{3,2,1,0:T(8,128)(2,1)S(1)} %get-tuple-element.76), channel_id=1, source_target_pairs={{4,0},{0,4},{12,8},{8,12},{20,16},{16,20},{28,24},{24,28},{5,1},{1... | collective-permute-start | bytes 688136 | tf_op jit(solution)/shard_map/ppermute | solution.py:308
  76.1 2.1 %collective-permute-start.17 = (bf16[2,1,224,256]{3,2,1,0:T(8,128)(2,1)S(1)}, bf16[2,1,224,256]{3,2,1,0:T(8,128)(2,1)S(1)}, u32[]{:S(2)}, u32[]{:S(2)}) collective-permute-start(bf16[2,1,224,256]{3,2,1,0:T(8,128)(2,1)S(1)} %get-tuple-element.75), channel_id=1, source_target_pairs={{4,0},{0,4},{12,8},{8,12},{20,16},{16,20},{28,24},{24,28},{5,1},{1... | collective-permute-start | bytes 688136 | tf_op jit(solution)/shard_map/ppermute | solution.py:308
  78.9 7.7 %collective-permute-start.19 = (bf16[2,224,256]{2,1,0:T(8,128)(2,1)S(1)}, bf16[2,224,256]{2,1,0:T(8,128)(2,1)S(1)}, u32[]{:S(2)}, u32[]{:S(2)}) collective-permute-start(bf16[2,224,256]{2,1,0:T(8,128)(2,1)S(1)} %bitcast.35), channel_id=1, source_target_pairs={{1,0},{0,1},{3,2},{2,3},{5,4},{4,5},{7,6},{6,7},{9,8},{8,9},{11,10... | collective-permute-start | bytes 688136 | tf_op jit(solution)/shard_map/ppermute | solution.py:301
  80.1 8.8 %collective-permute-start.14 = (bf16[2,288,256]{2,1,0:T(8,128)(2,1)S(1)}, bf16[2,288,256]{2,1,0:T(8,128)(2,1)S(1)}, u32[]{:S(2)}, u32[]{:S(2)}) collective-permute-start(bf16[2,288,256]{2,1,0:T(8,128)(2,1)S(1)} %bitcast.34), channel_id=1, source_target_pairs={{0,8},{4,12},{8,0},{12,4},{16,24},{20,28},{24,16},{28,20},{1,9},{5... | collective-permute-start | bytes 884744 | tf_op jit(solution)/shard_map/ppermute | solution.py:315
  87.2 10.0 %collective-permute-start.20 = (bf16[2,224,256]{2,1,0:T(8,128)(2,1)S(1)}, bf16[2,224,256]{2,1,0:T(8,128)(2,1)S(1)}, u32[]{:S(2)}, u32[]{:S(2)}) collective-permute-start(bf16[2,224,256]{2,1,0:T(8,128)(2,1)S(1)} %get-tuple-element.80), channel_id=1, source_target_pairs={{0,8},{4,12},{8,0},{12,4},{16,24},{20,28},{24,16},{28,20},{1,9},{5... | collective-permute-start | bytes 688136 | tf_op jit(solution)/shard_map/ppermute | solution.py:315
  89.6 9.3 %collective-permute-start.15 = (bf16[288,256]{1,0:T(8,128)(2,1)S(1)}, bf16[288,256]{1,0:T(8,128)(2,1)S(1)}, u32[]{:S(2)}, u32[]{:S(2)}) collective-permute-start(bf16[288,256]{1,0:T(8,128)(2,1)S(1)} %bitcast.36), channel_id=1, source_target_pairs={{0,16},{4,20},{8,24},{12,28},{16,0},{20,4},{24,8},{28,12},{1,17},{... | collective-permute-start | bytes 442376 | tf_op jit(solution)/shard_map/ppermute | solution.py:322
  97.8 6.3 %collective-permute-start.21 = (bf16[224,256]{1,0:T(8,128)(2,1)S(1)}, bf16[224,256]{1,0:T(8,128)(2,1)S(1)}, u32[]{:S(2)}, u32[]{:S(2)}) collective-permute-start(bf16[224,256]{1,0:T(8,128)(2,1)S(1)} %bitcast.37), channel_id=1, source_target_pairs={{0,16},{4,20},{8,24},{12,28},{16,0},{20,4},{24,8},{28,12},{1,17},{... | collective-permute-start | bytes 344072 | tf_op jit(solution)/shard_map/ppermute | solution.py:322
  98.9 9.2 %collective-permute-start.16 = (bf16[288,256]{1,0:T(8,128)(2,1)S(1)}, bf16[288,256]{1,0:T(8,128)(2,1)S(1)}, u32[]{:S(2)}, u32[]{:S(2)}) collective-permute-start(bf16[288,256]{1,0:T(8,128)(2,1)S(1)} %add_convert_fusion), channel_id=1, source_target_pairs={{0,0},{1,8},{2,2},{3,10},{4,4},{5,12},{6,6},{7,14},{8,1},{9,9},{10... | collective-permute-start | bytes 442376 | tf_op jit(solution)/shard_map/ppermute | solution.py:329

commit v8 on v7

--- a/solution.py
+++ b/solution.py
@@ -10,7 +10,7 @@
 
 SHARE = 4
 PIECES = 2
-FIRST = (9, 16)
+FIRST = (1, 2)
 VMEM_BYTES = 20 * 1024 * 1024
 COST = pl.CostEstimate(flops=1, bytes_accessed=1, transcendentals=0)
 WHOLE = pl.BlockSpec(memory_space=pltpu.VMEM)

time: 110 us -> 109 us (level)
  waiting for transfers between devices: 62.4 us -> 61.1 us
    ppermute x1, waiting for transfers between devices: 3.91 us -> 1.95 us  [crossed(): return lax.ppermute(value, ('term', 'row'), pairs)]
  transfers between devices with their start and end apart: 22 -> 22, of which waited for: 15 -> 13; matrix products, arithmetic and copies ran while one was open for 1% -> 1% of each run, Pallas kernels for 19% -> 19%
where the time goes in v8:
time: 109 us; the launch traced here: 108 us
  waiting for transfers between devices  61.1 us (56%)
  starting transfers between devices  22 us (20%)
  Pallas kernels  21.4 us (20%)
  local copies, waits for them, and re-layouts  2.72 us (2%)
    ppermute x4, waiting for transfers between devices, from_hi(): return lax.ppermute(value, 'row', pairs)  34.7 us
    pallas_call x2, Pallas kernels, inner_of(): pl.pallas_call(functools.partial(inner_kernel, sizes, len(parts)), in_spe...  10.5 us
    ppermute x3, waiting for transfers between devices, from_lo(): return lax.ppermute(value, 'row', pairs)  9.79 us
    ppermute x10, waiting for transfers between devices, from_term(): return lax.ppermute(value, 'term', [(a ^ bit, a) for a in range(terms)])  7.93 us
    ppermute x2, waiting for transfers between devices, to_zl(): return lax.ppermute(value, 'term', pairs)  5.26 us
    ppermute x1, starting transfers between devices, crossed(): return lax.ppermute(value, ('term', 'row'), pairs)  4.36 us
    ppermute x10, starting transfers between devices, from_term(): return lax.ppermute(value, 'term', [(a ^ bit, a) for a in range(terms)])  4.31 us
    ppermute x4, starting transfers between devices, from_hi(): return lax.ppermute(value, 'row', pairs)  4.28 us
  transfers between devices with their start and end apart: 22, of which 13 were waited for; matrix products, arithmetic and copies ran while one was open for 1% of the time, Pallas kernels for 19%

profile of v8, /device:TPU:2, one launch (start us, length us, event | category | flops | bytes accessed | tf_op | source)
XLA Modules:
  0.0 108.2 jit_solution(16369531713739220899)
XLA Ops:
  0.0 1.2 %shard_map.46 = bf16[128,2048]{1,0:T(8,128)(2,1)S(1)} custom-call(s32[1]{0:T(128)} %bitcast.start_ref, bf16[512,2048]{1,0:T(8,128)(2,1)} %refs_0_.1), custom_call_target="tpu_custom_call" | custom-call | flops 1 | bytes 1 | tf_op jit(solution)/shard_map/pallas_call | solution.py:65
  1.2 1.6 %collective-permute-start.1 = (bf16[128,2048]{1,0:T(8,128)(2,1)S(1)}, bf16[128,2048]{1,0:T(8,128)(2,1)}, u32[]{:S(2)}, u32[]{:S(2)}) collective-permute-start(bf16[128,2048]{1,0:T(8,128)(2,1)S(1)} %shard_map.46), channel_id=1, source_target_pairs={{2,0},{3,1},{0,2},{1,3},{6,4},{7,5},{4,6},{5,7},{10,8},{11,9},{8,1... | collective-permute-start | bytes 1572872 | tf_op jit(solution)/shard_map/ppermute | solution.py:305
  2.8 0.5 collective-permute-start
  3.3 1.3 %shard_map.47.rows_ref = bf16[512,2048]{1,0:T(8,128)(2,1)S(1)} custom-call(s32[4,16]{1,0:T(4,128)S(1)} %bitcast.33, bf16[512,2048]{1,0:T(8,128)(2,1)S(1)} %bitcast.32), custom_call_target="tpu_custom_call" | custom-call | flops 1 | bytes 1 | tf_op jit(solution)/shard_map/pallas_call | solution.py:45
  4.6 1.4 %copy-done.2 = bf16[512,2048]{1,0:T(8,128)(2,1)} copy-done((bf16[512,2048]{1,0:T(8,128)(2,1)}, bf16[512,2048]{1,0:T(8,128)(2,1)S(1)}, u32[]{:S(2)}) %copy-start.2) | copy-done | bytes 2097176
  6.0 0.1 stack.73.place_ref
  6.1 0.1 pad_add_fusion
  6.1 0.1 dynamic-slice_bitcast_fusion
  6.3 0.0 copy-start.1
  6.3 8.8 %collective-permute-done.1 = bf16[128,2048]{1,0:T(8,128)(2,1)} collective-permute-done((bf16[128,2048]{1,0:T(8,128)(2,1)S(1)}, bf16[128,2048]{1,0:T(8,128)(2,1)}, u32[]{:S(2)}, u32[]{:S(2)}) %collective-permute-start.1) | collective-permute-done | bytes 524320 | tf_op jit(solution)/shard_map/ppermute | solution.py:305
  15.0 1.1 %collective-permute-done = bf16[128,2048]{1,0:T(8,128)(2,1)S(1)} collective-permute-done((bf16[128,2048]{1,0:T(8,128)(2,1)S(1)}, bf16[128,2048]{1,0:T(8,128)(2,1)S(1)}, u32[]{:S(2)}, u32[]{:S(2)}) %collective-permute-start) | collective-permute-done | bytes 524320 | tf_op jit(solution)/shard_map/ppermute | solution.py:301
  16.2 0.5 collective-permute-start.2
  16.7 1.1 constant_dynamic-update-slice_fusion.refs_1_
  17.8 0.1 collective-permute-start.3
  17.9 1.6 %collective-permute-start.7 = (bf16[256,2048]{1,0:T(8,128)(2,1)S(1)}, bf16[256,2048]{1,0:T(8,128)(2,1)S(1)}, u32[]{:S(2)}, u32[]{:S(2)}) collective-permute-start(bf16[256,2048]{1,0:T(8,128)(2,1)S(1)} %get-tuple-element.53), channel_id=1, source_target_pairs={{2,0},{3,1},{0,2},{1,3},{6,4},{7,5},{4,6},{5,7},{10,8},{11,9},{8,1... | collective-permute-start | bytes 3145736 | tf_op jit(solution)/shard_map/ppermute | solution.py:305
  19.5 1.6 %collective-permute-start.5 = (bf16[256,2048]{1,0:T(8,128)(2,1)S(1)}, bf16[256,2048]{1,0:T(8,128)(2,1)S(1)}, u32[]{:S(2)}, u32[]{:S(2)}) collective-permute-start(bf16[256,2048]{1,0:T(8,128)(2,1)S(1)} %constant_dynamic-update-slice_fusion.refs_1_), channel_id=1, source_target_pairs={{8,0},{12,4},{0,8},{4,12},{24,16},{28,20},{16,24},{20,28},{9,1},{1... | collective-permute-start | bytes 3145736 | tf_op jit(solution)/shard_map/ppermute | solution.py:308
  21.1 0.5 collective-permute-start.10
  21.6 9.5 %collective-permute-done.2.refs_2_ = bf16[128,2048]{1,0:T(8,128)(2,1)S(1)} collective-permute-done((bf16[128,2048]{1,0:T(8,128)(2,1)S(1)}, bf16[128,2048]{1,0:T(8,128)(2,1)S(1)}, u32[]{:S(2)}, u32[]{:S(2)}) %collective-permute-start.2) | collective-permute-done | bytes 524320 | tf_op jit(solution)/shard_map/ppermute | solution.py:305
  31.0 0.0 collective-permute-start.4
  31.0 1.9 %collective-permute-done.4.refs_4_ = bf16[128,2048]{1,0:T(8,128)(2,1)S(1)} collective-permute-done((bf16[128,2048]{1,0:T(8,128)(2,1)S(1)}, bf16[128,2048]{1,0:T(8,128)(2,1)S(1)}, u32[]{:S(2)}, u32[]{:S(2)}) %collective-permute-start.4) | collective-permute-done | bytes 524320 | tf_op jit(solution)/shard_map/ppermute | solution.py:308
  33.0 1.6 %collective-permute-start.6 = (bf16[128,2048]{1,0:T(8,128)(2,1)S(1)}, bf16[128,2048]{1,0:T(8,128)(2,1)S(1)}, u32[]{:S(2)}, u32[]{:S(2)}) collective-permute-start(bf16[128,2048]{1,0:T(8,128)(2,1)S(1)} %collective-permute-done.2.refs_2_), channel_id=1, source_target_pairs={{8,0},{12,4},{0,8},{4,12},{24,16},{28,20},{16,24},{20,28},{9,1},{1... | collective-permute-start | bytes 1572872 | tf_op jit(solution)/shard_map/ppermute | solution.py:308
  34.5 0.0 collective-permute-done.3.refs_3_
  34.5 0.4 shard_map.48.refs_0_
  35.0 16.3 %collective-permute-done.7.refs_0_ = bf16[256,2048]{1,0:T(8,128)(2,1)S(1)} collective-permute-done((bf16[256,2048]{1,0:T(8,128)(2,1)S(1)}, bf16[256,2048]{1,0:T(8,128)(2,1)S(1)}, u32[]{:S(2)}, u32[]{:S(2)}) %collective-permute-start.7) | collective-permute-done | bytes 1048608 | tf_op jit(solution)/shard_map/ppermute | solution.py:305
  51.2 0.0 collective-permute-done.5.refs_1_
  51.2 0.0 collective-permute-start.8
  51.2 0.6 collective-permute-start.11
  51.8 4.1 %collective-permute-done.6.refs_2_ = bf16[128,2048]{1,0:T(8,128)(2,1)S(1)} collective-permute-done((bf16[128,2048]{1,0:T(8,128)(2,1)S(1)}, bf16[128,2048]{1,0:T(8,128)(2,1)S(1)}, u32[]{:S(2)}, u32[]{:S(2)}) %collective-permute-start.6) | collective-permute-done | bytes 524320 | tf_op jit(solution)/shard_map/ppermute | solution.py:308
  55.9 0.0 collective-permute-start.9
  55.9 1.9 %collective-permute-done.9.refs_4_ = bf16[128,2048]{1,0:T(8,128)(2,1)S(1)} collective-permute-done((bf16[128,2048]{1,0:T(8,128)(2,1)S(1)}, bf16[128,2048]{1,0:T(8,128)(2,1)S(1)}, u32[]{:S(2)}, u32[]{:S(2)}) %collective-permute-start.9) | collective-permute-done | bytes 524320 | tf_op jit(solution)/shard_map/ppermute | solution.py:308
  57.9 0.0 collective-permute-done.8.refs_3_
  57.9 5.3 %shard_map.49 = (bf16[512,2048]{1,0:T(8,128)(2,1)S(1)}, bf16[2,256,2048]{2,1,0:T(8,128)(2,1)S(1)}) custom-call(s32[13]{0:T(128)S(1)} %stack.73.place_ref, bf16[512,2048]{1,0:T(8,128)(2,1)S(1)} %copy-done.3, bf16[1280,2048]{1,0:T(8,128)(2,1)S(1)} %shard_map.48.refs_0_, bf16[256,2048]{1,0:T(8,128)(2,1)S(1)} %collective-permute-done.5.refs_1_, ...), custom_call_target="tpu_custom_call" | custom-call | flops 1 | bytes 1 | tf_op jit(solution)/shard_map/pallas_call | solution.py:136
  63.2 1.8 %shard_map.50 = (bf16[2,1,256,256]{3,2,1,0:T(8,128)(2,1)S(1)}, bf16[2,1,256,256]{3,2,1,0:T(8,128)(2,1)S(1)}, f32[1,1,256,256]{3,2,1,0:T(8,128)S(1)}, f32[1,1,256,256]{3,2,1,0:T(8,128)S(1)}) custom-call(bf16[512,2048]{1,0:T(8,128)(2,1)S(1)} %get-tuple-element.56.inner_ref.refs_0_, bf16[2,256,2048]{2,1,0:T(8,128)(2,1)S(1)} %get-tuple-element.57.own_ref, ...), custom_call_target="tpu_custom_call" | custom-call | flops 1 | bytes 1 | tf_op jit(solution)/shard_map/pallas_call | solution.py:171
  65.0 3.5 %collective-permute-done.10.rows_ref = bf16[512,2048]{1,0:T(8,128)(2,1)S(1)} collective-permute-done((bf16[512,2048]{1,0:T(8,128)(2,1)S(1)}, bf16[512,2048]{1,0:T(8,128)(2,1)S(1)}, u32[]{:S(2)}, u32[]{:S(2)}) %collective-permute-start.10) | collective-permute-done | bytes 2097184 | tf_op jit(solution)/shard_map/ppermute | solution.py:301
  68.5 5.2 %shard_map.51.inner_ref.refs_1_ = bf16[512,2048]{1,0:T(8,128)(2,1)S(1)} custom-call(s32[13]{0:T(128)S(1)} %stack.73.place_ref, bf16[512,2048]{1,0:T(8,128)(2,1)S(1)} %collective-permute-done.10.rows_ref, bf16[1280,2048]{1,0:T(8,128)(2,1)S(1)} %shard_map.48.refs_0_, bf16[256,2048]{1,0:T(8,128)(2,1)S(1)} %collective-permute-done.5.refs_1_, ...), custom_call_target="tpu_custom_call" | custom-call | flops 1 | bytes 1 | tf_op jit(solution)/shard_map/pallas_call | solution.py:136
  73.6 1.8 %shard_map.52 = (bf16[2,1,256,256]{3,2,1,0:T(8,128)(2,1)S(1)}, bf16[2,1,256,256]{3,2,1,0:T(8,128)(2,1)S(1)}, f32[1,1,256,256]{3,2,1,0:T(8,128)S(1)}, f32[1,1,256,256]{3,2,1,0:T(8,128)S(1)}) custom-call(bf16[512,2048]{1,0:T(8,128)(2,1)S(1)} %shard_map.51.inner_ref.refs_1_, bf16[2,256,2048]{2,1,0:T(8,128)(2,1)S(1)} %get-tuple-element.57.own_ref, ...), custom_call_target="tpu_custom_call" | custom-call | flops 1 | bytes 1 | tf_op jit(solution)/shard_map/pallas_call | solution.py:171
  75.5 0.1 collective-permute-start.18
  75.6 0.5 collective-permute-start.17
  76.1 0.1 collective-permute-start.13
  76.1 0.4 collective-permute-start.12
  76.6 0.2 collective-permute-done.11.refs_2_
  76.8 1.3 %shard_map.53 = (f32[1,2,256,256]{3,2,1,0:T(8,128)S(1)}, f32[1,2,256,256]{3,2,1,0:T(8,128)S(1)}) custom-call(bf16[512,2048]{1,0:T(8,128)(2,1)S(1)} %get-tuple-element.56.inner_ref.refs_0_, bf16[512,2048]{1,0:T(8,128)(2,1)S(1)} %shard_map.51.inner_ref.refs_1_, bf16[256,2048]{1,0:T(8,128)(2,1)S(1)} %collective-permute-done.11.refs_2_), custom_call_target="tpu_custom_call" | custom-call | flops 1 | bytes 1 | tf_op jit(solution)/shard_map/pallas_call | solution.py:190
  78.1 0.0 collective-permute-done.18.refs_3_
  78.1 0.0 collective-permute-done.17.refs_2_
  78.1 0.7 shard_map.56
  78.8 0.6 collective-permute-start.19
  79.4 0.0 collective-permute-done.13.refs_3_
  79.4 0.0 collective-permute-done.12.refs_2_
  79.4 0.7 shard_map.54
  80.1 1.6 %collective-permute-start.14 = (bf16[2,256,256]{2,1,0:T(8,128)(2,1)S(1)}, bf16[2,256,256]{2,1,0:T(8,128)(2,1)S(1)}, u32[]{:S(2)}, u32[]{:S(2)}) collective-permute-start(bf16[2,256,256]{2,1,0:T(8,128)(2,1)S(1)} %bitcast.35), channel_id=1, source_target_pairs={{0,8},{4,12},{8,0},{12,4},{16,24},{20,28},{24,16},{28,20},{1,9},{5... | collective-permute-start | bytes 786440 | tf_op jit(solution)/shard_map/ppermute | solution.py:315
  81.7 5.2 %collective-permute-done.19.refs_1_ = bf16[2,256,256]{2,1,0:T(8,128)(2,1)S(1)} collective-permute-done((bf16[2,256,256]{2,1,0:T(8,128)(2,1)S(1)}, bf16[2,256,256]{2,1,0:T(8,128)(2,1)S(1)}, u32[]{:S(2)}, u32[]{:S(2)}) %collective-permute-start.19) | collective-permute-done | bytes 262176 | tf_op jit(solution)/shard_map/ppermute | solution.py:301
  86.9 0.6 shard_map.57
  87.5 1.5 %collective-permute-start.20 = (bf16[2,256,256]{2,1,0:T(8,128)(2,1)S(1)}, bf16[2,256,256]{2,1,0:T(8,128)(2,1)S(1)}, u32[]{:S(2)}, u32[]{:S(2)}) collective-permute-start(bf16[2,256,256]{2,1,0:T(8,128)(2,1)S(1)} %get-tuple-element.80), channel_id=1, source_target_pairs={{0,8},{4,12},{8,0},{12,4},{16,24},{20,28},{24,16},{28,20},{1,9},{5... | collective-permute-start | bytes 786440 | tf_op jit(solution)/shard_map/ppermute | solution.py:315
  89.1 0.0 collective-permute-done.14.refs_0_
  89.1 0.6 shard_map.55
  89.7 2.7 %collective-permute-start.15 = (bf16[256,256]{1,0:T(8,128)(2,1)S(1)}, bf16[256,256]{1,0:T(8,128)(2,1)S(1)}, u32[]{:S(2)}, u32[]{:S(2)}) collective-permute-start(bf16[256,256]{1,0:T(8,128)(2,1)S(1)} %bitcast.36), channel_id=1, source_target_pairs={{0,16},{4,20},{8,24},{12,28},{16,0},{20,4},{24,8},{28,12},{1,17},{... | collective-permute-start | bytes 393224 | tf_op jit(solution)/shard_map/ppermute | solution.py:322
  92.3 5.3 %collective-permute-done.20.refs_0_ = bf16[2,256,256]{2,1,0:T(8,128)(2,1)S(1)} collective-permute-done((bf16[2,256,256]{2,1,0:T(8,128)(2,1)S(1)}, bf16[2,256,256]{2,1,0:T(8,128)(2,1)S(1)}, u32[]{:S(2)}, u32[]{:S(2)}) %collective-permute-start.20) | collective-permute-done | bytes 262176 | tf_op jit(solution)/shard_map/ppermute | solution.py:315
  97.6 0.6 shard_map.58
  98.2 1.5 %collective-permute-start.21 = (bf16[256,256]{1,0:T(8,128)(2,1)S(1)}, bf16[256,256]{1,0:T(8,128)(2,1)S(1)}, u32[]{:S(2)}, u32[]{:S(2)}) collective-permute-start(bf16[256,256]{1,0:T(8,128)(2,1)S(1)} %bitcast.37), channel_id=1, source_target_pairs={{0,16},{4,20},{8,24},{12,28},{16,0},{20,4},{24,8},{28,12},{1,17},{... | collective-permute-start | bytes 393224 | tf_op jit(solution)/shard_map/ppermute | solution.py:322
  99.7 0.0 collective-permute-done.15
  99.7 4.4 %collective-permute-start.16 = (bf16[256,256]{1,0:T(8,128)(2,1)S(1)}, bf16[256,256]{1,0:T(8,128)(2,1)S(1)}, u32[]{:S(2)}, u32[]{:S(2)}) collective-permute-start(bf16[256,256]{1,0:T(8,128)(2,1)S(1)} %add_convert_fusion.1), channel_id=1, source_target_pairs={{0,0},{1,8},{2,2},{3,10},{4,4},{5,12},{6,6},{7,14},{8,1},{9,9},{10... | collective-permute-start | bytes 393224 | tf_op jit(solution)/shard_map/ppermute | solution.py:329
  104.1 1.4 %collective-permute-done.21 = bf16[256,256]{1,0:T(8,128)(2,1)S(1)} collective-permute-done((bf16[256,256]{1,0:T(8,128)(2,1)S(1)}, bf16[256,256]{1,0:T(8,128)(2,1)S(1)}, u32[]{:S(2)}, u32[]{:S(2)}) %collective-permute-start.21) | collective-permute-done | bytes 131104 | tf_op jit(solution)/shard_map/ppermute | solution.py:322
  105.6 2.0 %collective-permute-done.16 = bf16[256,256]{1,0:T(8,128)(2,1)S(1)} collective-permute-done((bf16[256,256]{1,0:T(8,128)(2,1)S(1)}, bf16[256,256]{1,0:T(8,128)(2,1)S(1)}, u32[]{:S(2)}, u32[]{:S(2)}) %collective-permute-start.16) | collective-permute-done | bytes 131104 | tf_op jit(solution)/shard_map/ppermute | solution.py:329
  107.5 0.7 pad_maximum_fusion
  (14 shorter events, 0.1 us)
Async XLA Ops:
  0.0 3.3 %copy-start.5 = (s32[1,4,16]{2,1,0:T(4,128)S(1)}, s32[1,4,16]{2,1,0:T(4,128)}, u32[]{:S(2)}) copy-start(s32[1,4,16]{2,1,0:T(4,128)} %param.7) | copy-start | bytes 772
  0.0 3.3 %copy-start.4 = (bf16[1,512,2048]{2,1,0:T(8,128)(2,1)S(1)}, bf16[1,512,2048]{2,1,0:T(8,128)(2,1)}, u32[]{:S(2)}) copy-start(bf16[1,512,2048]{2,1,0:T(8,128)(2,1)} %param.5) | copy-start | bytes 6291460
  1.2 13.8 %collective-permute-start.1 = (bf16[128,2048]{1,0:T(8,128)(2,1)S(1)}, bf16[128,2048]{1,0:T(8,128)(2,1)}, u32[]{:S(2)}, u32[]{:S(2)}) collective-permute-start(bf16[128,2048]{1,0:T(8,128)(2,1)S(1)} %shard_map.46), channel_id=1, source_target_pairs={{2,0},{3,1},{0,2},{1,3},{6,4},{7,5},{4,6},{5,7},{10,8},{11,9},{8,1... | collective-permute-start | bytes 1572872 | tf_op jit(solution)/shard_map/ppermute | solution.py:305
  2.8 13.4 %collective-permute-start = (bf16[128,2048]{1,0:T(8,128)(2,1)S(1)}, bf16[128,2048]{1,0:T(8,128)(2,1)S(1)}, u32[]{:S(2)}, u32[]{:S(2)}) collective-permute-start(bf16[128,2048]{1,0:T(8,128)(2,1)S(1)} %shard_map.46), channel_id=1, source_target_pairs={{1,0},{0,1},{3,2},{2,3},{5,4},{4,5},{7,6},{6,7},{9,8},{8,9},{11,10... | collective-permute-start | bytes 1572872 | tf_op jit(solution)/shard_map/ppermute | solution.py:301
  3.3 2.8 %copy-start = (bf16[1,512,2048]{2,1,0:T(8,128)(2,1)S(1)}, bf16[1,512,2048]{2,1,0:T(8,128)(2,1)}, u32[]{:S(2)}) copy-start(bf16[1,512,2048]{2,1,0:T(8,128)(2,1)} %param.6) | copy-start | bytes 6291460
  4.6 1.4 %copy-start.2 = (bf16[512,2048]{1,0:T(8,128)(2,1)}, bf16[512,2048]{1,0:T(8,128)(2,1)S(1)}, u32[]{:S(2)}) copy-start(bf16[512,2048]{1,0:T(8,128)(2,1)S(1)} %shard_map.47.rows_ref) | copy-start | bytes 6291460
  6.1 14.9 %copy-start.3 = (bf16[512,2048]{1,0:T(8,128)(2,1)S(1)}, bf16[512,2048]{1,0:T(8,128)(2,1)}, u32[]{:S(2)}) copy-start(bf16[512,2048]{1,0:T(8,128)(2,1)} %copy-done.2) | copy-start | bytes 6291460
  6.3 28.3 %copy-start.1 = (bf16[512,2048]{1,0:T(8,128)(2,1)S(1)}, bf16[512,2048]{1,0:T(8,128)(2,1)}, u32[]{:S(2)}) copy-start(bf16[512,2048]{1,0:T(8,128)(2,1)} %refs_0_.1) | copy-start | bytes 6291460
  16.2 14.9 %collective-permute-start.2 = (bf16[128,2048]{1,0:T(8,128)(2,1)S(1)}, bf16[128,2048]{1,0:T(8,128)(2,1)S(1)}, u32[]{:S(2)}, u32[]{:S(2)}) collective-permute-start(bf16[128,2048]{1,0:T(8,128)(2,1)S(1)} %collective-permute-done), channel_id=1, source_target_pairs={{2,0},{3,1},{0,2},{1,3},{6,4},{7,5},{4,6},{5,7},{10,8},{11,9},{8,1... | collective-permute-start | bytes 1572872 | tf_op jit(solution)/shard_map/ppermute | solution.py:305
  17.8 16.7 %collective-permute-start.3 = (bf16[256,2048]{1,0:T(8,128)(2,1)S(1)}, bf16[256,2048]{1,0:T(8,128)(2,1)S(1)}, u32[]{:S(2)}, u32[]{:S(2)}) collective-permute-start(bf16[256,2048]{1,0:T(8,128)(2,1)S(1)} %constant_dynamic-update-slice_fusion.refs_1_), channel_id=1, source_target_pairs={{4,0},{0,4},{12,8},{8,12},{20,16},{16,20},{28,24},{24,28},{5,1},{1... | collective-permute-start | bytes 3145736 | tf_op jit(solution)/shard_map/ppermute | solution.py:308
  17.9 33.3 %collective-permute-start.7 = (bf16[256,2048]{1,0:T(8,128)(2,1)S(1)}, bf16[256,2048]{1,0:T(8,128)(2,1)S(1)}, u32[]{:S(2)}, u32[]{:S(2)}) collective-permute-start(bf16[256,2048]{1,0:T(8,128)(2,1)S(1)} %get-tuple-element.53), channel_id=1, source_target_pairs={{2,0},{3,1},{0,2},{1,3},{6,4},{7,5},{4,6},{5,7},{10,8},{11,9},{8,1... | collective-permute-start | bytes 3145736 | tf_op jit(solution)/shard_map/ppermute | solution.py:305
  19.5 31.8 %collective-permute-start.5 = (bf16[256,2048]{1,0:T(8,128)(2,1)S(1)}, bf16[256,2048]{1,0:T(8,128)(2,1)S(1)}, u32[]{:S(2)}, u32[]{:S(2)}) collective-permute-start(bf16[256,2048]{1,0:T(8,128)(2,1)S(1)} %constant_dynamic-update-slice_fusion.refs_1_), channel_id=1, source_target_pairs={{8,0},{12,4},{0,8},{4,12},{24,16},{28,20},{16,24},{20,28},{9,1},{1... | collective-permute-start | bytes 3145736 | tf_op jit(solution)/shard_map/ppermute | solution.py:308
  21.1 47.4 %collective-permute-start.10 = (bf16[512,2048]{1,0:T(8,128)(2,1)S(1)}, bf16[512,2048]{1,0:T(8,128)(2,1)S(1)}, u32[]{:S(2)}, u32[]{:S(2)}) collective-permute-start(bf16[512,2048]{1,0:T(8,128)(2,1)S(1)} %copy-done.3), channel_id=1, source_target_pairs={{1,0},{0,1},{3,2},{2,3},{5,4},{4,5},{7,6},{6,7},{9,8},{8,9},{11,10... | collective-permute-start | bytes 6291464 | tf_op jit(solution)/shard_map/ppermute | solution.py:301
  31.0 1.9 %collective-permute-start.4 = (bf16[128,2048]{1,0:T(8,128)(2,1)S(1)}, bf16[128,2048]{1,0:T(8,128)(2,1)S(1)}, u32[]{:S(2)}, u32[]{:S(2)}) collective-permute-start(bf16[128,2048]{1,0:T(8,128)(2,1)S(1)} %collective-permute-done.2.refs_2_), channel_id=1, source_target_pairs={{4,0},{0,4},{12,8},{8,12},{20,16},{16,20},{28,24},{24,28},{5,1},{1... | collective-permute-start | bytes 1572872 | tf_op jit(solution)/shard_map/ppermute | solution.py:308
  33.0 23.0 %collective-permute-start.6 = (bf16[128,2048]{1,0:T(8,128)(2,1)S(1)}, bf16[128,2048]{1,0:T(8,128)(2,1)S(1)}, u32[]{:S(2)}, u32[]{:S(2)}) collective-permute-start(bf16[128,2048]{1,0:T(8,128)(2,1)S(1)} %collective-permute-done.2.refs_2_), channel_id=1, source_target_pairs={{8,0},{12,4},{0,8},{4,12},{24,16},{28,20},{16,24},{20,28},{9,1},{1... | collective-permute-start | bytes 1572872 | tf_op jit(solution)/shard_map/ppermute | solution.py:308
  51.2 6.6 %collective-permute-start.8 = (bf16[256,2048]{1,0:T(8,128)(2,1)S(1)}, bf16[256,2048]{1,0:T(8,128)(2,1)S(1)}, u32[]{:S(2)}, u32[]{:S(2)}) collective-permute-start(bf16[256,2048]{1,0:T(8,128)(2,1)S(1)} %collective-permute-done.5.refs_1_), channel_id=1, source_target_pairs={{4,0},{0,4},{12,8},{8,12},{20,16},{16,20},{28,24},{24,28},{5,1},{1... | collective-permute-start | bytes 3145736 | tf_op jit(solution)/shard_map/ppermute | solution.py:308
  51.2 25.6 %collective-permute-start.11 = (bf16[256,2048]{1,0:T(8,128)(2,1)S(1)}, bf16[256,2048]{1,0:T(8,128)(2,1)S(1)}, u32[]{:S(2)}, u32[]{:S(2)}) collective-permute-start(bf16[256,2048]{1,0:T(8,128)(2,1)S(1)} %get-tuple-element.62), channel_id=1, source_target_pairs={{2,0},{3,1},{0,2},{1,3},{6,4},{7,5},{4,6},{5,7},{10,8},{11,9},{8,1... | collective-permute-start | bytes 3145736 | tf_op jit(solution)/shard_map/ppermute | solution.py:305
  55.9 1.9 %collective-permute-start.9 = (bf16[128,2048]{1,0:T(8,128)(2,1)S(1)}, bf16[128,2048]{1,0:T(8,128)(2,1)S(1)}, u32[]{:S(2)}, u32[]{:S(2)}) collective-permute-start(bf16[128,2048]{1,0:T(8,128)(2,1)S(1)} %collective-permute-done.6.refs_2_), channel_id=1, source_target_pairs={{4,0},{0,4},{12,8},{8,12},{20,16},{16,20},{28,24},{24,28},{5,1},{1... | collective-permute-start | bytes 1572872 | tf_op jit(solution)/shard_map/ppermute | solution.py:308
  75.5 2.6 %collective-permute-start.18 = (bf16[2,1,256,256]{3,2,1,0:T(8,128)(2,1)S(1)}, bf16[2,1,256,256]{3,2,1,0:T(8,128)(2,1)S(1)}, u32[]{:S(2)}, u32[]{:S(2)}) collective-permute-start(bf16[2,1,256,256]{3,2,1,0:T(8,128)(2,1)S(1)} %get-tuple-element.76), channel_id=1, source_target_pairs={{4,0},{0,4},{12,8},{8,12},{20,16},{16,20},{28,24},{24,28},{5,1},{1... | collective-permute-start | bytes 786440 | tf_op jit(solution)/shard_map/ppermute | solution.py:308
  75.6 2.6 %collective-permute-start.17 = (bf16[2,1,256,256]{3,2,1,0:T(8,128)(2,1)S(1)}, bf16[2,1,256,256]{3,2,1,0:T(8,128)(2,1)S(1)}, u32[]{:S(2)}, u32[]{:S(2)}) collective-permute-start(bf16[2,1,256,256]{3,2,1,0:T(8,128)(2,1)S(1)} %get-tuple-element.75), channel_id=1, source_target_pairs={{4,0},{0,4},{12,8},{8,12},{20,16},{16,20},{28,24},{24,28},{5,1},{1... | collective-permute-start | bytes 786440 | tf_op jit(solution)/shard_map/ppermute | solution.py:308
  76.1 3.3 %collective-permute-start.13 = (bf16[2,1,256,256]{3,2,1,0:T(8,128)(2,1)S(1)}, bf16[2,1,256,256]{3,2,1,0:T(8,128)(2,1)S(1)}, u32[]{:S(2)}, u32[]{:S(2)}) collective-permute-start(bf16[2,1,256,256]{3,2,1,0:T(8,128)(2,1)S(1)} %get-tuple-element.68), channel_id=1, source_target_pairs={{4,0},{0,4},{12,8},{8,12},{20,16},{16,20},{28,24},{24,28},{5,1},{1... | collective-permute-start | bytes 786440 | tf_op jit(solution)/shard_map/ppermute | solution.py:308
  76.1 3.3 %collective-permute-start.12 = (bf16[2,1,256,256]{3,2,1,0:T(8,128)(2,1)S(1)}, bf16[2,1,256,256]{3,2,1,0:T(8,128)(2,1)S(1)}, u32[]{:S(2)}, u32[]{:S(2)}) collective-permute-start(bf16[2,1,256,256]{3,2,1,0:T(8,128)(2,1)S(1)} %get-tuple-element.67), channel_id=1, source_target_pairs={{4,0},{0,4},{12,8},{8,12},{20,16},{16,20},{28,24},{24,28},{5,1},{1... | collective-permute-start | bytes 786440 | tf_op jit(solution)/shard_map/ppermute | solution.py:308
  78.8 8.1 %collective-permute-start.19 = (bf16[2,256,256]{2,1,0:T(8,128)(2,1)S(1)}, bf16[2,256,256]{2,1,0:T(8,128)(2,1)S(1)}, u32[]{:S(2)}, u32[]{:S(2)}) collective-permute-start(bf16[2,256,256]{2,1,0:T(8,128)(2,1)S(1)} %bitcast.34), channel_id=1, source_target_pairs={{1,0},{0,1},{3,2},{2,3},{5,4},{4,5},{7,6},{6,7},{9,8},{8,9},{11,10... | collective-permute-start | bytes 786440 | tf_op jit(solution)/shard_map/ppermute | solution.py:301
  80.1 9.0 %collective-permute-start.14 = (bf16[2,256,256]{2,1,0:T(8,128)(2,1)S(1)}, bf16[2,256,256]{2,1,0:T(8,128)(2,1)S(1)}, u32[]{:S(2)}, u32[]{:S(2)}) collective-permute-start(bf16[2,256,256]{2,1,0:T(8,128)(2,1)S(1)} %bitcast.35), channel_id=1, source_target_pairs={{0,8},{4,12},{8,0},{12,4},{16,24},{20,28},{24,16},{28,20},{1,9},{5... | collective-permute-start | bytes 786440 | tf_op jit(solution)/shard_map/ppermute | solution.py:315
  87.5 10.0 %collective-permute-start.20 = (bf16[2,256,256]{2,1,0:T(8,128)(2,1)S(1)}, bf16[2,256,256]{2,1,0:T(8,128)(2,1)S(1)}, u32[]{:S(2)}, u32[]{:S(2)}) collective-permute-start(bf16[2,256,256]{2,1,0:T(8,128)(2,1)S(1)} %get-tuple-element.80), channel_id=1, source_target_pairs={{0,8},{4,12},{8,0},{12,4},{16,24},{20,28},{24,16},{28,20},{1,9},{5... | collective-permute-start | bytes 786440 | tf_op jit(solution)/shard_map/ppermute | solution.py:315
  89.7 10.0 %collective-permute-start.15 = (bf16[256,256]{1,0:T(8,128)(2,1)S(1)}, bf16[256,256]{1,0:T(8,128)(2,1)S(1)}, u32[]{:S(2)}, u32[]{:S(2)}) collective-permute-start(bf16[256,256]{1,0:T(8,128)(2,1)S(1)} %bitcast.36), channel_id=1, source_target_pairs={{0,16},{4,20},{8,24},{12,28},{16,0},{20,4},{24,8},{28,12},{1,17},{... | collective-permute-start | bytes 393224 | tf_op jit(solution)/shard_map/ppermute | solution.py:322
  98.2 7.3 %collective-permute-start.21 = (bf16[256,256]{1,0:T(8,128)(2,1)S(1)}, bf16[256,256]{1,0:T(8,128)(2,1)S(1)}, u32[]{:S(2)}, u32[]{:S(2)}) collective-permute-start(bf16[256,256]{1,0:T(8,128)(2,1)S(1)} %bitcast.37), channel_id=1, source_target_pairs={{0,16},{4,20},{8,24},{12,28},{16,0},{20,4},{24,8},{28,12},{1,17},{... | collective-permute-start | bytes 393224 | tf_op jit(solution)/shard_map/ppermute | solution.py:322
  99.7 7.8 %collective-permute-start.16 = (bf16[256,256]{1,0:T(8,128)(2,1)S(1)}, bf16[256,256]{1,0:T(8,128)(2,1)S(1)}, u32[]{:S(2)}, u32[]{:S(2)}) collective-permute-start(bf16[256,256]{1,0:T(8,128)(2,1)S(1)} %add_convert_fusion.1), channel_id=1, source_target_pairs={{0,0},{1,8},{2,2},{3,10},{4,4},{5,12},{6,6},{7,14},{8,1},{9,9},{10... | collective-permute-start | bytes 393224 | tf_op jit(solution)/shard_map/ppermute | solution.py:329
